TPU v7x, 32 devices: a whole 2x2x4 slice. The times are simulated.
32 devices in a mesh: view: 2 (over y), dp: 16 (over z, x, core).
Axes of the slice: x: 2, y: 2, z: 4, core: 2. Of those that a mesh axis runs over, the one named last changes fastest.
Arguments:
- inputs: bfloat16 [2, 64, 14, 14, 1024], P('view', 'dp'), may hold values from -6 to 6
- resolution: int32 [2, 64], P('view', 'dp'), may hold values from 160 to 224, as said below
- reduce_a: bfloat16 [1024, 256], replicated, may hold values from -0.1875 to 0.1875
- spatial_a: bfloat16 [3, 3, 256, 256], replicated, may hold values from -0.125 to 0.125
- expand_a: bfloat16 [256, 1024], replicated, may hold values from -0.375 to 0.375
- reduce_b: bfloat16 [1024, 512], replicated, may hold values from -0.1875 to 0.1875
- spatial_b: bfloat16 [3, 3, 512, 512], replicated, may hold values from -0.09375 to 0.09375
- expand_b: bfloat16 [512, 2048], replicated, may hold values from -0.25 to 0.25
- shortcut_b: bfloat16 [1024, 2048], replicated, may hold values from -0.1875 to 0.1875
- scale_reduce_a: float32 [256], replicated, may hold values from 0.5 to 1.5
- shift_reduce_a: float32 [256], replicated, may hold values from -3 to 3
- scale_spatial_a: float32 [256], replicated, may hold values from 0.5 to 1.5
- shift_spatial_a: float32 [256], replicated, may hold values from -3 to 3
- scale_expand_a: float32 [1024], replicated, may hold values from 0.5 to 1.5
- shift_expand_a: float32 [1024], replicated, may hold values from -3 to 3
- scale_reduce_b: float32 [512], replicated, may hold values from 0.5 to 1.5
- shift_reduce_b: float32 [512], replicated, may hold values from -3 to 3
- scale_spatial_b: float32 [512], replicated, may hold values from 0.5 to 1.5
- shift_spatial_b: float32 [512], replicated, may hold values from -3 to 3
- scale_expand_b: float32 [2048], replicated, may hold values from 0.5 to 1.5
- shift_expand_b: float32 [2048], replicated, may hold values from -3 to 3
- scale_shortcut: float32 [2048], replicated, may hold values from 0.5 to 1.5
- shift_shortcut: float32 [2048], replicated, may hold values from -3 to 3
Outputs:
- loss: float32 [2, 64], P('view', 'dp')
- block_a: bfloat16 [2, 64, 14, 14, 1024], P('view', 'dp')
- block_b: bfloat16 [2, 64, 7, 7, 2048], P('view', 'dp')
- input_grad: bfloat16 [2, 64, 14, 14, 1024], P('view', 'dp')
- grads_a: float32 [1117184], P(('view', 'dp'))
- grads_b: float32 [6039552], P(('view', 'dp'))
Inputs may be any that keep to these rules, and one draw needn't show every extreme that they name: Each view of each image has resolution 160 or 224; both values occur in every draw.
All inputs are finite; a program needn't handle non-finite values.
Results may differ from a plain program's by a relative error of at most 0.018.
Values sent between devices are 32-bit elements; how exact they have to be, the bound alone decides.
No kernel may reach another device: no remote copies, remote signals or barrier semaphores. Data moves between devices by JAX's collectives and lax.ppermute only.
A program may use at most 192 MiB of HBM per device.

v0:
```python
import jax
import jax.numpy as jnp
from jax import lax
from jax.sharding import PartitionSpec as P

eps_norm = 1e-05
eps_cos = 1e-06
loss_scale = 65536.0


def swapped(value, axis, bit):
    return lax.ppermute(value, axis, [(i, i ^ 1 << bit) for i in range(lax.axis_size(axis))])


def build_masks(resolution, height, divisor):
    bounds = resolution // divisor
    places = jnp.arange(height, dtype=jnp.int32)
    inside = (places[None, :, None] < bounds[:, None, None]) & (
        places[None, None, :] < bounds[:, None, None]
    )
    return inside.astype(jnp.float32)[..., None]


def smooth(tensor):
    return jax.nn.gelu(tensor, approximate=False)


def smooth_back(tensor, upstream):
    _, pullback = jax.vjp(smooth, tensor)
    return pullback(upstream)[0]


def tap_block(tensor):
    height = tensor.shape[1]
    padded = jnp.pad(tensor, ((0, 0), (1, 1), (1, 1), (0, 0)))
    return jnp.concatenate(
        [
            padded[:, row_pos : row_pos + height, col_pos : col_pos + height, :]
            for row_pos in range(3)
            for col_pos in range(3)
        ],
        axis=3,
    )


def tap_stride(tensor):
    height = tensor.shape[1]
    padded = jnp.pad(tensor, ((0, 0), (1, 1), (1, 1), (0, 0)))
    return jnp.concatenate(
        [
            padded[:, row_pos : row_pos + height - 1 : 2, col_pos : col_pos + height - 1 : 2, :]
            for row_pos in range(3)
            for col_pos in range(3)
        ],
        axis=3,
    )


def matmul_in(tensor, weight):
    flat = tensor.reshape(-1, tensor.shape[-1])
    result = jnp.dot(flat, weight, preferred_element_type=jnp.float32)
    return result.reshape(tensor.shape[:-1] + (weight.shape[1],))


def matmul_back(upstream, weight):
    flat = upstream.reshape(-1, upstream.shape[-1])
    result = jnp.einsum("pd,cd->pc", flat, weight, preferred_element_type=jnp.float32)
    return result.reshape(upstream.shape[:-1] + (weight.shape[0],))


def weight_grad(tensor, upstream):
    return jnp.einsum(
        "pc,pd->cd",
        tensor.reshape(-1, tensor.shape[-1]),
        upstream.reshape(-1, upstream.shape[-1]),
        preferred_element_type=jnp.float32,
    )


def local_moments(tensor, keep_mask):
    return jnp.stack(
        [
            jnp.sum(tensor * keep_mask, axis=(0, 1, 2)),
            jnp.sum(tensor * tensor * keep_mask, axis=(0, 1, 2)),
        ]
    )


def finish_moments(moments, total_count):
    center = moments[0] / total_count
    inverse = lax.rsqrt(moments[1] / total_count - center * center + eps_norm)
    return (center, inverse)


def normalize(tensor, center, inverse, factor, offset):
    unit = (tensor - center) * inverse
    return (unit, factor * unit + offset)


def share_moments(moments):
    return lax.psum(moments, "dp")


def share_partials(partials):
    return lax.psum(partials, "dp")


def grad_partials(upstream, unit):
    return jnp.stack([jnp.sum(upstream, axis=(0, 1, 2)), jnp.sum(upstream * unit, axis=(0, 1, 2))])


def norm_input(upstream, unit, totals, total_count, factor, inverse, keep_mask):
    return (
        factor
        * inverse
        * (upstream - totals[0] / total_count - unit * totals[1] / total_count)
        * keep_mask
    )


def spread_even(tensor):
    images, height, width, depth = tensor.shape
    rows_done = jnp.stack([tensor, jnp.zeros_like(tensor)], axis=2).reshape(
        images, 2 * height, width, depth
    )
    both_done = jnp.stack([rows_done, jnp.zeros_like(rows_done)], axis=3)
    return both_done.reshape(images, 2 * height, 2 * width, depth)


def pack_flat(parts):
    return jnp.concatenate([part_item.reshape(-1) for part_item in parts])


def per_device(
    inputs,
    resolution,
    reduce_a,
    spatial_a,
    expand_a,
    reduce_b,
    spatial_b,
    expand_b,
    shortcut_b,
    scale_reduce_a,
    shift_reduce_a,
    scale_spatial_a,
    shift_spatial_a,
    scale_expand_a,
    shift_expand_a,
    scale_reduce_b,
    shift_reduce_b,
    scale_spatial_b,
    shift_spatial_b,
    scale_expand_b,
    shift_expand_b,
    scale_shortcut,
    shift_shortcut,
):
    images = inputs[0]
    sizes_here = resolution[0]
    height = images.shape[1]
    mask_big = build_masks(sizes_here, height, 16)
    mask_small = build_masks(sizes_here, height // 2, 32)
    pixels = (sizes_here // 32 * (sizes_here // 32)).astype(jnp.float32)
    start = images.astype(jnp.float32) * mask_big
    start_low = start.astype(jnp.bfloat16)
    spatial_a_flat = spatial_a.reshape(-1, spatial_a.shape[3])
    spatial_b_flat = spatial_b.reshape(-1, spatial_b.shape[3])
    reduced_a = matmul_in(start_low, reduce_a)
    counts_here = jnp.stack([jnp.sum(mask_big), jnp.sum(mask_small)])
    moments_ra, counts = lax.psum((local_moments(reduced_a, mask_big), counts_here), "dp")
    count_big = counts[0]
    count_small = counts[1]
    center, inverse_ra = finish_moments(moments_ra, count_big)
    unit_ra, pre_ra = normalize(reduced_a, center, inverse_ra, scale_reduce_a, shift_reduce_a)
    hidden_one_a = (smooth(pre_ra) * mask_big).astype(jnp.bfloat16)
    taps_a = tap_block(hidden_one_a)
    mixed_a = matmul_in(taps_a, spatial_a_flat)
    center, inverse_sa = finish_moments(share_moments(local_moments(mixed_a, mask_big)), count_big)
    unit_sa, pre_sa = normalize(mixed_a, center, inverse_sa, scale_spatial_a, shift_spatial_a)
    hidden_two_a = (smooth(pre_sa) * mask_big).astype(jnp.bfloat16)
    expanded_a = matmul_in(hidden_two_a, expand_a)
    center, inverse_ea = finish_moments(
        share_moments(local_moments(expanded_a, mask_big)), count_big
    )
    unit_ea, pre_ea = normalize(expanded_a, center, inverse_ea, scale_expand_a, shift_expand_a)
    joined_a = pre_ea + start
    block_a = (smooth(joined_a) * mask_big).astype(jnp.bfloat16)
    reduced_b = matmul_in(block_a, reduce_b)
    picked = block_a[:, ::2, ::2, :]
    side_b = matmul_in(picked, shortcut_b)
    width_rb = reduced_b.shape[3]
    moments_b = share_moments(
        jnp.concatenate(
            [local_moments(reduced_b, mask_big), local_moments(side_b, mask_small)], axis=1
        )
    )
    center, inverse_rb = finish_moments(moments_b[:, :width_rb], count_big)
    unit_rb, pre_rb = normalize(reduced_b, center, inverse_rb, scale_reduce_b, shift_reduce_b)
    center, inverse_sc = finish_moments(moments_b[:, width_rb:], count_small)
    unit_sc, pre_sc = normalize(side_b, center, inverse_sc, scale_shortcut, shift_shortcut)
    hidden_one_b = (smooth(pre_rb) * mask_big).astype(jnp.bfloat16)
    taps_b = tap_stride(hidden_one_b)
    mixed_b = matmul_in(taps_b, spatial_b_flat)
    center, inverse_sb = finish_moments(
        share_moments(local_moments(mixed_b, mask_small)), count_small
    )
    unit_sb, pre_sb = normalize(mixed_b, center, inverse_sb, scale_spatial_b, shift_spatial_b)
    hidden_two_b = (smooth(pre_sb) * mask_small).astype(jnp.bfloat16)
    expanded_b = matmul_in(hidden_two_b, expand_b)
    center, inverse_eb = finish_moments(
        share_moments(local_moments(expanded_b, mask_small)), count_small
    )
    unit_eb, pre_eb = normalize(expanded_b, center, inverse_eb, scale_expand_b, shift_expand_b)
    joined_b = pre_eb + pre_sc
    out_b = smooth(joined_b) * mask_small
    pooled = jnp.sum(out_b, axis=(1, 2)) / pixels[:, None]
    partner = swapped(pooled, "view", 0)
    inverse_own = lax.rsqrt(jnp.sum(pooled * pooled, axis=1, keepdims=True) + eps_cos)
    unit_own = pooled * inverse_own
    unit_other = partner * lax.rsqrt(jnp.sum(partner * partner, axis=1, keepdims=True) + eps_cos)
    cosine = jnp.sum(unit_own * unit_other, axis=1)
    loss = -0.5 * cosine
    grad_pooled = -0.5 * loss_scale * inverse_own * (unit_other - cosine[:, None] * unit_own)
    grad_out = (grad_pooled / pixels[:, None])[:, None, None, :] * mask_small
    grad_joined_b = smooth_back(joined_b, grad_out)
    width_eb = grad_joined_b.shape[3]
    local_eb = grad_partials(grad_joined_b, unit_eb)
    local_sc = grad_partials(grad_joined_b, unit_sc)
    totals_b = share_partials(jnp.concatenate([local_eb, local_sc], axis=1))
    low_eb = norm_input(
        grad_joined_b,
        unit_eb,
        totals_b[:, :width_eb],
        count_small,
        scale_expand_b,
        inverse_eb,
        mask_small,
    ).astype(jnp.bfloat16)
    low_sc = norm_input(
        grad_joined_b,
        unit_sc,
        totals_b[:, width_eb:],
        count_small,
        scale_shortcut,
        inverse_sc,
        mask_small,
    ).astype(jnp.bfloat16)
    grad_expand_b = weight_grad(hidden_two_b, low_eb)
    grad_shortcut = weight_grad(picked, low_sc)
    grad_pre_sb = smooth_back(pre_sb, matmul_back(low_eb, expand_b) * mask_small)
    grad_picked = matmul_back(low_sc, shortcut_b)
    local_sb = grad_partials(grad_pre_sb, unit_sb)
    low_sb = norm_input(
        grad_pre_sb,
        unit_sb,
        share_partials(local_sb),
        count_small,
        scale_spatial_b,
        inverse_sb,
        mask_small,
    ).astype(jnp.bfloat16)
    grad_spatial_b = weight_grad(taps_b, low_sb).reshape(spatial_b.shape)
    _, untap_b = jax.vjp(tap_stride, jnp.zeros(hidden_one_b.shape, jnp.float32))
    grad_hidden_b = untap_b(matmul_back(low_sb, spatial_b_flat))[0]
    grad_pre_rb = smooth_back(pre_rb, grad_hidden_b * mask_big)
    local_rb = grad_partials(grad_pre_rb, unit_rb)
    low_rb = norm_input(
        grad_pre_rb,
        unit_rb,
        share_partials(local_rb),
        count_big,
        scale_reduce_b,
        inverse_rb,
        mask_big,
    ).astype(jnp.bfloat16)
    grad_reduce_b = weight_grad(block_a, low_rb)
    grad_block_a = matmul_back(low_rb, reduce_b) + spread_even(grad_picked)
    late_flat = pack_flat(
        [
            grad_reduce_b,
            grad_spatial_b,
            grad_expand_b,
            grad_shortcut,
            local_rb,
            local_sb,
            local_eb,
            local_sc,
        ]
    )
    grad_joined_a = smooth_back(joined_a, grad_block_a * mask_big)
    local_ea = grad_partials(grad_joined_a, unit_ea)
    low_ea = norm_input(
        grad_joined_a,
        unit_ea,
        share_partials(local_ea),
        count_big,
        scale_expand_a,
        inverse_ea,
        mask_big,
    ).astype(jnp.bfloat16)
    grad_expand_a = weight_grad(hidden_two_a, low_ea)
    grad_pre_sa = smooth_back(pre_sa, matmul_back(low_ea, expand_a) * mask_big)
    local_sa = grad_partials(grad_pre_sa, unit_sa)
    low_sa = norm_input(
        grad_pre_sa,
        unit_sa,
        share_partials(local_sa),
        count_big,
        scale_spatial_a,
        inverse_sa,
        mask_big,
    ).astype(jnp.bfloat16)
    grad_spatial_a = weight_grad(taps_a, low_sa).reshape(spatial_a.shape)
    _, untap_a = jax.vjp(tap_block, jnp.zeros(hidden_one_a.shape, jnp.float32))
    grad_hidden_a = untap_a(matmul_back(low_sa, spatial_a_flat))[0]
    grad_pre_ra = smooth_back(pre_ra, grad_hidden_a * mask_big)
    local_ra = grad_partials(grad_pre_ra, unit_ra)
    low_ra = norm_input(
        grad_pre_ra,
        unit_ra,
        share_partials(local_ra),
        count_big,
        scale_reduce_a,
        inverse_ra,
        mask_big,
    ).astype(jnp.bfloat16)
    grad_reduce_a = weight_grad(start_low, low_ra)
    grad_start = grad_joined_a + matmul_back(low_ra, reduce_a)
    input_grad = (grad_start * mask_big).astype(jnp.bfloat16)
    early_flat = pack_flat(
        [grad_reduce_a, grad_spatial_a, grad_expand_a, local_ra, local_sa, local_ea]
    )
    late_done, early_done = (
        lax.psum_scatter(late_flat, ("view", "dp"), scatter_dimension=0, tiled=True),
        lax.psum_scatter(early_flat, ("view", "dp"), scatter_dimension=0, tiled=True),
    )
    return (
        loss[None],
        block_a[None],
        out_b.astype(jnp.bfloat16)[None],
        input_grad[None],
        early_done,
        late_done,
    )


def solution(mesh):
    in_specs = (
        P("view", "dp", None, None, None),
        P("view", "dp"),
        P(),
        P(),
        P(),
        P(),
        P(),
        P(),
        P(),
        P(),
        P(),
        P(),
        P(),
        P(),
        P(),
        P(),
        P(),
        P(),
        P(),
        P(),
        P(),
        P(),
        P(),
    )
    out_specs = (
        P("view", "dp"),
        P("view", "dp", None, None, None),
        P("view", "dp", None, None, None),
        P("view", "dp", None, None, None),
        P(("view", "dp")),
        P(("view", "dp")),
    )
    return jax.shard_map(
        per_device, mesh=mesh, in_specs=in_specs, out_specs=out_specs, check_vma=False
    )
```

profile of v0, /device:TPU:0, one launch (start us, length us, event | category | flops | bytes accessed | tf_op | source)
XLA Modules:
  0.0 1291.8 jit_solution(17267586314048002392)
XLA Ops:
  14.1 34.9 %all-reduce.25 = (f32[2,256]{1,0:T(2,128)S(1)}, f32[2]{0:T(128)S(1)}) all-reduce(f32[2,256]{1,0:T(2,128)S(1)} %pad_maximum_fusion.8, f32[2]{0:T(128)S(1)} %pad_maximum_fusion.12), channel_id=1, replica_groups=mesh['view'=2,'dp'=16] {'dp'}, use_global_device_ids=true, to_apply=%region_2.3 | all-reduce | flops 514 | bytes 4112 | tf_op jit(solution)/shard_map/psum | solution.py:171
  58.5 29.5 %psum.93 = f32[2,256]{1,0:T(2,128)S(1)} all-reduce(f32[2,256]{1,0:T(2,128)S(1)} %pad_maximum_fusion.9), channel_id=1, replica_groups=mesh['view'=2,'dp'=16] {'dp'}, use_global_device_ids=true, to_apply=%region_8.9 | all-reduce | flops 512 | bytes 4096 | tf_op jit(solution)/shard_map/psum | solution.py:101
  94.5 30.2 %psum.94 = f32[2,1024]{1,0:T(2,128)S(1)} all-reduce(f32[2,1024]{1,0:T(2,128)S(1)} %pad_maximum_fusion.3), channel_id=1, replica_groups=mesh['view'=2,'dp'=16] {'dp'}, use_global_device_ids=true, to_apply=%region_11.12 | all-reduce | flops 2048 | bytes 16384 | tf_op jit(solution)/shard_map/psum | solution.py:101
  125.5 11.9 multiply_convert_fusion.2
  137.4 12.2 slice.174
  149.7 4.5 multiply_reduce_fusion.11
  157.5 57.6 %psum.95 = f32[2,2560]{1,0:T(2,128)S(1)} all-reduce(f32[2,2560]{1,0:T(2,128)S(1)} %maximum_maximum_fusion.1), channel_id=1, replica_groups=mesh['view'=2,'dp'=16] {'dp'}, use_global_device_ids=true, to_apply=%region_16.17 | all-reduce | flops 5120 | bytes 40960 | tf_op jit(solution)/shard_map/psum | solution.py:101
  215.9 5.7 multiply_convert_fusion.6
  221.9 8.7 slice.177
  230.6 8.7 slice.178
  239.2 8.6 slice.179
  247.9 8.6 slice.180
  256.5 8.6 slice.181
  265.1 8.6 slice.182
  273.7 8.6 slice.183
  282.3 8.6 slice.184
  295.8 5.4 multiply_reduce_fusion.20
  301.3 29.9 %psum.96 = f32[2,512]{1,0:T(2,128)S(1)} all-reduce(f32[2,512]{1,0:T(2,128)S(1)} %pad_maximum_fusion.5), channel_id=1, replica_groups=mesh['view'=2,'dp'=16] {'dp'}, use_global_device_ids=true, to_apply=%region_19.20 | all-reduce | flops 1024 | bytes 8192 | tf_op jit(solution)/shard_map/psum | solution.py:101
  335.4 57.6 %psum.97 = f32[2,2048]{1,0:T(2,128)S(1)} all-reduce(f32[2,2048]{1,0:T(2,128)S(1)} %pad_maximum_fusion.2), channel_id=1, replica_groups=mesh['view'=2,'dp'=16] {'dp'}, use_global_device_ids=true, to_apply=%region_22.23 | all-reduce | flops 4096 | bytes 32768 | tf_op jit(solution)/shard_map/psum | solution.py:101
  393.8 6.8 convert_bitcast_fusion
  409.1 57.9 %psum.98 = f32[2,4096]{1,0:T(2,128)S(1)} all-reduce(f32[2,4096]{1,0:T(2,128)S(1)} %maximum_maximum_fusion), channel_id=1, replica_groups=mesh['view'=2,'dp'=16] {'dp'}, use_global_device_ids=true, to_apply=%region_30.31 | all-reduce | flops 8192 | bytes 65536 | tf_op jit(solution)/shard_map/psum | solution.py:105
  467.7 4.6 multiply_convert_fusion.5
  480.5 29.5 %psum.99 = f32[2,512]{1,0:T(2,128)S(1)} all-reduce(f32[2,512]{1,0:T(2,128)S(1)} %get-tuple-element.120), channel_id=1, replica_groups=mesh['view'=2,'dp'=16] {'dp'}, use_global_device_ids=true, to_apply=%region_33.34 | all-reduce | flops 1024 | bytes 8192 | tf_op jit(solution)/shard_map/psum | solution.py:105
  511.5 4.2 fusion.111
  517.2 9.8 pad.132
  527.0 9.9 pad.131
  536.9 10.0 pad.78
  546.8 10.0 pad.76
  556.8 10.0 pad.77
  566.8 9.9 pad.264
  576.7 10.0 pad.263
  586.6 10.0 pad.262
  596.6 9.9 pad.261
  611.7 7.9 fusion.100
  620.2 29.9 %psum.100 = f32[2,512]{1,0:T(2,128)S(1)} all-reduce(f32[2,512]{1,0:T(2,128)S(1)} %get-tuple-element.122), channel_id=1, replica_groups=mesh['view'=2,'dp'=16] {'dp'}, use_global_device_ids=true, to_apply=%region_36.37 | all-reduce | flops 1024 | bytes 8192 | tf_op jit(solution)/shard_map/psum | solution.py:105
  653.9 9.4 fusion.99
  663.9 30.0 %psum.101 = f32[2,1024]{1,0:T(2,128)S(1)} all-reduce(f32[2,1024]{1,0:T(2,128)S(1)} %get-tuple-element.112), channel_id=1, replica_groups=mesh['view'=2,'dp'=16] {'dp'}, use_global_device_ids=true, to_apply=%region_39.40 | all-reduce | flops 2048 | bytes 16384 | tf_op jit(solution)/shard_map/psum | solution.py:105
  694.6 5.1 multiply_convert_fusion.1
  702.3 29.5 %psum.102 = f32[2,256]{1,0:T(2,128)S(1)} all-reduce(f32[2,256]{1,0:T(2,128)S(1)} %get-tuple-element.134), channel_id=1, replica_groups=mesh['view'=2,'dp'=16] {'dp'}, use_global_device_ids=true, to_apply=%region_42.43 | all-reduce | flops 512 | bytes 4096 | tf_op jit(solution)/shard_map/psum | solution.py:105
  744.1 5.7 convolution_bitcast_fusion
  749.8 4.0 convolution_bitcast_fusion.2
  753.9 5.0 convolution_bitcast_fusion.1
  765.3 29.7 %psum.103 = f32[2,256]{1,0:T(2,128)S(1)} all-reduce(f32[2,256]{1,0:T(2,128)S(1)} %get-tuple-element.136), channel_id=1, replica_groups=mesh['view'=2,'dp'=16] {'dp'}, use_global_device_ids=true, to_apply=%region_45.46 | all-reduce | flops 512 | bytes 4096 | tf_op jit(solution)/shard_map/psum | solution.py:105
  808.6 9.7 copy.79
  818.3 5.3 copy.80
  823.7 5.6 copy.81
  835.2 4.5 constant_dynamic-update-slice_fusion.22
  859.7 421.1 %all-reduce.28.cloned.1.call-done = (f32[1117184]{0:T(1024)}, f32[6039552]{0:T(1024)}) async-done(((f32[1117184]{0:T(1024)}, f32[6039552]{0:T(1024)}), (f32[1117184]{0:T(1024)}, f32[6039552]{0:T(1024)})) %all-reduce.28.cloned.1.call-update) | async-done | bytes 28626960
  (325 shorter events, 133.1 us)
Async XLA Ops:
  7.2 324.7 %copy-start = (bf16[512,2048]{1,0:T(8,128)(2,1)S(1)}, bf16[512,2048]{1,0:T(8,128)(2,1)}, u32[]{:S(2)}) copy-start(bf16[512,2048]{1,0:T(8,128)(2,1)} %param.30) | copy-start | bytes 6291460
  7.2 1273.6 %all-reduce.28.cloned.1.call-start = ((), (), s32[]{:S(2)}) async-start(), calls=%async_computation | async-start | bytes 57253888
  8.4 724.1 %copy-start.17 = (f32[4,14,14]{2,1,0:T(8,128)}, f32[4,14,14]{2,1,0:T(8,128)S(1)}, u32[]{:S(2)}) copy-start(f32[4,14,14]{2,1,0:T(8,128)S(1)} %and_convert_fusion) | copy-start | bytes 9412
  9.9 40.3 %copy-start.72 = (f32[256]{0:T(256)S(1)}, f32[256]{0:T(256)}, u32[]{:S(2)}) copy-start(f32[256]{0:T(256)} %param.32) | copy-start | bytes 3076
  9.9 40.9 %copy-start.74 = (f32[256]{0:T(256)S(1)}, f32[256]{0:T(256)}, u32[]{:S(2)}) copy-start(f32[256]{0:T(256)} %param.33) | copy-start | bytes 3076
  12.6 41.0 %copy-start.6 = (f32[4,14,14,256]{3,2,1,0:T(8,128)}, f32[4,14,14,256]{3,2,1,0:T(8,128)S(1)}, u32[]{:S(2)}) copy-start(f32[4,14,14,256]{3,2,1,0:T(8,128)S(1)} %get-tuple-element.154) | copy-start | bytes 2408452
  57.2 31.6 %copy-start.81 = (f32[256]{0:T(256)S(1)}, f32[256]{0:T(256)}, u32[]{:S(2)}) copy-start(f32[256]{0:T(256)} %param.34) | copy-start | bytes 3076
  57.2 31.6 %copy-start.86 = (f32[256]{0:T(256)S(1)}, f32[256]{0:T(256)}, u32[]{:S(2)}) copy-start(f32[256]{0:T(256)} %param.35) | copy-start | bytes 3076
  58.5 36.0 %copy-start.20 = (f32[4,14,14,256]{3,2,1,0:T(8,128)}, f32[4,14,14,256]{3,2,1,0:T(8,128)S(1)}, u32[]{:S(2)}) copy-start(f32[4,14,14,256]{3,2,1,0:T(8,128)S(1)} %get-tuple-element.155) | copy-start | bytes 2408452
  91.8 33.6 %copy-start.69 = (f32[1024]{0:T(1024)S(1)}, f32[1024]{0:T(1024)}, u32[]{:S(2)}) copy-start(f32[1024]{0:T(1024)} %param.36) | copy-start | bytes 12292
  91.8 33.6 %copy-start.80 = (f32[1024]{0:T(1024)S(1)}, f32[1024]{0:T(1024)}, u32[]{:S(2)}) copy-start(f32[1024]{0:T(1024)} %param.37) | copy-start | bytes 12292
  154.2 61.7 %copy-start.68 = (f32[512]{0:T(512)S(1)}, f32[512]{0:T(512)}, u32[]{:S(2)}) copy-start(f32[512]{0:T(512)} %param.38) | copy-start | bytes 6148
  154.2 61.7 %copy-start.77 = (f32[512]{0:T(512)S(1)}, f32[512]{0:T(512)}, u32[]{:S(2)}) copy-start(f32[512]{0:T(512)} %param.39) | copy-start | bytes 6148
  295.8 5.5 copy-start.66
  295.8 36.0 %copy-start.85 = (f32[512]{0:T(512)S(1)}, f32[512]{0:T(512)}, u32[]{:S(2)}) copy-start(f32[512]{0:T(512)} %param.40) | copy-start | bytes 6148
  295.8 36.1 %copy-start.92 = (f32[512]{0:T(512)S(1)}, f32[512]{0:T(512)}, u32[]{:S(2)}) copy-start(f32[512]{0:T(512)} %param.41) | copy-start | bytes 6148
  301.3 209.4 %copy-start.49 = (f32[4,7,7,512]{3,2,1,0:T(8,128)}, f32[4,7,7,512]{3,2,1,0:T(8,128)S(1)}, u32[]{:S(2)}) copy-start(f32[4,7,7,512]{3,2,1,0:T(8,128)S(1)} %get-tuple-element.159) | copy-start | bytes 1204228
  331.9 61.8 %copy-start.62 = (f32[2048]{0:T(1024)S(1)}, f32[2048]{0:T(1024)}, u32[]{:S(2)}) copy-start(f32[2048]{0:T(1024)} %param.44) | copy-start | bytes 24580
  331.9 61.8 %copy-start.63 = (f32[2048]{0:T(1024)S(1)}, f32[2048]{0:T(1024)}, u32[]{:S(2)}) copy-start(f32[2048]{0:T(1024)} %param.42) | copy-start | bytes 24580
  331.9 61.8 %copy-start.78 = (f32[2048]{0:T(1024)S(1)}, f32[2048]{0:T(1024)}, u32[]{:S(2)}) copy-start(f32[2048]{0:T(1024)} %param.45) | copy-start | bytes 24580
  331.9 61.8 %copy-start.79 = (f32[2048]{0:T(1024)S(1)}, f32[2048]{0:T(1024)}, u32[]{:S(2)}) copy-start(f32[2048]{0:T(1024)} %param.43) | copy-start | bytes 24580
  400.5 5.2 copy-start.4
  400.5 5.2 copy-start.5
  401.3 4.0 collective-permute-start
  472.4 5.4 copy-start.44
  527.0 9.9 copy-start.31
  536.9 10.0 copy-start.30
  546.8 10.0 copy-start.29
  606.5 5.1 copy-start.14
  611.7 42.2 %copy-start.89 = (bf16[1024,512]{1,0:T(8,128)(2,1)S(1)}, bf16[1024,512]{1,0:T(8,128)(2,1)}, u32[]{:S(2)}) copy-start(bf16[1024,512]{1,0:T(8,128)(2,1)} %param.28) | copy-start | bytes 3145732
  653.8 9.4 copy-start.40
  694.6 5.1 copy-start.21
  694.6 5.1 copy-start.35
  694.6 5.1 copy-start.91
  701.8 32.9 %copy-start.34 = (bf16[3,3,256,256]{3,2,1,0:T(8,128)(2,1)S(1)}, bf16[3,3,256,256]{3,2,1,0:T(8,128)(2,1)}, u32[]{:S(2)}) copy-start(bf16[3,3,256,256]{3,2,1,0:T(8,128)(2,1)} %param.26) | copy-start | bytes 3538948
  744.1 5.7 copy-start.45
  744.1 5.7 copy-start.50
  753.8 5.1 copy-start.52
  753.8 5.1 copy-start.54
  753.8 5.1 copy-start.56
  761.4 34.4 %copy-start.82 = (f32[256]{0:T(256)S(1)}, f32[256]{0:T(256)}, u32[]{:S(2)}) copy-start(f32[256]{0:T(256)} %get-tuple-element.137) | copy-start | bytes 3076
  818.3 16.9 %slice-start = ((s8[9437184]{0:T(1024)(128)(4,1)}), s8[4194304]{0:T(1024)(128)(4,1)S(1)}, s32[]{:S(2)}) async-start(s8[9437184]{0:T(1024)(128)(4,1)} %bitcast.262), calls=%async_computation.1 | async-start | bytes 8388608
  823.6 5.6 copy-start.71
  823.6 5.6 copy-start.70
  823.6 5.7 copy-start.9
  823.6 11.5 slice-start.1
  823.6 11.5 slice-start.2
  853.8 430.9 %copy-start.1 = (bf16[512,2048]{1,0:T(8,128)(2,1)S(1)}, bf16[512,2048]{1,0:T(8,128)(2,1)}, u32[]{:S(2)}) copy-start(bf16[512,2048]{1,0:T(8,128)(2,1)} %param.30) | copy-start | bytes 6291460
  (50 other events, 134.0 us)
Sparse Core Ops, SparseCore 0:
  848.4 432.3 all-reduce.27
where the time goes:
time: 1300 us; the launch traced here: 1290 us
  blocking collectives  446 us (34%)
  waiting for transfers between devices  424 us (33%)
  local copies, waits for them, and re-layouts  250 us (19%)
  other arithmetic  85.7 us (7%)
  matrix products  69.5 us (5%)
  between operations  15.6 us (1%)
    unnamed x2, waiting for transfers between devices  421 us
    psum x6, blocking collectives, share_partials(): return lax.psum(partials, 'dp')  206 us
    psum x5, blocking collectives, share_moments(): return lax.psum(moments, 'dp')  205 us
    unnamed x242, local copies, waits for them, and re-layouts  110 us
    slice x9, local copies, waits for them, and re-layouts, tap_stride(): padded[:, row_pos:row_pos + height - 1:2, col_pos:col_pos + height - 1:2, :]  69.8 us
    psum x1, blocking collectives, per_device(): lax.psum((local_moments(reduced_a, mask_big), counts_here), 'dp')  34.9 us
    pad x3, local copies, waits for them, and re-layouts, tap_stride(): padded[:, row_pos:row_pos + height - 1:2, col_pos:col_pos + height - 1:2, :]  29.9 us
  transfers between devices with their start and end apart: 2, of which 2 were waited for; matrix products, arithmetic and copies ran while one was open for 1% of the time, Pallas kernels for 0%

commit v1 on v0

v1 whole, which is shorter than its diff:
```python
import functools

import jax
import jax.numpy as jnp
from jax import lax
from jax.experimental import pallas as pl
from jax.experimental.pallas import tpu as pltpu
from jax.sharding import PartitionSpec as P

eps_norm = 1e-05
eps_cos = 1e-06
loss_scale = 65536.0
low_type = jnp.bfloat16
full_type = jnp.float32
vmem_bytes = 40 * 1024 * 1024

even_width = 8


def call(body, outs, args, cost_us=2, scratch=()):
    whole = pl.BlockSpec(memory_space=pltpu.VMEM)
    sizes = [len(item) if isinstance(item, tuple) else None for item in args]
    flat = [one for item in args for one in (item if isinstance(item, tuple) else (item,))]

    def run(*refs):
        rest = iter(refs)
        given = [next(rest) if size is None else tuple(next(rest) for _ in range(size)) for size in sizes]
        body(*given, *rest)

    return pl.pallas_call(
        run,
        out_shape=outs,
        in_specs=[whole] * len(flat),
        out_specs=[whole] * len(outs),
        scratch_shapes=[pltpu.VMEM(dims, kind) for dims, kind in scratch],
        compiler_params=pltpu.CompilerParams(vmem_limit_bytes=vmem_bytes),
        cost_estimate=pl.CostEstimate(flops=int(cost_us * 1e9), bytes_accessed=int(cost_us * 1e6), transcendentals=0),
    )(*flat)


def shaped(*dims, kind=full_type):
    return jax.ShapeDtypeStruct(dims, kind)


def tail_parts(pre):
    size = jnp.abs(pre)
    base = 1.0 + (0.3275911 * 0.7071067811865476) * size
    guess = pl.reciprocal(base, approx=True)
    guess = guess * (2.0 - base * guess)
    guess = guess * (2.0 - base * guess)
    bell = jnp.exp(-0.5 * (pre * pre))
    series = 0.5 * 1.061405429
    for term in (-1.453152027, 1.421413741, -0.284496736, 0.254829592):
        series = series * guess + 0.5 * term
    return size, bell, series * guess * bell


def smooth(pre):
    size, _, tail = tail_parts(pre)
    return jnp.maximum(pre, 0.0) - size * tail


def smooth_slope(pre):
    _, bell, tail = tail_parts(pre)
    return jnp.where(pre >= 0.0, 1.0 - tail, tail) + 0.3989422804014327 * (pre * bell)


def wide(mask, width):
    return jnp.concatenate([mask] * (width // mask.shape[1]), axis=1)


def fold(value):
    rows, width = value.shape
    return jnp.sum(value.reshape(rows // 8, 8, width), axis=0)


def column_sum(value):
    return jnp.sum(value, axis=0, keepdims=True)


def total(parts):
    result = parts[0][...]
    for part in parts[1:]:
        result = result + part[...]
    return result


def statistics(sums, count):
    center = sums[0:1] / count
    inverse = lax.rsqrt(sums[1:2] / count - center * center + eps_norm)
    return center, inverse


def add_rows(store, row, value):
    store[row * 8 : row * 8 + 8, :] += fold(value)


def finish_rows(store, out_ref, rows):
    for row in range(rows):
        out_ref[row : row + 1, :] = column_sum(store[row * 8 : row * 8 + 8, :])


def times(lhs, rhs):
    return lax.dot_general(lhs, rhs, (((1,), (0,)), ((), ())), preferred_element_type=full_type)


def times_back(lhs, rhs):
    return lax.dot_general(lhs, rhs, (((1,), (1,)), ((), ())), preferred_element_type=full_type)


def times_rows(lhs, rhs):
    return lax.dot_general(lhs, rhs, (((0,), (0,)), ((), ())), preferred_element_type=full_type)


def low(value):
    return value.astype(low_type)


def enter_body(images, x_ref, mask_ref, filter_ref, start_ref, out_ref, sums_ref, store):
    height, pairs = x_ref.shape[0], x_ref.shape[1]
    depth = x_ref.shape[4]
    line = even_width * images
    blank = jnp.zeros((even_width - pairs, images, depth), low_type)
    store[...] = jnp.zeros_like(store)

    def step(index, carry):
        rows = pl.ds(pl.multiple_of(index * 4 * line, 4 * line), 4 * line)
        parts = []
        for row in range(2):
            for side in range(2):
                cells = jnp.concatenate([x_ref[index * 2 + row, :, side], blank], axis=0)
                parts.append(cells.reshape(line, depth))
        value = jnp.concatenate(parts, axis=0).astype(full_type) * wide(mask_ref[rows, :], depth)
        value = low(value)
        start_ref[rows, :] = value
        result = times(value, filter_ref[...])
        out_ref[rows, :] = result
        add_rows(store, 0, result)
        add_rows(store, 1, result * result)
        return carry

    lax.fori_loop(0, height // 2, step, 0)
    finish_rows(store, sums_ref, 2)


def split_store(even_ref, moved_ref, place, value, line):
    even, odd = value[:line], value[line:]
    even_ref[place, 0] = low(even)
    even_ref[place, 1] = low(odd)
    moved_ref[place, 0] = low(pltpu.roll(even, line - line // even_width, 0))
    moved_ref[place, 1] = low(pltpu.roll(odd, line // even_width, 0))


def blank_border(*refs):
    for ref in refs:
        empty = jnp.zeros(ref.shape[1:], ref.dtype)
        ref[0] = empty
        ref[ref.shape[0] - 1] = empty


def tap_sources(even_ref, moved_ref):
    return (
        ((moved_ref, 1), (even_ref, 0), (even_ref, 1)),
        ((even_ref, 0), (even_ref, 1), (moved_ref, 0)),
    )


def block_body(images, parts, u_ref, count_ref, scale_ref, shift_ref, mask_ref, filter_ref, even_ref, moved_ref, out_ref, sums_ref, store):
    depth = filter_ref.shape[1]
    line = even_width * images
    height = even_ref.shape[0] - 2
    center, inverse = statistics(total(parts), count_ref[0:1, 0:1])
    factor = scale_ref[...] * inverse
    shift = shift_ref[...]
    blank_border(even_ref, moved_ref)
    store[...] = jnp.zeros_like(store)

    def first(index, carry):
        rows = pl.ds(pl.multiple_of(index * 2 * line, 2 * line), 2 * line)
        pre = (u_ref[rows, :] - center) * factor + shift
        value = smooth(pre) * wide(mask_ref[rows, :], depth)
        split_store(even_ref, moved_ref, index + 1, value, line)
        return carry

    lax.fori_loop(0, height, first, 0)
    half = height // 2
    sources = tap_sources(even_ref, moved_ref)
    for side in range(2):
        for part in range(2):
            lhs = jnp.concatenate(
                [
                    ref[half * part + row : half * part + row + half, plane].reshape(half * line, depth)
                    for row in range(3)
                    for ref, plane in sources[side]
                ],
                axis=1,
            )
            result = times(lhs, filter_ref[...])
            for index in range(half):
                begin = (half * part + index) * 2 * line + side * line
                piece = result[index * line : index * line + line]
                out_ref[begin : begin + line, :] = piece
                kept = piece * wide(mask_ref[begin : begin + line, :], piece.shape[1])
                add_rows(store, 0, kept)
                add_rows(store, 1, kept * piece)
    finish_rows(store, sums_ref, 2)


def expand_body(parts, u_ref, count_ref, scale_ref, shift_ref, mask_ref, filter_ref, hidden_ref, out_ref, sums_ref, store, which, rows_step):
    center, inverse = statistics(total(parts), count_ref[which : which + 1, 0:1])
    factor = scale_ref[...] * inverse
    shift = shift_ref[...]
    depth = u_ref.shape[1]
    store[...] = jnp.zeros_like(store)

    def step(index, carry):
        rows = pl.ds(pl.multiple_of(index * rows_step, rows_step), rows_step)
        pre = (u_ref[rows, :] - center) * factor + shift
        value = low(smooth(pre) * wide(mask_ref[rows, :], depth))
        hidden_ref[rows, :] = value
        result = times(value, filter_ref[...])
        out_ref[rows, :] = result
        add_rows(store, 0, result)
        add_rows(store, 1, result * result)
        return carry

    lax.fori_loop(0, u_ref.shape[0] // rows_step, step, 0)
    finish_rows(store, sums_ref, 2)


def join_body(images, parts, u_ref, count_ref, scale_ref, shift_ref, mask_ref, start_ref, reduce_ref, side_ref, block_ref, reduced_ref, picked_ref, sided_ref, sums_ref, side_sums_ref, store, side_store):
    center, inverse = statistics(total(parts), count_ref[0:1, 0:1])
    factor = scale_ref[...] * inverse
    shift = shift_ref[...]
    depth = u_ref.shape[1]
    line = even_width * images
    store[...] = jnp.zeros_like(store)
    side_store[...] = jnp.zeros_like(side_store)

    def step(index, carry):
        rows = pl.ds(pl.multiple_of(index * 4 * line, 4 * line), 4 * line)
        pre = (u_ref[rows, :] - center) * factor + shift + start_ref[rows, :].astype(full_type)
        value = low(smooth(pre) * wide(mask_ref[rows, :], depth))
        block_ref[rows, :] = value
        picked_ref[pl.ds(pl.multiple_of(index * line, line), line), :] = value[:line]
        result = times(value, reduce_ref[...])
        reduced_ref[rows, :] = result
        add_rows(store, 0, result)
        add_rows(store, 1, result * result)
        return carry

    lax.fori_loop(0, u_ref.shape[0] // (4 * line), step, 0)
    finish_rows(store, sums_ref, 2)
    width = 512

    def side(index, carry):
        columns = pl.ds(pl.multiple_of(index * width, width), width)
        result = times(picked_ref[...], side_ref[:, columns])
        sided_ref[:, columns] = result
        side_sums_ref[0:1, columns] = column_sum(fold(result))
        side_sums_ref[1:2, columns] = column_sum(fold(result * result))
        return carry

    lax.fori_loop(0, side_ref.shape[1] // width, side, 0)


def shrink_body(images, parts, u_ref, count_ref, scale_ref, shift_ref, mask_ref, small_ref, filter_ref, even_ref, moved_ref, out_ref, sums_ref):
    depth = u_ref.shape[1]
    line = even_width * images
    height = even_ref.shape[0] - 2
    center, inverse = statistics(total(parts), count_ref[0:1, 0:1])
    factor = scale_ref[...] * inverse
    shift = shift_ref[...]
    blank_border(even_ref, moved_ref)

    def first(index, carry):
        rows = pl.ds(pl.multiple_of(index * 2 * line, 2 * line), 2 * line)
        pre = (u_ref[rows, :] - center) * factor + shift
        value = smooth(pre) * wide(mask_ref[rows, :], depth)
        split_store(even_ref, moved_ref, index + 1, value, line)
        return carry

    lax.fori_loop(0, height, first, 0)
    half = height // 2
    result = None
    for row in range(3):
        lhs = jnp.concatenate(
            [
                jnp.concatenate([ref[2 * index + row, plane] for index in range(half)], axis=0)
                for ref, plane in ((moved_ref, 1), (even_ref, 0), (even_ref, 1))
            ],
            axis=1,
        )
        term = times(lhs, filter_ref[row * 3 * depth : row * 3 * depth + 3 * depth, :])
        result = term if result is None else result + term
    out_ref[...] = result
    kept = result * wide(small_ref[...], result.shape[1])
    sums_ref[0:1, :] = column_sum(fold(kept))
    sums_ref[1:2, :] = column_sum(fold(kept * result))


def leave_body(images, parts, side_parts, u_ref, side_ref, count_ref, scale_ref, shift_ref, side_scale_ref, side_shift_ref, small_ref, pixel_ref, block_ref, joined_ref, pooled_ref, store):
    center, inverse = statistics(total(parts), count_ref[1:2, 0:1])
    factor = scale_ref[...] * inverse
    side_center, side_inverse = statistics(total(side_parts), count_ref[1:2, 0:1])
    side_factor = side_scale_ref[...] * side_inverse
    shift = shift_ref[...] + side_shift_ref[...]
    depth = u_ref.shape[1]
    line = even_width * images
    pairs = block_ref.shape[1]
    store[...] = jnp.zeros_like(store)

    def step(index, carry):
        rows = pl.ds(pl.multiple_of(index * line, line), line)
        pre = (u_ref[rows, :] - center) * factor + (side_ref[rows, :] - side_center) * side_factor + shift
        joined_ref[rows, :] = pre
        value = smooth(pre) * wide(small_ref[rows, :], depth)
        block_ref[index] = low(value).reshape(even_width, images, depth)[:pairs]
        add_rows(store, 0, value)
        return carry

    lax.fori_loop(0, u_ref.shape[0] // line, step, 0)
    summed = store[0:images, :]
    for begin in range(images, 8, images):
        summed = summed + store[begin : begin + images, :]
    pooled_ref[...] = summed * pixel_ref[:, 0:1]


def gather_images(store, row, images):
    summed = store[row * 8 : row * 8 + images, :]
    for begin in range(images, 8, images):
        summed = summed + store[row * 8 + begin : row * 8 + begin + images, :]
    return summed


def slope_sums_body(images, parts, side_parts, joined_ref, u_ref, side_ref, count_ref, small_ref, slope_ref, plain_ref, unit_ref, side_unit_ref, store):
    center, inverse = statistics(total(parts), count_ref[1:2, 0:1])
    side_center, side_inverse = statistics(total(side_parts), count_ref[1:2, 0:1])
    depth = u_ref.shape[1]
    line = even_width * images
    store[...] = jnp.zeros_like(store)

    def step(index, carry):
        rows = pl.ds(pl.multiple_of(index * line, line), line)
        slope = smooth_slope(joined_ref[rows, :]) * wide(small_ref[rows, :], depth)
        slope_ref[rows, :] = slope
        add_rows(store, 0, slope)
        add_rows(store, 1, slope * (u_ref[rows, :] - center))
        add_rows(store, 2, slope * (side_ref[rows, :] - side_center))
        return carry

    lax.fori_loop(0, u_ref.shape[0] // line, step, 0)
    plain_ref[...] = gather_images(store, 0, images)
    unit_ref[...] = gather_images(store, 1, images) * inverse
    side_unit_ref[...] = gather_images(store, 2, images) * side_inverse


def compare_body(pooled_ref, partner_ref, pixel_ref, plain_ref, unit_ref, side_unit_ref, loss_ref, grad_ref, sums_ref):
    pooled, partner = pooled_ref[...], partner_ref[...]
    inverse_own = lax.rsqrt(jnp.sum(pooled * pooled, axis=1, keepdims=True) + eps_cos)
    unit_own = pooled * inverse_own
    unit_other = partner * lax.rsqrt(jnp.sum(partner * partner, axis=1, keepdims=True) + eps_cos)
    cosine = jnp.sum(unit_own * unit_other, axis=1, keepdims=True)
    loss_ref[...] = jnp.broadcast_to(-0.5 * cosine, loss_ref.shape)
    grad = (-0.5 * loss_scale) * inverse_own * (unit_other - cosine * unit_own) * pixel_ref[:, 0:1]
    grad_ref[...] = grad
    sums_ref[0:1, :] = column_sum(grad * plain_ref[...])
    sums_ref[1:2, :] = column_sum(grad * unit_ref[...])
    sums_ref[2:3, :] = column_sum(grad * side_unit_ref[...])


def norm_back(sums, totals, count, scale):
    center, inverse = statistics(sums, count)
    factor = scale * inverse
    return center, inverse, factor, -(factor * inverse * totals[1:2] / count), -(factor * totals[0:1] / count)


def leave_back_body(images, parts, side_parts, grads, slope_ref, grad_ref, u_ref, side_ref, count_ref, scale_ref, side_scale_ref, small_ref, filter_ref, inner_parts, inner_u_ref, inner_slope_ref, low_ref, side_low_ref, out_ref, sums_ref, store):
    totals = total(grads)
    count = count_ref[1:2, 0:1]
    center, _, factor, along, level = norm_back(total(parts), totals, count, scale_ref[...])
    side_totals = jnp.concatenate([totals[0:1], totals[2:3]], axis=0)
    side_center, _, side_factor, side_along, side_level = norm_back(total(side_parts), side_totals, count, side_scale_ref[...])
    depth = u_ref.shape[1]
    line = even_width * images
    grad = jnp.concatenate([grad_ref[...]] * (line // images), axis=0)

    def step(index, carry):
        rows = pl.ds(pl.multiple_of(index * line, line), line)
        mask = wide(small_ref[rows, :], depth)
        joined = slope_ref[rows, :] * grad
        low_ref[rows, :] = low((joined * factor + (u_ref[rows, :] - center) * along + level) * mask)
        side_low_ref[rows, :] = low((joined * side_factor + (side_ref[rows, :] - side_center) * side_along + side_level) * mask)
        return carry

    lax.fori_loop(0, u_ref.shape[0] // line, step, 0)
    inner_center, inner_inverse = statistics(total(inner_parts), count)
    result = times_back(low_ref[...], filter_ref[...]) * inner_slope_ref[...]
    out_ref[...] = result
    sums_ref[0:1, :] = column_sum(fold(result))
    sums_ref[1:2, :] = column_sum(fold(result * (inner_u_ref[...] - inner_center))) * inner_inverse


def shrink_back_body(images, parts, grads, g_ref, u_ref, count_ref, scale_ref, small_ref, filter_ref, inner_parts, inner_u_ref, inner_slope_ref, low_ref, out_ref, sums_ref, store):
    depth = u_ref.shape[1]
    inner = filter_ref.shape[2]
    line = even_width * images
    half = u_ref.shape[0] // line
    center, _, factor, along, level = norm_back(total(parts), total(grads), count_ref[1:2, 0:1], scale_ref[...])
    exact = (g_ref[...] * factor + (u_ref[...] - center) * along + level) * wide(small_ref[...], depth)
    here = low(exact)
    low_ref[...] = here
    right = low(pltpu.roll(exact, exact.shape[0] - images, 0))
    blank = jnp.zeros((line, depth), low_type)
    below = jnp.concatenate([here[line:], blank], axis=0)
    below_right = jnp.concatenate([right[line:], blank], axis=0)
    inner_center, inner_inverse = statistics(total(inner_parts), count_ref[0:1, 0:1])
    store[...] = jnp.zeros_like(store)
    for row in range(2):
        for side in range(2):
            terms = [(here, 1 + row, 1 + side)]
            if side:
                terms.append((right, 1 + row, 0))
            if row:
                terms.append((below, 0, 1 + side))
            if row and side:
                terms.append((below_right, 0, 0))
            lhs = jnp.concatenate([value for value, _, _ in terms], axis=1)
            rhs = jnp.concatenate([filter_ref[down * 3 + over] for _, down, over in terms], axis=1)
            result = times_back(lhs, rhs)
            for index in range(half):
                begin = (index * 4 + row * 2 + side) * line
                rows = slice(begin, begin + line)
                piece = result[index * line : index * line + line] * inner_slope_ref[rows, :]
                out_ref[rows, :] = piece
                add_rows(store, 0, piece)
                add_rows(store, 1, piece * (inner_u_ref[rows, :] - inner_center))
    sums_ref[0:1, :] = column_sum(store[0:8, :])
    sums_ref[1:2, :] = column_sum(store[8:16, :]) * inner_inverse


def join_back_body(images, parts, grads, g_ref, u_ref, count_ref, scale_ref, mask_ref, filter_ref, picked_ref, inner_parts, inner_u_ref, inner_slope_ref, low_ref, out_ref, sums_ref, store):
    depth = u_ref.shape[1]
    line = even_width * images
    center, _, factor, along, level = norm_back(total(parts), total(grads), count_ref[0:1, 0:1], scale_ref[...])
    inner_center, inner_inverse = statistics(total(inner_parts), count_ref[0:1, 0:1])
    store[...] = jnp.zeros_like(store)

    def step(index, carry):
        rows = pl.ds(pl.multiple_of(index * 4 * line, 4 * line), 4 * line)
        value = low((g_ref[rows, :] * factor + (u_ref[rows, :] - center) * along + level) * wide(mask_ref[rows, :], depth))
        low_ref[rows, :] = value
        result = times_back(value, filter_ref[...])
        extra = picked_ref[pl.ds(pl.multiple_of(index * line, line), line), :]
        result = jnp.concatenate([result[:line] + extra, result[line:]], axis=0) * inner_slope_ref[rows, :]
        out_ref[rows, :] = result
        add_rows(store, 0, result)
        add_rows(store, 1, result * (inner_u_ref[rows, :] - inner_center))
        return carry

    lax.fori_loop(0, u_ref.shape[0] // (4 * line), step, 0)
    sums_ref[0:1, :] = column_sum(store[0:8, :])
    sums_ref[1:2, :] = column_sum(store[8:16, :]) * inner_inverse


def expand_back_body(parts, grads, g_ref, u_ref, count_ref, scale_ref, mask_ref, filter_ref, inner_parts, inner_u_ref, inner_slope_ref, low_ref, out_ref, sums_ref, store, rows_step):
    depth = u_ref.shape[1]
    center, _, factor, along, level = norm_back(total(parts), total(grads), count_ref[0:1, 0:1], scale_ref[...])
    inner_center, inner_inverse = statistics(total(inner_parts), count_ref[0:1, 0:1])
    store[...] = jnp.zeros_like(store)

    def step(index, carry):
        rows = pl.ds(pl.multiple_of(index * rows_step, rows_step), rows_step)
        value = low((g_ref[rows, :] * factor + (u_ref[rows, :] - center) * along + level) * wide(mask_ref[rows, :], depth))
        low_ref[rows, :] = value
        result = times_back(value, filter_ref[...]) * inner_slope_ref[rows, :]
        out_ref[rows, :] = result
        add_rows(store, 0, result)
        add_rows(store, 1, result * (inner_u_ref[rows, :] - inner_center))
        return carry

    lax.fori_loop(0, u_ref.shape[0] // rows_step, step, 0)
    sums_ref[0:1, :] = column_sum(store[0:8, :])
    sums_ref[1:2, :] = column_sum(store[8:16, :]) * inner_inverse


def block_back_body(images, parts, grads, g_ref, u_ref, count_ref, scale_ref, mask_ref, filter_ref, inner_parts, inner_u_ref, inner_slope_ref, low_ref, out_ref, sums_ref, even_ref, moved_ref, store):
    depth = u_ref.shape[1]
    line = even_width * images
    height = even_ref.shape[0] - 2
    center, _, factor, along, level = norm_back(total(parts), total(grads), count_ref[0:1, 0:1], scale_ref[...])
    inner_center, inner_inverse = statistics(total(inner_parts), count_ref[0:1, 0:1])
    blank_border(even_ref, moved_ref)
    store[...] = jnp.zeros_like(store)

    def first(index, carry):
        rows = pl.ds(pl.multiple_of(index * 2 * line, 2 * line), 2 * line)
        value = (g_ref[rows, :] * factor + (u_ref[rows, :] - center) * along + level) * wide(mask_ref[rows, :], depth)
        low_ref[rows, :] = low(value)
        split_store(even_ref, moved_ref, index + 1, value, line)
        return carry

    lax.fori_loop(0, height, first, 0)
    half = height // 2
    sources = tap_sources(even_ref, moved_ref)
    rhs = jnp.concatenate([filter_ref[8 - tap] for tap in range(9)], axis=1)
    for side in range(2):
        for part in range(2):
            lhs = jnp.concatenate(
                [
                    ref[half * part + row : half * part + row + half, plane].reshape(half * line, depth)
                    for row in range(3)
                    for ref, plane in sources[side]
                ],
                axis=1,
            )
            result = times_back(lhs, rhs)
            for index in range(half):
                begin = (half * part + index) * 2 * line + side * line
                rows = slice(begin, begin + line)
                piece = result[index * line : index * line + line] * inner_slope_ref[rows, :]
                out_ref[rows, :] = piece
                add_rows(store, 0, piece)
                add_rows(store, 1, piece * (inner_u_ref[rows, :] - inner_center))
    sums_ref[0:1, :] = column_sum(store[0:8, :])
    sums_ref[1:2, :] = column_sum(store[8:16, :]) * inner_inverse


def exit_body(images, parts, grads, g_ref, u_ref, count_ref, scale_ref, mask_ref, filter_ref, joined_ref, low_ref, out_ref):
    depth = u_ref.shape[1]
    pairs = out_ref.shape[1]
    line = even_width * images
    center, _, factor, along, level = norm_back(total(parts), total(grads), count_ref[0:1, 0:1], scale_ref[...])

    def step(index, carry):
        rows = pl.ds(pl.multiple_of(index * 4 * line, 4 * line), 4 * line)
        mask = mask_ref[rows, :]
        value = low((g_ref[rows, :] * factor + (u_ref[rows, :] - center) * along + level) * wide(mask, depth))
        low_ref[rows, :] = value
        result = low((times_back(value, filter_ref[...]) + joined_ref[rows, :]) * wide(mask, joined_ref.shape[1]))
        for row in range(2):
            for side in range(2):
                begin = (row * 2 + side) * line
                cells = result[begin : begin + line].reshape(even_width, images, result.shape[1])
                out_ref[index * 2 + row, :, side] = cells[:pairs]
        return carry

    lax.fori_loop(0, u_ref.shape[0] // (4 * line), step, 0)


def natural_body(images, value_ref, out_ref):
    pairs = out_ref.shape[1]
    line = even_width * images
    depth = value_ref.shape[1]

    def step(index, carry):
        for side in range(2):
            rows = pl.ds(pl.multiple_of(index * 2 * line + side * line, line), line)
            out_ref[index, :, side] = value_ref[rows, :].reshape(even_width, images, depth)[:pairs]
        return carry

    lax.fori_loop(0, out_ref.shape[0], step, 0)


def slope_body(parts, u_ref, count_ref, scale_ref, shift_ref, mask_ref, extras, out_ref, which, rows_step):
    center, inverse = statistics(total(parts), count_ref[which : which + 1, 0:1])
    factor = scale_ref[...] * inverse
    shift = shift_ref[...]
    depth = u_ref.shape[1]

    def step(index, carry):
        rows = pl.ds(pl.multiple_of(index * rows_step, rows_step), rows_step)
        pre = (u_ref[rows, :] - center) * factor + shift
        for extra_ref in extras:
            pre = pre + extra_ref[rows, :].astype(full_type)
        out_ref[rows, :] = smooth_slope(pre) * wide(mask_ref[rows, :], depth)
        return carry

    lax.fori_loop(0, u_ref.shape[0] // rows_step, step, 0)


def times_back_body(value_ref, filter_ref, out_ref):
    out_ref[...] = times_back(value_ref[...], filter_ref[...])


def filter_grad_body(value_ref, grad_ref, out_ref):
    out_ref[...] = times_rows(value_ref[...], grad_ref[...])


def block_filter_body(even_ref, moved_ref, grad_ref, out_ref):
    height, _, line, depth = even_ref.shape
    height = height - 2
    width = grad_ref.shape[1]
    grad = grad_ref[...].reshape(height, 2, line, width)
    grad = jnp.concatenate([grad[:, side].reshape(height * line, width) for side in range(2)], axis=0)
    sources = tap_sources(even_ref, moved_ref)
    for row in range(3):
        for over in range(3):
            lhs = jnp.concatenate(
                [
                    sources[side][over][0][row : row + height, sources[side][over][1]].reshape(height * line, depth)
                    for side in range(2)
                ],
                axis=0,
            )
            out_ref[row * 3 + over] = times_rows(lhs, grad)


def shrink_filter_body(even_ref, moved_ref, grad_ref, out_ref):
    half = even_ref.shape[0] // 2 - 1
    for row in range(3):
        for over, (ref, plane) in enumerate(((moved_ref, 1), (even_ref, 0), (even_ref, 1))):
            lhs = jnp.concatenate([ref[2 * index + row, plane] for index in range(half)], axis=0)
            out_ref[row * 3 + over] = times_rows(lhs, grad_ref[...])


def exchange(value, axis, bits):
    return lax.ppermute(value, axis, [(i, i ^ bits) for i in range(lax.axis_size(axis))])


def share(sums):
    size = lax.axis_size("dp")
    if size > 1:
        sums = sums + exchange(sums, "dp", 1)
    if size > 2:
        sums = sums + exchange(sums, "dp", 3)
    parts = (sums,)
    bit = 4
    while bit < size:
        if len(parts) > 1:
            parts = (sum(parts[1:], parts[0]),)
        steps = [bit + 1, 2 * bit + 1, 3 * bit + 1] if 2 * bit < size else [bit + 1]
        parts = parts + tuple(exchange(parts[0], "dp", step) for step in steps)
        bit *= 4
    return parts


def pack_flat(parts):
    return jnp.concatenate([part.reshape(-1) for part in parts])


def as_row(value):
    return value.reshape(1, -1)


def per_device(
    inputs,
    resolution,
    reduce_a,
    spatial_a,
    expand_a,
    reduce_b,
    spatial_b,
    expand_b,
    shortcut_b,
    scale_reduce_a,
    shift_reduce_a,
    scale_spatial_a,
    shift_spatial_a,
    scale_expand_a,
    shift_expand_a,
    scale_reduce_b,
    shift_reduce_b,
    scale_spatial_b,
    shift_spatial_b,
    scale_expand_b,
    shift_expand_b,
    scale_shortcut,
    shift_shortcut,
):
    images, height, depth_a = inputs.shape[1], inputs.shape[2], inputs.shape[4]
    pairs = height // 2
    middle_a, middle_b, depth_b = reduce_a.shape[1], reduce_b.shape[1], shortcut_b.shape[1]
    line = even_width * images
    rows_big, rows_small = height * 2 * line, pairs * line
    sizes = resolution[0]
    places_h = jnp.arange(height).reshape(height, 1, 1, 1, 1)
    places_w = (2 * jnp.arange(even_width) + jnp.arange(2).reshape(2, 1)).reshape(1, 2, even_width, 1, 1)
    bound = (sizes // 16).reshape(1, 1, 1, images, 1)
    mask_big = ((places_h < bound) & (places_w < bound)).astype(full_type)
    count_big = jnp.sum(mask_big)
    mask_big = jnp.broadcast_to(mask_big, (height, 2, even_width, images, 128)).reshape(rows_big, 128)
    places_h = jnp.arange(pairs).reshape(pairs, 1, 1, 1)
    places_w = jnp.arange(even_width).reshape(1, even_width, 1, 1)
    bound = (sizes // 32).reshape(1, 1, images, 1)
    mask_small = ((places_h < bound) & (places_w < bound)).astype(full_type)
    count_small = jnp.sum(mask_small)
    mask_small = jnp.broadcast_to(mask_small, (pairs, even_width, images, 128)).reshape(rows_small, 128)
    pixel = 1.0 / (sizes // 32 * (sizes // 32)).astype(full_type)
    pixel = jnp.broadcast_to(pixel.reshape(images, 1), (images, 128))
    counts = jnp.broadcast_to(jnp.stack([count_big, count_small]).reshape(2, 1), (2, 128))
    counts = sum(share(counts)[1:], share(counts)[0])
    spatial_a9 = spatial_a.reshape(9, middle_a, middle_a)
    spatial_b9 = spatial_b.reshape(9, middle_b, middle_b)
    cells = inputs[0].transpose(1, 2, 0, 3).reshape(height, pairs, 2, images, depth_a)

    def padded(width):
        return shaped(height + 2, 2, line, width, kind=low_type)

    def with_images(body):
        return functools.partial(body, images)

    start, reduced_a, sums = call(
        with_images(enter_body),
        [shaped(rows_big, depth_a, kind=low_type), shaped(rows_big, middle_a), shaped(2, middle_a)],
        [cells, mask_big, reduce_a],
        scratch=[((16, middle_a), full_type)],
    )
    sums_ra = share(sums)
    scale_ra, shift_ra = as_row(scale_reduce_a), as_row(shift_reduce_a)
    even_a, moved_a, mixed_a, sums = call(
        with_images(block_body),
        [padded(middle_a), padded(middle_a), shaped(rows_big, middle_a), shaped(2, middle_a)],
        [sums_ra, reduced_a, counts, scale_ra, shift_ra, mask_big, spatial_a.reshape(9 * middle_a, middle_a)],
        scratch=[((16, middle_a), full_type)],
    )
    sums_sa = share(sums)
    scale_sa, shift_sa = as_row(scale_spatial_a), as_row(shift_spatial_a)
    hidden_two_a, expanded_a, sums = call(
        functools.partial(expand_body, which=0, rows_step=4 * line),
        [shaped(rows_big, middle_a, kind=low_type), shaped(rows_big, depth_a), shaped(2, depth_a)],
        [sums_sa, mixed_a, counts, scale_sa, shift_sa, mask_big, expand_a],
        scratch=[((16, depth_a), full_type)],
    )
    sums_ea = share(sums)
    scale_ea, shift_ea = as_row(scale_expand_a), as_row(shift_expand_a)
    block_a, reduced_b, picked, side_b, sums, side_sums = call(
        with_images(join_body),
        [
            shaped(rows_big, depth_a, kind=low_type),
            shaped(rows_big, middle_b),
            shaped(rows_small, depth_a, kind=low_type),
            shaped(rows_small, depth_b),
            shaped(2, middle_b),
            shaped(2, depth_b),
        ],
        [sums_ea, expanded_a, counts, scale_ea, shift_ea, mask_big, start, reduce_b, shortcut_b],
        scratch=[((16, middle_b), full_type), ((16, 128), full_type)],
    )
    shared = share(jnp.concatenate([sums, side_sums], axis=1))
    sums_rb = tuple(part[:, :middle_b] for part in shared)
    sums_sc = tuple(part[:, middle_b:] for part in shared)
    scale_rb, shift_rb = as_row(scale_reduce_b), as_row(shift_reduce_b)
    scale_sc, shift_sc = as_row(scale_shortcut), as_row(shift_shortcut)
    even_b, moved_b, mixed_b, sums = call(
        with_images(shrink_body),
        [padded(middle_b), padded(middle_b), shaped(rows_small, middle_b), shaped(2, middle_b)],
        [sums_rb, reduced_b, counts, scale_rb, shift_rb, mask_big, mask_small, spatial_b.reshape(9 * middle_b, middle_b)],
    )
    sums_sb = share(sums)
    scale_sb, shift_sb = as_row(scale_spatial_b), as_row(shift_spatial_b)
    hidden_two_b, expanded_b, sums = call(
        functools.partial(expand_body, which=1, rows_step=line),
        [shaped(rows_small, middle_b, kind=low_type), shaped(rows_small, depth_b), shaped(2, depth_b)],
        [sums_sb, mixed_b, counts, scale_sb, shift_sb, mask_small, expand_b],
        scratch=[((16, depth_b), full_type)],
    )
    sums_eb = share(sums)
    scale_eb, shift_eb = as_row(scale_expand_b), as_row(shift_expand_b)
    block_b, joined_b, pooled = call(
        with_images(leave_body),
        [shaped(pairs, pairs, images, depth_b, kind=low_type), shaped(rows_small, depth_b), shaped(images, depth_b)],
        [sums_eb, sums_sc, expanded_b, side_b, counts, scale_eb, shift_eb, scale_sc, shift_sc, mask_small, pixel],
        scratch=[((8, depth_b), full_type)],
    )
    partner = exchange(pooled, "view", 1)
    slope_b, plain, unit, side_unit = call(
        with_images(slope_sums_body),
        [shaped(rows_small, depth_b)] + [shaped(images, depth_b)] * 3,
        [sums_eb, sums_sc, joined_b, expanded_b, side_b, counts, mask_small],
        scratch=[((24, depth_b), full_type)],
    )
    loss, grad_out, sums = call(
        compare_body,
        [shaped(images, 128), shaped(images, depth_b), shaped(3, depth_b)],
        [pooled, partner, pixel, plain, unit, side_unit],
        cost_us=1,
    )
    grads_eb = share(sums)

    def slope(parts, value, scale, shift, mask, extras, which, rows_step):
        return call(
            functools.partial(slope_body, which=which, rows_step=rows_step),
            [shaped(*value.shape)],
            [parts, value, counts, scale, shift, mask, extras],
        )[0]

    slope_sb = slope(sums_sb, mixed_b, scale_sb, shift_sb, mask_small, (), 1, line)
    slope_rb = slope(sums_rb, reduced_b, scale_rb, shift_rb, mask_big, (), 0, 2 * line)
    slope_ea = slope(sums_ea, expanded_a, scale_ea, shift_ea, mask_big, (start,), 0, 2 * line)
    slope_sa = slope(sums_sa, mixed_a, scale_sa, shift_sa, mask_big, (), 0, 2 * line)
    slope_ra = slope(sums_ra, reduced_a, scale_ra, shift_ra, mask_big, (), 0, 2 * line)

    low_eb, low_sc, grad_sb, sums = call(
        with_images(leave_back_body),
        [
            shaped(rows_small, depth_b, kind=low_type),
            shaped(rows_small, depth_b, kind=low_type),
            shaped(rows_small, middle_b),
            shaped(2, middle_b),
        ],
        [
            sums_eb,
            sums_sc,
            grads_eb,
            slope_b,
            grad_out,
            expanded_b,
            side_b,
            counts,
            scale_eb,
            scale_sc,
            mask_small,
            expand_b,
            sums_sb,
            mixed_b,
            slope_sb,
        ],
        scratch=[((8, 128), full_type)],
    )
    grads_sb = share(sums)
    low_sb, grad_rb, sums = call(
        with_images(shrink_back_body),
        [shaped(rows_small, middle_b, kind=low_type), shaped(rows_big, middle_b), shaped(2, middle_b)],
        [sums_sb, grads_sb, grad_sb, mixed_b, counts, scale_sb, mask_small, spatial_b9, sums_rb, reduced_b, slope_rb],
        scratch=[((16, middle_b), full_type)],
    )
    grads_rb = share(sums)
    grad_picked = call(times_back_body, [shaped(rows_small, depth_a)], [low_sc, shortcut_b])[0]
    low_rb, joined_grad, sums = call(
        with_images(join_back_body),
        [shaped(rows_big, middle_b, kind=low_type), shaped(rows_big, depth_a), shaped(2, depth_a)],
        [sums_rb, grads_rb, grad_rb, reduced_b, counts, scale_rb, mask_big, reduce_b, grad_picked, sums_ea, expanded_a, slope_ea],
        scratch=[((16, depth_a), full_type)],
    )
    grads_ea = share(sums)
    low_ea, grad_sa, sums = call(
        functools.partial(expand_back_body, rows_step=4 * line),
        [shaped(rows_big, depth_a, kind=low_type), shaped(rows_big, middle_a), shaped(2, middle_a)],
        [sums_ea, grads_ea, joined_grad, expanded_a, counts, scale_ea, mask_big, expand_a, sums_sa, mixed_a, slope_sa],
        scratch=[((16, middle_a), full_type)],
    )
    grads_sa = share(sums)
    low_sa, grad_ra, sums = call(
        with_images(block_back_body),
        [shaped(rows_big, middle_a, kind=low_type), shaped(rows_big, middle_a), shaped(2, middle_a)],
        [sums_sa, grads_sa, grad_sa, mixed_a, counts, scale_sa, mask_big, spatial_a9, sums_ra, reduced_a, slope_ra],
        scratch=[
            ((height + 2, 2, line, middle_a), low_type),
            ((height + 2, 2, line, middle_a), low_type),
            ((16, middle_a), full_type),
        ],
    )
    grads_ra = share(sums)
    low_ra, input_grad = call(
        with_images(exit_body),
        [shaped(rows_big, middle_a, kind=low_type), shaped(height, pairs, 2, images, depth_a, kind=low_type)],
        [sums_ra, grads_ra, grad_ra, reduced_a, counts, scale_ra, mask_big, reduce_a, joined_grad],
    )

    def filter_grad(value, grad):
        return call(filter_grad_body, [shaped(value.shape[1], grad.shape[1])], [value, grad])[0]

    grad_expand_b = filter_grad(hidden_two_b, low_eb)
    grad_shortcut = filter_grad(picked, low_sc)
    grad_spatial_b = call(shrink_filter_body, [shaped(9, middle_b, middle_b)], [even_b, moved_b, low_sb])[0]
    grad_reduce_b = filter_grad(block_a, low_rb)
    grad_expand_a = filter_grad(hidden_two_a, low_ea)
    grad_spatial_a = call(block_filter_body, [shaped(9, middle_a, middle_a)], [even_a, moved_a, low_sa])[0]
    grad_reduce_a = filter_grad(start, low_ra)
    block_out = call(
        with_images(natural_body), [shaped(height, pairs, 2, images, depth_a, kind=low_type)], [block_a]
    )[0]

    def both_views(parts):
        value = sum(parts[1:], parts[0])
        return value + exchange(value, "view", 1)

    def once(value):
        first = (lax.axis_index("dp") == 0) & (lax.axis_index("view") == 0)
        return jnp.where(first, value, 0.0)

    all_eb = both_views(grads_eb)
    late_flat = pack_flat(
        [grad_reduce_b, grad_spatial_b, grad_expand_b, grad_shortcut]
        + [once(v) for v in (both_views(grads_rb), both_views(grads_sb), all_eb[:2], all_eb[0], all_eb[2])]
    )
    early_flat = pack_flat(
        [grad_reduce_a, grad_spatial_a, grad_expand_a]
        + [once(v) for v in (both_views(grads_ra), both_views(grads_sa), both_views(grads_ea))]
    )
    late_done = lax.psum_scatter(late_flat, ("view", "dp"), scatter_dimension=0, tiled=True)
    early_done = lax.psum_scatter(early_flat, ("view", "dp"), scatter_dimension=0, tiled=True)

    def natural(value):
        return value.reshape(height, height, images, depth_a).transpose(2, 0, 1, 3)[None]

    return (
        loss[:, 0][None],
        natural(block_out),
        block_b.transpose(2, 0, 1, 3)[None],
        natural(input_grad),
        early_done,
        late_done,
    )


def solution(mesh):
    copied = (P(),) * 21
    images = P("view", "dp", None, None, None)
    packed = P(("view", "dp"))
    return jax.shard_map(
        per_device,
        mesh=mesh,
        in_specs=(images, P("view", "dp")) + copied,
        out_specs=(P("view", "dp"), images, images, images, packed, packed),
        check_vma=False,
    )
```

time: 1300 us -> 750 us (0.58)
  blocking collectives: 446 us -> 0 us
  local copies, waits for them, and re-layouts: 250 us -> 100 us
  other arithmetic: 85.7 us -> 7.2 us
  starting transfers between devices: 1.62 us -> 77.8 us
  matrix products: 69.5 us -> 0 us
  Pallas kernels: 0 us -> 68.4 us
  waiting for transfers between devices: 424 us -> 480 us
    psum x12 -> x0, blocking collectives: 446 us -> none  [the longest x6 206 us: share_partials(): return lax.psum(partials, 'dp')]
    slice x11 -> x9, local copies, waits for them, and re-layouts: 82.6 us -> 0.65 us  [the longest x1 0.63 us: per_device(): loss[:, 0][None]]
    ppermute x1 -> x72, starting transfers between devices: 1.58 us -> 77.8 us  [exchange(): lax.ppermute(value, axis, [(i, i ^ bits) for i in range(lax.axis_size(axi...]
    dot_general x21 -> x0, matrix products: 69.5 us -> none  [the longest x7 23.8 us: matmul_back(): jnp.einsum('pd,cd->pc', flat, weight, preferred_element_type=jnp.float32)]
    pallas_call x0 -> x29, Pallas kernels: none -> 68.4 us  [call(): pl.pallas_call(run, out_shape=outs, in_specs=[whole] * len(flat), out_spe...]
    pad x6 -> x0, local copies, waits for them, and re-layouts: 50 us -> none  [the longest x3 29.9 us: tap_stride(): padded[:, row_pos:row_pos + height - 1:2, col_pos:col_pos + height - 1:2, :]]
    ppermute x1 -> x72, waiting for transfers between devices: 2.39 us -> 49 us  [exchange(): lax.ppermute(value, axis, [(i, i ^ bits) for i in range(lax.axis_size(axi...]
    convert_element_type x13 -> x2, other arithmetic: 41.7 us -> 0.02 us  [the longest x1 0.01 us: per_device(): mask_big = ((places_h < bound) & (places_w < bound)).astype(full_type)]
  transfers between devices with their start and end apart: 2 -> 73, of which waited for: 2 -> 31; matrix products, arithmetic and copies ran while one was open for 1% -> 6% of each run, Pallas kernels for 0% -> 5%
where the time goes in v1:
time: 750 us; the launch traced here: 749 us
  waiting for transfers between devices  480 us (64%)
  local copies, waits for them, and re-layouts  100 us (13%)
  starting transfers between devices  77.8 us (10%)
  Pallas kernels  68.4 us (9%)
  between operations  15.5 us (2%)
    unnamed x2, waiting for transfers between devices  431 us
    unnamed x286, local copies, waits for them, and re-layouts  97.7 us
    ppermute x72, starting transfers between devices, exchange(): lax.ppermute(value, axis, [(i, i ^ bits) for i in range(lax.axis_size(axi...  77.8 us
    pallas_call x29, Pallas kernels, call(): pl.pallas_call(run, out_shape=outs, in_specs=[whole] * len(flat), out_spe...  68.4 us
    ppermute x72, waiting for transfers between devices, exchange(): lax.ppermute(value, axis, [(i, i ^ bits) for i in range(lax.axis_size(axi...  49 us
  transfers between devices with their start and end apart: 73, of which 31 were waited for; matrix products, arithmetic and copies ran while one was open for 6% of the time, Pallas kernels for 5%

profile of v1, /device:TPU:0, one launch (start us, length us, event | category | flops | bytes accessed | tf_op | source)
XLA Modules:
  0.0 749.2 jit_solution(3009638114143645906)
XLA Ops:
  17.9 2.6 collective-permute-start.6
  21.8 3.9 collective-permute-start.9
  27.6 2.6 collective-permute-start.3
  31.5 3.5 collective-permute-done.4.refs_3_.refs_17_
  35.0 2.5 shard_map.263
  44.3 3.3 collective-permute-start.14
  49.1 2.7 shard_map.264
  56.9 3.5 collective-permute-start.18
  61.8 3.5 collective-permute-done.19.refs_3_.refs_18_
  65.4 9.4 %shard_map.265 = (bf16[896,1024]{1,0:T(8,128)(2,1)S(1)}, f32[896,512]{1,0:T(8,128)S(1)}, bf16[224,1024]{1,0:T(8,128)(2,1)S(1)}, f32[224,2048]{1,0:T(8,128)S(1)},...) custom-call(f32[2,1024]{1,0:T(2,128)S(1)} %add.208.refs_0_.refs_15_, ...), custom_call_target="tpu_custom_call" | custom-call | flops 2000000000 | bytes 2000000 | tf_op jit(solution)/shard_map/pallas_call | solution.py:30
  84.7 3.3 collective-permute-start.24
  92.1 2.3 copy-done.10
  94.4 3.7 shard_map.266
  102.5 3.4 collective-permute-start.28
  107.2 3.5 collective-permute-done.29.refs_3_.refs_24_
  112.1 3.4 shard_map.267
  128.5 3.1 collective-permute-start.34
  136.5 3.6 shard_map.268
  141.6 2.6 shard_map.269
  145.6 4.7 shard_map.277.refs_20_
  152.8 2.3 shard_map.274.refs_19_
  157.4 2.8 collective-permute-start.40
  162.9 2.4 shard_map.273
  171.9 2.9 collective-permute-start.44
  176.4 2.8 copy.40
  179.3 5.2 copy.41
  185.0 2.3 copy-done.11
  194.7 3.7 copy-done.4
  198.4 9.9 %copy.39 = f32[576,4,8,128]{3,1,2,0:T(4,128)} copy(f32[576,4,8,128]{3,2,1,0:T(8,128)} %bitcast.90) | data formatting | bytes 18874368
  208.4 3.2 collective-permute-start.49
  212.9 3.5 collective-permute-done.50.refs_7_
  216.4 2.0 copy-done.2
  222.6 5.8 shard_map.278
  234.0 8.6 %constant_dynamic-update-slice_fusion.15 = f32[6039552]{0:T(1024)} fusion(f32[6039552]{0:T(1024)} %constant_dynamic-update-slice_fusion.3, f32[2359296]{0:T(1024)} %bitcast.133), kind=kLoop, calls=%fused_computation.28 | loop fusion | bytes 18874368
  242.6 2.4 constant_dynamic-update-slice_fusion.14
  246.4 4.4 constant_dynamic-update-slice_fusion.13
  252.8 2.5 collective-permute-done.52
  256.5 2.6 collective-permute-start.55
  261.4 2.5 shard_map.280
  265.4 2.7 collective-permute-done.57
  268.1 3.2 collective-permute-start.59
  276.2 2.0 shard_map.282
  282.4 2.8 collective-permute-done.62
  286.5 2.6 collective-permute-start.65
  289.2 2.1 collective-permute-done.65.refs_7_
  291.3 3.4 shard_map.283
  307.6 430.8 %all-reduce.5.cloned.1.call-done = (f32[1117184]{0:T(1024)}, f32[6039552]{0:T(1024)}) async-done(((f32[1117184]{0:T(1024)}, f32[6039552]{0:T(1024)}), (f32[1117184]{0:T(1024)}, f32[6039552]{0:T(1024)})) %all-reduce.5.cloned.1.call-update) | async-done | bytes 28626960
  740.1 2.3 dynamic-slice.1
  (490 shorter events, 139.0 us)
Async XLA Ops:
  7.2 731.2 %all-reduce.5.cloned.1.call-start = ((), (), s32[]{:S(2)}) async-start(), calls=%async_computation | async-start | bytes 57253888
  12.7 5.2 collective-permute-start.5
  20.5 5.9 collective-permute-start.1
  21.8 8.4 %collective-permute-start.9 = (f32[2,128]{1,0:T(2,128)S(1)}, f32[2,128]{1,0:T(2,128)S(1)}, u32[]{:S(2)}, u32[]{:S(2)}) collective-permute-start(f32[2,128]{1,0:T(2,128)S(1)} %fusion.1), channel_id=1, source_target_pairs={{0,13},{1,12},{2,15},{3,14},{4,9},{5,8},{6,11},{7,10},{8,5},{9,4},... | collective-permute-start | bytes 3080 | tf_op jit(solution)/shard_map/ppermute | solution.py:618
  25.7 4.8 collective-permute-start.8
  25.7 4.8 collective-permute-start.7
  26.3 4.2 collective-permute-start.2
  30.2 4.8 collective-permute-start.4
  43.5 4.1 collective-permute-start.12
  43.5 4.1 collective-permute-start.13
  44.3 4.8 collective-permute-start.14
  56.9 4.9 collective-permute-start.18
  60.5 4.9 collective-permute-start.19
  83.9 4.2 collective-permute-start.22
  84.0 4.2 collective-permute-start.23
  84.7 5.1 collective-permute-start.24
  102.5 4.7 collective-permute-start.28
  105.9 4.8 collective-permute-start.29
  119.5 8.1 %collective-permute-start.31 = (f32[2,2048]{1,0:T(2,128)S(1)}, f32[2,2048]{1,0:T(2,128)S(1)}, u32[]{:S(2)}, u32[]{:S(2)}) collective-permute-start(f32[2,2048]{1,0:T(2,128)S(1)} %add.213), channel_id=1, source_target_pairs={{0,3},{1,2},{2,1},{3,0},{4,7},{5,6},{6,5},{7,4},{8,11},{9,10},{10,... | collective-permute-start | bytes 49160 | tf_op jit(solution)/shard_map/ppermute | solution.py:618
  127.7 8.7 %collective-permute-start.32 = (f32[2,2048]{1,0:T(2,128)S(1)}, f32[2,2048]{1,0:T(2,128)S(1)}, u32[]{:S(2)}, u32[]{:S(2)}) collective-permute-start(f32[2,2048]{1,0:T(2,128)S(1)} %add.214.refs_0_), channel_id=1, source_target_pairs={{0,5},{1,4},{2,7},{3,6},{4,1},{5,0},{6,3},{7,2},{8,13},{9,12},{10,... | collective-permute-start | bytes 49160 | tf_op jit(solution)/shard_map/ppermute | solution.py:618
  127.7 8.6 %collective-permute-start.33 = (f32[2,2048]{1,0:T(2,128)S(1)}, f32[2,2048]{1,0:T(2,128)S(1)}, u32[]{:S(2)}, u32[]{:S(2)}) collective-permute-start(f32[2,2048]{1,0:T(2,128)S(1)} %add.214.refs_0_), channel_id=1, source_target_pairs={{0,9},{1,8},{2,11},{3,10},{4,13},{5,12},{6,15},{7,14},{8,1},{9,0},... | collective-permute-start | bytes 49160 | tf_op jit(solution)/shard_map/ppermute | solution.py:618
  128.5 7.9 %collective-permute-start.34 = (f32[2,2048]{1,0:T(2,128)S(1)}, f32[2,2048]{1,0:T(2,128)S(1)}, u32[]{:S(2)}, u32[]{:S(2)}) collective-permute-start(f32[2,2048]{1,0:T(2,128)S(1)} %add.214.refs_0_), channel_id=1, source_target_pairs={{0,13},{1,12},{2,15},{3,14},{4,9},{5,8},{6,11},{7,10},{8,5},{9,4},... | collective-permute-start | bytes 49160 | tf_op jit(solution)/shard_map/ppermute | solution.py:618
  140.1 4.1 collective-permute-start.35
  145.5 6.5 collective-permute-start.36
  152.1 4.3 collective-permute-start.37
  156.4 4.6 collective-permute-start.38
  156.5 4.5 collective-permute-start.39
  157.4 5.5 collective-permute-start.40
  171.6 13.4 %collective-permute-start.43 = (f32[2,512]{1,0:T(2,128)S(1)}, f32[2,512]{1,0:T(2,128)S(1)}, u32[]{:S(2)}, u32[]{:S(2)}) collective-permute-start(f32[2,512]{1,0:T(2,128)S(1)} %add.218.refs_4_), channel_id=1, source_target_pairs={{0,5},{1,4},{2,7},{3,6},{4,1},{5,0},{6,3},{7,2},{8,13},{9,12},{10,... | collective-permute-start | bytes 12296 | tf_op jit(solution)/shard_map/ppermute | solution.py:618
  171.9 13.2 %collective-permute-start.44 = (f32[2,512]{1,0:T(2,128)S(1)}, f32[2,512]{1,0:T(2,128)S(1)}, u32[]{:S(2)}, u32[]{:S(2)}) collective-permute-start(f32[2,512]{1,0:T(2,128)S(1)} %add.218.refs_4_), channel_id=1, source_target_pairs={{0,9},{1,8},{2,11},{3,10},{4,13},{5,12},{6,15},{7,14},{8,1},{9,0},... | collective-permute-start | bytes 12296 | tf_op jit(solution)/shard_map/ppermute | solution.py:618
  174.8 10.2 %collective-permute-start.45 = (f32[2,512]{1,0:T(2,128)S(1)}, f32[2,512]{1,0:T(2,128)S(1)}, u32[]{:S(2)}, u32[]{:S(2)}) collective-permute-start(f32[2,512]{1,0:T(2,128)S(1)} %add.218.refs_4_), channel_id=1, source_target_pairs={{0,13},{1,12},{2,15},{3,14},{4,9},{5,8},{6,11},{7,10},{8,5},{9,4},... | collective-permute-start | bytes 12296 | tf_op jit(solution)/shard_map/ppermute | solution.py:618
  184.5 48.7 %collective-permute-start.71 = (f32[3,2048]{1,0:T(4,128)}, f32[3,2048]{1,0:T(4,128)}, u32[]{:S(2)}, u32[]{:S(2)}) collective-permute-start(f32[3,2048]{1,0:T(4,128)} %add_add_fusion), channel_id=1, source_target_pairs={{0,16},{16,0},{1,17},{17,1},{2,18},{18,2},{3,19},{19,3},{4,20},{20... | collective-permute-start | bytes 73736 | tf_op jit(solution)/shard_map/ppermute | solution.py:618
  190.4 22.1 %collective-permute-start.70 = (f32[2,512]{1,0:T(2,128)S(1)}, f32[2,512]{1,0:T(2,128)S(1)}, u32[]{:S(2)}, u32[]{:S(2)}) collective-permute-start(f32[2,512]{1,0:T(2,128)S(1)} %add_add_fusion.2), channel_id=1, source_target_pairs={{0,16},{16,0},{1,17},{17,1},{2,18},{18,2},{3,19},{19,3},{4,20},{20... | collective-permute-start | bytes 12296 | tf_op jit(solution)/shard_map/ppermute | solution.py:618
  191.9 16.4 %collective-permute-start.47 = (f32[2,512]{1,0:T(2,128)S(1)}, f32[2,512]{1,0:T(2,128)S(1)}, u32[]{:S(2)}, u32[]{:S(2)}) collective-permute-start(f32[2,512]{1,0:T(2,128)S(1)} %add.219), channel_id=1, source_target_pairs={{0,3},{1,2},{2,1},{3,0},{4,7},{5,6},{6,5},{7,4},{8,11},{9,10},{10,... | collective-permute-start | bytes 12296 | tf_op jit(solution)/shard_map/ppermute | solution.py:618
  208.3 4.2 collective-permute-start.48
  208.4 4.5 collective-permute-start.49
  211.6 4.8 collective-permute-start.50
  228.4 23.7 %collective-permute-start.51 = (f32[2,1024]{1,0:T(2,128)S(1)}, f32[2,1024]{1,0:T(2,128)S(1)}, u32[]{:S(2)}, u32[]{:S(2)}) collective-permute-start(f32[2,1024]{1,0:T(2,128)S(1)} %get-tuple-element.88), channel_id=1, source_target_pairs={{0,1},{1,0},{2,3},{3,2},{4,5},{5,4},{6,7},{7,6},{8,9},{9,8},{10,11... | collective-permute-start | bytes 24584 | tf_op jit(solution)/shard_map/ppermute | solution.py:618
  232.1 18.7 %collective-permute-start.69 = (f32[2,512]{1,0:T(2,128)S(1)}, f32[2,512]{1,0:T(2,128)S(1)}, u32[]{:S(2)}, u32[]{:S(2)}) collective-permute-start(f32[2,512]{1,0:T(2,128)S(1)} %add_add_fusion.3), channel_id=1, source_target_pairs={{0,16},{16,0},{1,17},{17,1},{2,18},{18,2},{3,19},{19,3},{4,20},{20... | collective-permute-start | bytes 12296 | tf_op jit(solution)/shard_map/ppermute | solution.py:618
  255.2 4.4 collective-permute-start.53
  255.2 4.4 collective-permute-start.54
  256.5 4.9 collective-permute-start.55
  268.1 6.0 collective-permute-start.58
  268.1 6.0 collective-permute-start.59
  271.3 4.8 collective-permute-start.60
  273.0 9.4 %collective-permute-start.68 = (f32[2,1024]{1,0:T(2,128)S(1)}, f32[2,1024]{1,0:T(2,128)S(1)}, u32[]{:S(2)}, u32[]{:S(2)}) collective-permute-start(f32[2,1024]{1,0:T(2,128)S(1)} %add_add_fusion.1), channel_id=1, source_target_pairs={{0,16},{16,0},{1,17},{17,1},{2,18},{18,2},{3,19},{19,3},{4,20},{20... | collective-permute-start | bytes 24584 | tf_op jit(solution)/shard_map/ppermute | solution.py:618
  281.1 7.9 %collective-permute-start.67 = (f32[2,256]{1,0:T(2,128)S(1)}, f32[2,256]{1,0:T(2,128)S(1)}, u32[]{:S(2)}, u32[]{:S(2)}) collective-permute-start(f32[2,256]{1,0:T(2,128)S(1)} %add_add_fusion.4), channel_id=1, source_target_pairs={{0,16},{16,0},{1,17},{17,1},{2,18},{18,2},{3,19},{19,3},{4,20},{20... | collective-permute-start | bytes 6152 | tf_op jit(solution)/shard_map/ppermute | solution.py:618
  286.5 4.8 collective-permute-start.65
  (154 other events, 1254.6 us)
Sparse Core Ops, SparseCore 0:
  304.3 434.1 all-reduce.4

commit v2 on v1

--- a/solution.py
+++ b/solution.py
@@ -12,30 +12,54 @@
 loss_scale = 65536.0
 low_type = jnp.bfloat16
 full_type = jnp.float32
-vmem_bytes = 40 * 1024 * 1024
+vmem_small, vmem_large = 6 * 1024 * 1024, 18 * 1024 * 1024
+cost_small, cost_large = 0.1, 0.1
+halved_of_128 = 56
 
 even_width = 8
 
 
-def call(body, outs, args, cost_us=2, scratch=()):
+class View:
+    def __init__(self, value, rows, columns):
+        self.value, self.rows, self.columns = value, slice(*rows), slice(*columns)
+
+
+def call(body, outs, args, cost_us=cost_small, scratch=(), copies=0, vmem=vmem_small, after=(), scalars=()):
     whole = pl.BlockSpec(memory_space=pltpu.VMEM)
-    sizes = [len(item) if isinstance(item, tuple) else None for item in args]
-    flat = [one for item in args for one in (item if isinstance(item, tuple) else (item,))]
+    placed = [pl.BlockSpec(memory_space=pltpu.HBM) if copies and len(out.shape) == 3 else whole for out in outs]
+    flat, places = [], {}
+
+    def place(item):
+        value = item.value if isinstance(item, View) else item
+        if id(value) not in places:
+            places[id(value)] = len(flat)
+            flat.append(value)
+        return places[id(value)]
+
+    for item in args:
+        for one in item if isinstance(item, tuple) else (item,):
+            place(one)
 
     def run(*refs):
-        rest = iter(refs)
-        given = [next(rest) if size is None else tuple(next(rest) for _ in range(size)) for size in sizes]
-        body(*given, *rest)
+        def found(item):
+            if isinstance(item, tuple):
+                return tuple(found(one) for one in item)
+            ref = refs[place(item)]
+            return ref.at[item.rows, item.columns] if isinstance(item, View) else ref
+
+        body(*[found(item) for item in args], *refs[len(flat) + len(after) :])
 
     return pl.pallas_call(
         run,
         out_shape=outs,
-        in_specs=[whole] * len(flat),
-        out_specs=[whole] * len(outs),
-        scratch_shapes=[pltpu.VMEM(dims, kind) for dims, kind in scratch],
-        compiler_params=pltpu.CompilerParams(vmem_limit_bytes=vmem_bytes),
+        in_specs=[pl.BlockSpec(memory_space=pltpu.SMEM) if i in scalars else whole for i in range(len(flat))]
+        + [pl.BlockSpec(memory_space=pl.ANY)] * len(after),
+        out_specs=placed,
+        scratch_shapes=[pltpu.VMEM(dims, kind) for dims, kind in scratch]
+        + ([pltpu.SemaphoreType.DMA((copies,))] if copies else []),
+        compiler_params=pltpu.CompilerParams(vmem_limit_bytes=vmem),
         cost_estimate=pl.CostEstimate(flops=int(cost_us * 1e9), bytes_accessed=int(cost_us * 1e6), transcendentals=0),
-    )(*flat)
+    )(*flat, *after)
 
 
 def shaped(*dims, kind=full_type):
@@ -116,12 +140,30 @@
     return value.astype(low_type)
 
 
-def enter_body(images, x_ref, mask_ref, filter_ref, start_ref, out_ref, sums_ref, store):
+def inside(rows, sides, size_ref, unit):
+    images = size_ref.shape[1]
+    place = lax.broadcasted_iota(jnp.int32, (rows, 128), 0)
+    image = place % images
+    bound = jnp.zeros((rows, 128), jnp.int32)
+    for index in range(images):
+        bound = jnp.where(image == index, size_ref[0, index] // unit, bound)
+    pair = place // images
+    over = pair % even_width * sides + pair // even_width % sides
+    down = pair // (even_width * sides)
+    return jnp.where((over < bound) & (down < bound), 1.0, 0.0)
+
+
+def enter_body(images, x_ref, size_ref, filter_ref, start_ref, out_ref, sums_ref, mask_ref, small_ref, pixel_ref, store):
     height, pairs = x_ref.shape[0], x_ref.shape[1]
     depth = x_ref.shape[4]
     line = even_width * images
     blank = jnp.zeros((even_width - pairs, images, depth), low_type)
     store[...] = jnp.zeros_like(store)
+    mask_ref[...] = inside(mask_ref.shape[0], 2, size_ref, 16)
+    small_ref[...] = inside(small_ref.shape[0], 1, size_ref, 32)
+    for index in range(images):
+        bound = (size_ref[0, index] // 32).astype(full_type)
+        pixel_ref[index : index + 1, :] = 1.0 / jnp.full((1, 128), bound * bound)
 
     def step(index, carry):
         rows = pl.ds(pl.multiple_of(index * 4 * line, 4 * line), 4 * line)
@@ -141,6 +183,8 @@
 
     lax.fori_loop(0, height // 2, step, 0)
     finish_rows(store, sums_ref, 2)
+    sums_ref[2:3, :] = wide(column_sum(fold(mask_ref[...])), sums_ref.shape[1])
+    sums_ref[3:4, :] = wide(column_sum(fold(small_ref[...])), sums_ref.shape[1])
 
 
 def split_store(even_ref, moved_ref, place, value, line):
@@ -165,11 +209,13 @@
     )
 
 
-def block_body(images, parts, u_ref, count_ref, scale_ref, shift_ref, mask_ref, filter_ref, even_ref, moved_ref, out_ref, sums_ref, store):
+def block_body(images, parts, u_ref, scale_ref, shift_ref, mask_ref, filter_ref, even_ref, moved_ref, out_ref, sums_ref, count_ref, store):
     depth = filter_ref.shape[1]
     line = even_width * images
     height = even_ref.shape[0] - 2
-    center, inverse = statistics(total(parts), count_ref[0:1, 0:1])
+    sums = total(parts)
+    count_ref[...] = sums[2:4, 0:128]
+    center, inverse = statistics(sums, sums[2:3, 0:1])
     factor = scale_ref[...] * inverse
     shift = shift_ref[...]
     blank_border(even_ref, moved_ref)
@@ -573,7 +619,7 @@
         pre = (u_ref[rows, :] - center) * factor + shift
         for extra_ref in extras:
             pre = pre + extra_ref[rows, :].astype(full_type)
-        out_ref[rows, :] = smooth_slope(pre) * wide(mask_ref[rows, :], depth)
+        out_ref[rows, :] = low(smooth_slope(pre) * wide(mask_ref[rows, :], depth))
         return carry
 
     lax.fori_loop(0, u_ref.shape[0] // rows_step, step, 0)
@@ -583,35 +629,104 @@
     out_ref[...] = times_back(value_ref[...], filter_ref[...])
 
 
-def filter_grad_body(value_ref, grad_ref, out_ref):
-    out_ref[...] = times_rows(value_ref[...], grad_ref[...])
-
-
-def block_filter_body(even_ref, moved_ref, grad_ref, out_ref):
-    height, _, line, depth = even_ref.shape
+def window_start(device, share_size, width):
+    return (device * share_size) // (8 * width) * 8
+
+
+def window_rows(share_size, width):
+    return -(-(share_size + 8 * width) // (16 * width)) * 16
+
+
+def low_rows(rows):
+    part = rows * halved_of_128 // 2048 * 8
+    return [part, part, rows - 2 * part]
+
+
+def copy_windows(source, outs, sems, first_device, first_row, share_size, offsets):
+    owners, _, width = outs[0].shape
+    pieces = len(offsets)
+    core = lax.axis_index("dp") % 2
+    copies = []
+    for piece in range(pieces):
+        for which, chosen in enumerate((1 - core, core)):
+            out = outs[which * pieces + piece]
+            for owner in range(owners):
+                begin = window_start(first_device + 2 * owner + chosen, share_size, width) - first_row + offsets[piece]
+                rows_here = pl.ds(pl.multiple_of(begin, 8), out.shape[1])
+                copies.append(pltpu.make_async_copy(source.at[rows_here], out.at[owner], sems.at[len(copies)]))
+    for copy in copies:
+        copy.start()
+    for copy in copies:
+        copy.wait()
+
+
+def put_filter(store, begin, value, grad):
+    step, across = 256, min(512, grad.shape[1])
+    lanes = store.shape[1]
+    cuts = grad.shape[1] // lanes
+    for row in range(0, value.shape[1], step):
+        for column in range(0, grad.shape[1], across):
+            result = times_rows(value[:, row : row + step], grad[:, column : column + across])
+            for cut in range(across // lanes):
+                place = begin + row * cuts + column // lanes + cut
+                store[pl.ds(place, step, stride=cuts), :] = result[:, cut * lanes : cut * lanes + lanes]
+    return begin + value.shape[1] * cuts
+
+
+def late_filters_body(first_device, first_row, share_size, hidden_ref, picked_ref, low_ref, side_low_ref, *rest):
+    *outs, spill_ref, store, sems = rest
+    filled = put_filter(store, 0, hidden_ref, low_ref)
+    filled = put_filter(store, filled, picked_ref, side_low_ref)
+    store[filled:, :] = jnp.zeros((store.shape[0] - filled, store.shape[1]), full_type)
+    spill_ref[...] = store[: spill_ref.shape[0], :]
+    view = lax.axis_index("view")
+    rows = outs[0].shape[1]
+    copy_windows(store, outs, sems, first_device, first_row, share_size, ((1 - view) * rows, view * rows))
+
+
+def middle_filters_body(share_size, block_ref, low_ref, even_ref, moved_ref, inner_low_ref, spill_ref, *rest):
+    *outs, store, sems = rest
+    filled = put_filter(store, 0, block_ref, low_ref)
+    half = even_ref.shape[0] // 2 - 1
+    for row in range(3):
+        for ref, plane in ((moved_ref, 1), (even_ref, 0), (even_ref, 1)):
+            lhs = jnp.concatenate([ref[2 * index + row, plane] for index in range(half)], axis=0)
+            filled = put_filter(store, filled, lhs, inner_low_ref)
+    store[filled:, :] = spill_ref[...]
+    view = lax.axis_index("view")
+    rows = outs[0].shape[1]
+    copy_windows(store, outs, sems, 0, 0, share_size, ((1 - view) * rows, view * rows, 2 * rows))
+
+
+def block_filter_body(even_ref, moved_ref, inner_low_ref, hidden_ref, outer_low_ref, out_ref):
+    height, _, line, inner = even_ref.shape
     height = height - 2
-    width = grad_ref.shape[1]
-    grad = grad_ref[...].reshape(height, 2, line, width)
+    width = inner_low_ref.shape[1]
+    grad = inner_low_ref[...].reshape(height, 2, line, width)
     grad = jnp.concatenate([grad[:, side].reshape(height * line, width) for side in range(2)], axis=0)
     sources = tap_sources(even_ref, moved_ref)
+    filled = 0
     for row in range(3):
         for over in range(3):
             lhs = jnp.concatenate(
                 [
-                    sources[side][over][0][row : row + height, sources[side][over][1]].reshape(height * line, depth)
+                    sources[side][over][0][row : row + height, sources[side][over][1]].reshape(height * line, inner)
                     for side in range(2)
                 ],
                 axis=0,
             )
-            out_ref[row * 3 + over] = times_rows(lhs, grad)
-
-
-def shrink_filter_body(even_ref, moved_ref, grad_ref, out_ref):
-    half = even_ref.shape[0] // 2 - 1
-    for row in range(3):
-        for over, (ref, plane) in enumerate(((moved_ref, 1), (even_ref, 0), (even_ref, 1))):
-            lhs = jnp.concatenate([ref[2 * index + row, plane] for index in range(half)], axis=0)
-            out_ref[row * 3 + over] = times_rows(lhs, grad_ref[...])
+            filled = put_filter(out_ref, filled, lhs, grad)
+    put_filter(out_ref, filled, hidden_ref, outer_low_ref)
+
+
+def early_filters_body(share_size, start_ref, low_ref, later_ref, *rest):
+    *outs, store, sems = rest
+    filled = put_filter(store, 0, start_ref, low_ref)
+    later = later_ref.shape[0]
+    store[filled : filled + later, :] = later_ref[...]
+    filled += later
+    store[filled:, :] = jnp.zeros((store.shape[0] - filled, store.shape[1]), full_type)
+    copy_windows(store, outs, sems, 0, 0, share_size, (0,))
 
 
 def exchange(value, axis, bits):
@@ -635,12 +750,38 @@
     return parts
 
 
-def pack_flat(parts):
-    return jnp.concatenate([part.reshape(-1) for part in parts])
-
-
-def as_row(value):
-    return value.reshape(1, -1)
+def own_bit(axis, bit):
+    return (lax.axis_index(axis) >> bit) & 1
+
+
+class Windows:
+    def __init__(self, kept, received, bits):
+        self.kept, self.received, self.bits = kept, received, list(bits)
+
+    def step(self, item, *gates):
+        axis, bit = item
+        place = self.bits.index(item)
+        own = own_bit(axis, bit)
+        rows, width = self.kept.shape[1:]
+        before, after = 1 << place, 1 << (len(self.bits) - place - 1)
+
+        def pick(value, index):
+            cut = value.reshape(before, 2, after, rows, width)
+            part = lax.dynamic_slice(cut, (0, index, 0, 0, 0), (before, 1, after, rows, width))
+            return part.reshape(before * after, rows, width)
+
+        self.sent = pick(self.kept, 1 - own) + pick(self.received, 1 - own) + sum(gates, 0.0)
+        self.kept = pick(self.kept, own) + pick(self.received, own)
+        self.received = exchange(self.sent, axis, 1 << bit)
+        self.bits.pop(place)
+
+    def total(self):
+        return (self.kept + self.received)[0]
+
+
+def gate(value):
+    corner = value[(slice(0, 1),) * (value.ndim - 1) + (slice(0, 128),)]
+    return 0.0 * corner.reshape(1, 1, 128)
 
 
 def per_device(
@@ -673,57 +814,73 @@
     middle_a, middle_b, depth_b = reduce_a.shape[1], reduce_b.shape[1], shortcut_b.shape[1]
     line = even_width * images
     rows_big, rows_small = height * 2 * line, pairs * line
-    sizes = resolution[0]
-    places_h = jnp.arange(height).reshape(height, 1, 1, 1, 1)
-    places_w = (2 * jnp.arange(even_width) + jnp.arange(2).reshape(2, 1)).reshape(1, 2, even_width, 1, 1)
-    bound = (sizes // 16).reshape(1, 1, 1, images, 1)
-    mask_big = ((places_h < bound) & (places_w < bound)).astype(full_type)
-    count_big = jnp.sum(mask_big)
-    mask_big = jnp.broadcast_to(mask_big, (height, 2, even_width, images, 128)).reshape(rows_big, 128)
-    places_h = jnp.arange(pairs).reshape(pairs, 1, 1, 1)
-    places_w = jnp.arange(even_width).reshape(1, even_width, 1, 1)
-    bound = (sizes // 32).reshape(1, 1, images, 1)
-    mask_small = ((places_h < bound) & (places_w < bound)).astype(full_type)
-    count_small = jnp.sum(mask_small)
-    mask_small = jnp.broadcast_to(mask_small, (pairs, even_width, images, 128)).reshape(rows_small, 128)
-    pixel = 1.0 / (sizes // 32 * (sizes // 32)).astype(full_type)
-    pixel = jnp.broadcast_to(pixel.reshape(images, 1), (images, 128))
-    counts = jnp.broadcast_to(jnp.stack([count_big, count_small]).reshape(2, 1), (2, 128))
-    counts = sum(share(counts)[1:], share(counts)[0])
     spatial_a9 = spatial_a.reshape(9, middle_a, middle_a)
     spatial_b9 = spatial_b.reshape(9, middle_b, middle_b)
     cells = inputs[0].transpose(1, 2, 0, 3).reshape(height, pairs, 2, images, depth_a)
 
+    vectors = [
+        (scale_reduce_a, shift_reduce_a),
+        (scale_spatial_a, shift_spatial_a),
+        (scale_expand_a, shift_expand_a),
+        (scale_reduce_b, shift_reduce_b),
+        (scale_spatial_b, shift_spatial_b),
+        (scale_expand_b, shift_expand_b),
+        (scale_shortcut, shift_shortcut),
+    ]
+    packed = jnp.stack([jnp.pad(vector, (0, depth_b - vector.size)) for pair in vectors for vector in pair])
+
+    def affine(index):
+        width = vectors[index][0].size
+        return tuple(View(packed, (row, row + 1), (0, width)) for row in (2 * index, 2 * index + 1))
+
     def padded(width):
         return shaped(height + 2, 2, line, width, kind=low_type)
 
     def with_images(body):
         return functools.partial(body, images)
 
-    start, reduced_a, sums = call(
+    start, reduced_a, sums, mask_big, mask_small, pixel = call(
         with_images(enter_body),
-        [shaped(rows_big, depth_a, kind=low_type), shaped(rows_big, middle_a), shaped(2, middle_a)],
-        [cells, mask_big, reduce_a],
+        [
+            shaped(rows_big, depth_a, kind=low_type),
+            shaped(rows_big, middle_a),
+            shaped(4, middle_a),
+            shaped(rows_big, 128),
+            shaped(rows_small, 128),
+            shaped(images, 128),
+        ],
+        [cells, resolution, reduce_a],
         scratch=[((16, middle_a), full_type)],
+        scalars=(1,),
     )
     sums_ra = share(sums)
-    scale_ra, shift_ra = as_row(scale_reduce_a), as_row(shift_reduce_a)
-    even_a, moved_a, mixed_a, sums = call(
+    scale_ra, shift_ra = affine(0)
+    even_a, moved_a, mixed_a, sums, counts = call(
         with_images(block_body),
-        [padded(middle_a), padded(middle_a), shaped(rows_big, middle_a), shaped(2, middle_a)],
-        [sums_ra, reduced_a, counts, scale_ra, shift_ra, mask_big, spatial_a.reshape(9 * middle_a, middle_a)],
+        [padded(middle_a), padded(middle_a), shaped(rows_big, middle_a), shaped(2, middle_a), shaped(2, 128)],
+        [sums_ra, reduced_a, scale_ra, shift_ra, mask_big, spatial_a.reshape(9 * middle_a, middle_a)],
         scratch=[((16, middle_a), full_type)],
     )
+    def slope(parts, value, scale, shift, mask, extras, which, rows_step):
+        return call(
+            functools.partial(slope_body, which=which, rows_step=rows_step),
+            [shaped(*value.shape, kind=low_type)],
+            [parts, value, counts, scale, shift, mask, extras],
+        )[0]
+
+    slope_ra = slope(sums_ra, reduced_a, scale_ra, shift_ra, mask_big, (), 0, 2 * line)
     sums_sa = share(sums)
-    scale_sa, shift_sa = as_row(scale_spatial_a), as_row(shift_spatial_a)
+    scale_sa, shift_sa = affine(1)
     hidden_two_a, expanded_a, sums = call(
         functools.partial(expand_body, which=0, rows_step=4 * line),
         [shaped(rows_big, middle_a, kind=low_type), shaped(rows_big, depth_a), shaped(2, depth_a)],
         [sums_sa, mixed_a, counts, scale_sa, shift_sa, mask_big, expand_a],
         scratch=[((16, depth_a), full_type)],
-    )
+        after=(slope_ra,),
+    )
+    slope_sa = slope(sums_sa, mixed_a, scale_sa, shift_sa, mask_big, (), 0, 2 * line)
     sums_ea = share(sums)
-    scale_ea, shift_ea = as_row(scale_expand_a), as_row(shift_expand_a)
+    scale_ea, shift_ea = affine(2)
     block_a, reduced_b, picked, side_b, sums, side_sums = call(
         with_images(join_body),
         [
@@ -736,32 +893,42 @@
         ],
         [sums_ea, expanded_a, counts, scale_ea, shift_ea, mask_big, start, reduce_b, shortcut_b],
         scratch=[((16, middle_b), full_type), ((16, 128), full_type)],
-    )
+        after=(slope_sa,),
+    )
+    slope_ea = slope(sums_ea, expanded_a, scale_ea, shift_ea, mask_big, (start,), 0, 2 * line)
     shared = share(jnp.concatenate([sums, side_sums], axis=1))
-    sums_rb = tuple(part[:, :middle_b] for part in shared)
-    sums_sc = tuple(part[:, middle_b:] for part in shared)
-    scale_rb, shift_rb = as_row(scale_reduce_b), as_row(shift_reduce_b)
-    scale_sc, shift_sc = as_row(scale_shortcut), as_row(shift_shortcut)
+    sums_rb = tuple(View(part, (0, 2), (0, middle_b)) for part in shared)
+    sums_sc = tuple(View(part, (0, 2), (middle_b, middle_b + depth_b)) for part in shared)
+    scale_rb, shift_rb = affine(3)
+    scale_sc, shift_sc = affine(6)
     even_b, moved_b, mixed_b, sums = call(
         with_images(shrink_body),
         [padded(middle_b), padded(middle_b), shaped(rows_small, middle_b), shaped(2, middle_b)],
         [sums_rb, reduced_b, counts, scale_rb, shift_rb, mask_big, mask_small, spatial_b.reshape(9 * middle_b, middle_b)],
-    )
+        after=(slope_ea,),
+    )
+    block_out = call(
+        with_images(natural_body), [shaped(height, pairs, 2, images, depth_a, kind=low_type)], [block_a]
+    )[0]
+    slope_rb = slope(sums_rb, reduced_b, scale_rb, shift_rb, mask_big, (), 0, 2 * line)
     sums_sb = share(sums)
-    scale_sb, shift_sb = as_row(scale_spatial_b), as_row(shift_spatial_b)
+    scale_sb, shift_sb = affine(4)
     hidden_two_b, expanded_b, sums = call(
         functools.partial(expand_body, which=1, rows_step=line),
         [shaped(rows_small, middle_b, kind=low_type), shaped(rows_small, depth_b), shaped(2, depth_b)],
         [sums_sb, mixed_b, counts, scale_sb, shift_sb, mask_small, expand_b],
         scratch=[((16, depth_b), full_type)],
-    )
+        after=(slope_rb, block_out),
+    )
+    slope_sb = slope(sums_sb, mixed_b, scale_sb, shift_sb, mask_small, (), 1, line)
     sums_eb = share(sums)
-    scale_eb, shift_eb = as_row(scale_expand_b), as_row(shift_expand_b)
+    scale_eb, shift_eb = affine(5)
     block_b, joined_b, pooled = call(
         with_images(leave_body),
         [shaped(pairs, pairs, images, depth_b, kind=low_type), shaped(rows_small, depth_b), shaped(images, depth_b)],
         [sums_eb, sums_sc, expanded_b, side_b, counts, scale_eb, shift_eb, scale_sc, shift_sc, mask_small, pixel],
         scratch=[((8, depth_b), full_type)],
+        after=(slope_sb,),
     )
     partner = exchange(pooled, "view", 1)
     slope_b, plain, unit, side_unit = call(
@@ -774,22 +941,29 @@
         compare_body,
         [shaped(images, 128), shaped(images, depth_b), shaped(3, depth_b)],
         [pooled, partner, pixel, plain, unit, side_unit],
-        cost_us=1,
     )
     grads_eb = share(sums)
 
-    def slope(parts, value, scale, shift, mask, extras, which, rows_step):
-        return call(
-            functools.partial(slope_body, which=which, rows_step=rows_step),
-            [shaped(*value.shape)],
-            [parts, value, counts, scale, shift, mask, extras],
-        )[0]
-
-    slope_sb = slope(sums_sb, mixed_b, scale_sb, shift_sb, mask_small, (), 1, line)
-    slope_rb = slope(sums_rb, reduced_b, scale_rb, shift_rb, mask_big, (), 0, 2 * line)
-    slope_ea = slope(sums_ea, expanded_a, scale_ea, shift_ea, mask_big, (start,), 0, 2 * line)
-    slope_sa = slope(sums_sa, mixed_a, scale_sa, shift_sa, mask_big, (), 0, 2 * line)
-    slope_ra = slope(sums_ra, reduced_a, scale_ra, shift_ra, mask_big, (), 0, 2 * line)
+    size = lax.axis_size("dp")
+    half = size // 2
+    bits = [("dp", bit) for bit in range(size.bit_length() - 2, 0, -1)]
+    low_first = sorted(bits, key=lambda item: item[1])
+    high_first = low_first[1:] + low_first[:1]
+    lanes = 128
+    first_rows = (depth_a + 9 * middle_b) * middle_b // lanes
+    norm_rows_b = (4 * middle_b + 4 * depth_b) // lanes
+    total_b = first_rows + (middle_b + depth_a) * depth_b // lanes + norm_rows_b
+    share_b = total_b * lanes // (2 * size)
+    window_b = window_rows(share_b, lanes)
+    end_low = window_start(size - 1, share_b, lanes) + window_b
+    end_high = window_start(2 * size - 1, share_b, lanes) + window_b
+
+    def windows(count, pieces):
+        return [pltpu.HBM((count, piece, lanes), full_type) for piece in pieces] * 2
+
+    def pairs_of(outs):
+        count = len(outs) // 2
+        return [(kept, exchange(send, "dp", 1)) for send, kept in zip(outs[:count], outs[count:])]
 
     low_eb, low_sc, grad_sb, sums = call(
         with_images(leave_back_body),
@@ -819,14 +993,28 @@
         scratch=[((8, 128), full_type)],
     )
     grads_sb = share(sums)
+    *outs, spill = call(
+        functools.partial(late_filters_body, size, first_rows, share_b),
+        windows(half, [window_b // 2] * 2) + [shaped(end_low - first_rows, lanes)],
+        [hidden_two_b, picked, low_eb, low_sc],
+        scratch=[((end_high - first_rows, lanes), full_type)],
+        copies=4 * half,
+        vmem=vmem_large,
+        cost_us=cost_large,
+        after=(grads_sb[0],),
+    )
+    grad_picked = call(times_back_body, [shaped(rows_small, depth_a)], [low_sc, shortcut_b])[0]
+    far, near = pairs_of(outs)
+    far_sum = far[0] + far[1]
+    high = Windows(near[0] + near[1], exchange(far_sum, "view", 1), bits)
     low_sb, grad_rb, sums = call(
         with_images(shrink_back_body),
         [shaped(rows_small, middle_b, kind=low_type), shaped(rows_big, middle_b), shaped(2, middle_b)],
         [sums_sb, grads_sb, grad_sb, mixed_b, counts, scale_sb, mask_small, spatial_b9, sums_rb, reduced_b, slope_rb],
         scratch=[((16, middle_b), full_type)],
+        after=(far_sum, grad_picked),
     )
     grads_rb = share(sums)
-    grad_picked = call(times_back_body, [shaped(rows_small, depth_a)], [low_sc, shortcut_b])[0]
     low_rb, joined_grad, sums = call(
         with_images(join_back_body),
         [shaped(rows_big, middle_b, kind=low_type), shaped(rows_big, depth_a), shaped(2, depth_a)],
@@ -841,6 +1029,20 @@
         scratch=[((16, middle_a), full_type)],
     )
     grads_sa = share(sums)
+    outs = call(
+        functools.partial(middle_filters_body, share_b),
+        windows(half, low_rows(window_b)),
+        [block_a, low_rb, even_b, moved_b, low_sb, spill],
+        scratch=[((end_low, lanes), full_type)],
+        copies=6 * half,
+        vmem=vmem_large,
+        cost_us=cost_large,
+        after=(grads_ea[0],),
+    )
+    far, near, whole = pairs_of(outs)
+    far_sum = far[0] + far[1]
+    low_half = Windows(near[0] + near[1], exchange(far_sum, "view", 1), bits)
+    low_whole = Windows(*whole, bits)
     low_sa, grad_ra, sums = call(
         with_images(block_back_body),
         [shaped(rows_big, middle_a, kind=low_type), shaped(rows_big, middle_a), shaped(2, middle_a)],
@@ -850,47 +1052,99 @@
             ((height + 2, 2, line, middle_a), low_type),
             ((16, middle_a), full_type),
         ],
+        after=(far_sum, high.received),
     )
     grads_ra = share(sums)
+    ready, x_bit, z_bits = [], low_first[:1], low_first[1:]
+    if bits:
+        x_bit = x_bit[0]
+        high.step(x_bit, gate(grads_ra[0]))
+        low_whole.step(z_bits[0] if z_bits else x_bit, *(gate(part) for part in grads_ra[1:]))
+        ready = [high.sent, low_whole.sent]
     low_ra, input_grad = call(
         with_images(exit_body),
         [shaped(rows_big, middle_a, kind=low_type), shaped(height, pairs, 2, images, depth_a, kind=low_type)],
         [sums_ra, grads_ra, grad_ra, reduced_a, counts, scale_ra, mask_big, reduce_a, joined_grad],
-    )
-
-    def filter_grad(value, grad):
-        return call(filter_grad_body, [shaped(value.shape[1], grad.shape[1])], [value, grad])[0]
-
-    grad_expand_b = filter_grad(hidden_two_b, low_eb)
-    grad_shortcut = filter_grad(picked, low_sc)
-    grad_spatial_b = call(shrink_filter_body, [shaped(9, middle_b, middle_b)], [even_b, moved_b, low_sb])[0]
-    grad_reduce_b = filter_grad(block_a, low_rb)
-    grad_expand_a = filter_grad(hidden_two_a, low_ea)
-    grad_spatial_a = call(block_filter_body, [shaped(9, middle_a, middle_a)], [even_a, moved_a, low_sa])[0]
-    grad_reduce_a = filter_grad(start, low_ra)
-    block_out = call(
-        with_images(natural_body), [shaped(height, pairs, 2, images, depth_a, kind=low_type)], [block_a]
+        after=ready,
+    )
+    norm_rows_a = (4 * middle_a + 2 * depth_a) // lanes
+    total_a = (depth_a * 2 + 9 * middle_a) * middle_a // lanes + norm_rows_a
+    share_a = total_a * lanes // (2 * size)
+    window_a = window_rows(share_a, lanes)
+    end_a = window_start(2 * size - 1, share_a, lanes) + window_a
+    later = call(
+        block_filter_body,
+        [shaped((total_a - norm_rows_a) - depth_a * middle_a // lanes, lanes)],
+        [even_a, moved_a, low_sa, hidden_two_a, low_ea],
+        cost_us=cost_large,
     )[0]
-
-    def both_views(parts):
-        value = sum(parts[1:], parts[0])
-        return value + exchange(value, "view", 1)
-
-    def once(value):
-        first = (lax.axis_index("dp") == 0) & (lax.axis_index("view") == 0)
-        return jnp.where(first, value, 0.0)
-
-    all_eb = both_views(grads_eb)
-    late_flat = pack_flat(
-        [grad_reduce_b, grad_spatial_b, grad_expand_b, grad_shortcut]
-        + [once(v) for v in (both_views(grads_rb), both_views(grads_sb), all_eb[:2], all_eb[0], all_eb[2])]
-    )
-    early_flat = pack_flat(
-        [grad_reduce_a, grad_spatial_a, grad_expand_a]
-        + [once(v) for v in (both_views(grads_ra), both_views(grads_sa), both_views(grads_ea))]
-    )
-    late_done = lax.psum_scatter(late_flat, ("view", "dp"), scatter_dimension=0, tiled=True)
-    early_done = lax.psum_scatter(early_flat, ("view", "dp"), scatter_dimension=0, tiled=True)
+    outs = call(
+        functools.partial(early_filters_body, share_a),
+        windows(size, [window_a]),
+        [start, low_ra, later],
+        scratch=[((end_a, lanes), full_type)],
+        copies=2 * size,
+        vmem=2 * vmem_small,
+        cost_us=cost_large,
+        after=(low_half.received,),
+    )
+    early = Windows(*pairs_of(outs)[0], [("view", 0)] + bits)
+    early.step(("view", 0))
+    if z_bits:
+        high.step(z_bits[0])
+        low_whole.step(x_bit)
+        low_half.step(x_bit, gate(low_whole.sent))
+        for item in z_bits[1:]:
+            high.step(item)
+            low_whole.step(item)
+        early.step(x_bit, gate(low_half.sent))
+        low_half.step(z_bits[0], gate(high.sent))
+        early.step(z_bits[0], gate(low_half.sent))
+        for item in z_bits[1:]:
+            low_half.step(item)
+            early.step(item)
+    elif bits:
+        low_half.step(x_bit)
+        early.step(x_bit)
+    early_window = early.total()
+    view = lax.axis_index("view")
+    all_grads = [sum(parts[1:], parts[0]) for parts in (grads_rb, grads_sb, grads_eb, grads_ra, grads_sa, grads_ea)]
+    norms = jnp.concatenate([value.reshape(-1, lanes) for value in all_grads], axis=0)
+    norms = norms + exchange(norms + gate(early.received)[0], "view", 1)
+    high_half, low_half, low_rest = high.total(), low_half.total(), low_whole.total()
+    short = low_half.shape[0] + low_rest.shape[0] - high_half.shape[0]
+    swapped = exchange(
+        jnp.where(
+            view == 0, jnp.pad(high_half, ((0, short), (0, 0))), jnp.concatenate([low_half, low_rest], axis=0)
+        ),
+        "view",
+        1,
+    )
+    late_window = jnp.where(
+        view == 0,
+        jnp.concatenate([low_half, swapped[: low_half.shape[0]], low_rest + swapped[low_half.shape[0] :]], axis=0),
+        jnp.concatenate([swapped[: high_half.shape[0]], high_half], axis=0),
+    )
+    cut = []
+    for value in all_grads:
+        rows = value.size // lanes
+        cut.append(norms[:rows].reshape(value.shape))
+        norms = norms[rows:]
+    norms_b = [cut[0], cut[1], cut[2][:2], cut[2][0], cut[2][2]]
+    norms_a = cut[3:]
+    device = lax.axis_index("view") * size + lax.axis_index("dp")
+
+    def finish(window, norms, rows, norm_rows, share_size):
+        width = window.shape[1]
+        place = rows - norm_rows - window_start(2 * size - 1, share_size, width)
+        values = jnp.concatenate([value.reshape(-1) for value in norms]).reshape(norm_rows, width)
+        values = jnp.where(device == 2 * size - 1, values, 0.0)
+        window = window + jnp.pad(values, ((place, window.shape[0] - place - norm_rows), (0, 0)))
+        begin = device * share_size - window_start(device, share_size, width) * width
+        return lax.dynamic_slice(window.reshape(-1), (begin,), (share_size,))
+
+    late_done = finish(late_window, norms_b, total_b, norm_rows_b, share_b)
+    early_done = finish(early_window, norms_a, total_a, norm_rows_a, share_a)
 
     def natural(value):
         return value.reshape(height, height, images, depth_a).transpose(2, 0, 1, 3)[None]

time: 750 us -> 364 us (0.49)
  waiting for transfers between devices: 480 us -> 132 us
  local copies, waits for them, and re-layouts: 100 us -> 24.7 us
  other arithmetic: 7.2 us -> 31.2 us
  starting transfers between devices: 77.8 us -> 92.4 us
  between operations: 15.5 us -> 1.99 us
  Pallas kernels: 68.4 us -> 80.6 us
    unnamed x2 -> x0, waiting for transfers between devices: 431 us -> none
    ppermute x72 -> x84, waiting for transfers between devices: 49 us -> 132 us  [exchange(): lax.ppermute(value, axis, [(i, i ^ bits) for i in range(lax.axis_size(axi...]
    unnamed x286 -> x169, local copies, waits for them, and re-layouts: 97.7 us -> 20.4 us
    add x9 -> x40, other arithmetic: 1.46 us -> 30.7 us  [the longest x9 9.73 us: step(): self.kept = pick(self.kept, own) + pick(self.received, own)]
    ppermute x72 -> x84, starting transfers between devices: 77.8 us -> 92.4 us  [exchange(): lax.ppermute(value, axis, [(i, i ^ bits) for i in range(lax.axis_size(axi...]
    pallas_call x29 -> x26, Pallas kernels: 68.4 us -> 80.6 us  [call(): pl.pallas_call(run, out_shape=outs, in_specs=[pl.BlockSpec(memory_space=p...]
  transfers between devices with their start and end apart: 73 -> 84, of which waited for: 31 -> 51; matrix products, arithmetic and copies ran while one was open for 6% -> 8% of each run, Pallas kernels for 5% -> 12%
where the time goes in v2:
time: 364 us; the launch traced here: 363 us
  waiting for transfers between devices  132 us (36%)
  starting transfers between devices  92.4 us (25%)
  Pallas kernels  80.6 us (22%)
  other arithmetic  31.2 us (9%)
  local copies, waits for them, and re-layouts  24.7 us (7%)
    ppermute x84, waiting for transfers between devices, exchange(): lax.ppermute(value, axis, [(i, i ^ bits) for i in range(lax.axis_size(axi...  132 us
    ppermute x84, starting transfers between devices, exchange(): lax.ppermute(value, axis, [(i, i ^ bits) for i in range(lax.axis_size(axi...  92.4 us
    pallas_call x26, Pallas kernels, call(): pl.pallas_call(run, out_shape=outs, in_specs=[pl.BlockSpec(memory_space=p...  80.6 us
    unnamed x169, local copies, waits for them, and re-layouts  20.4 us
    add x9, other arithmetic, step(): self.kept = pick(self.kept, own) + pick(self.received, own)  9.73 us
    add x16, other arithmetic, step(): pick(self.kept, 1 - own) + pick(self.received, 1 - own) + sum(gates, 0.0)  8.86 us
  transfers between devices with their start and end apart: 84, of which 51 were waited for; matrix products, arithmetic and copies ran while one was open for 8% of the time, Pallas kernels for 12%

profile of v2, /device:TPU:0, one launch (start us, length us, event | category | flops | bytes accessed | tf_op | source)
XLA Modules:
  0.0 363.1 jit_solution(6072755445696034)
XLA Ops:
  3.8 2.8 shard_map.262
  8.0 2.6 collective-permute-start.1
  11.9 3.8 %collective-permute-start.4 = (f32[4,256]{1,0:T(4,128)S(1)}, f32[4,256]{1,0:T(4,128)S(1)}, u32[]{:S(2)}, u32[]{:S(2)}) collective-permute-start(f32[4,256]{1,0:T(4,128)S(1)} %add.531.refs_0_.refs_14_), channel_id=1, source_target_pairs={{0,13},{1,12},{2,15},{3,14},{4,9},{5,8},{6,11},{7,10},{8,5},{9,4},... | collective-permute-start | bytes 12296 | tf_op jit(solution)/shard_map/ppermute | solution.py:733
  21.0 2.5 shard_map.263
  31.1 2.2 collective-permute-start.7
  35.1 2.6 shard_map.265
  49.2 7.2 %shard_map.267 = (bf16[896,1024]{1,0:T(8,128)(2,1)S(1)}, f32[896,512]{1,0:T(8,128)S(1)}, bf16[224,1024]{1,0:T(8,128)(2,1)S(1)}, f32[224,2048]{1,0:T(8,128)S(1)},...) custom-call(f32[2,1024]{1,0:T(2,128)S(1)} %add.535.refs_0_.refs_15_, ...), custom_call_target="tpu_custom_call" | custom-call | flops 100000000 | bytes 100000 | tf_op jit(solution)/shard_map/pallas_call | solution.py:52
  65.1 4.7 %shard_map.268.refs_10_.refs_20_ = bf16[896,1024]{1,0:T(8,128)(2,1)S(1)} custom-call(f32[2,1024]{1,0:T(2,128)S(1)} %add.535.refs_0_.refs_15_, f32[2,1024]{1,0:T(2,128)S(1)} %collective-permute-done.12.refs_1_.refs_16_, f32[2,1024]{1,0:T(2,128)S(1)} %collective-permute-done.13.refs_2_.refs_17_, f32[2,1024]{1,0:T(2,128)S(1)} %collective-permute-done.14.refs_3_.refs_18_, ...), custom_call_target="tpu_custom_call" | custom-call | flops 100000000 | bytes 100000 | tf_op jit(solution)/shard_map/pallas_call | solution.py:52
  69.9 3.7 %shard_map.269 = (bf16[16,2,32,512]{3,2,1,0:T(8,128)(2,1)S(1)}, bf16[16,2,32,512]{3,2,1,0:T(8,128)(2,1)S(1)}, f32[224,512]{1,0:T(8,128)S(1)}, f32[2,512]{1,0:T(2,128)S(1)}) custom-call(f32[2,2560]{1,0:T(2,128)S(1)} %add.537.refs_0_.refs_4_.refs_14_, f32[2,2560]{1,0:T(2,128)S(1)} %collective-permute-done.17.refs_1_.refs_5_.refs_15_, ...), custom_call_target="tpu_custom_call" | custom-call | flops 100000000 | bytes 100000 | tf_op jit(solution)/shard_map/pallas_call | solution.py:52
  79.6 2.2 collective-permute-start.22
  81.8 2.3 shard_map.270.refs_9_.refs_19_
  85.6 3.4 shard_map.272
  99.6 3.6 shard_map.274
  104.6 2.6 shard_map.275
  110.7 2.1 collective-permute-done.32
  119.6 2.4 shard_map.277
  126.3 9.7 %shard_map.278 = (f32[8,744,128]{2,1,0:T(8,128)}, f32[8,744,128]{2,1,0:T(8,128)}, f32[8,744,128]{2,1,0:T(8,128)}, f32[8,744,128]{2,1,0:T(8,128)}, f32[1072,128]{1,0:T(8,128)S(1)}) custom-call(bf16[224,512]{1,0:T(8,128)(2,1)S(1)} %get-tuple-element.106.refs_0_, bf16[224,1024]{1,0:T(8,128)(2,1)S(1)} %get-tuple-element.107.refs_1_, ...), custom_call_target="tpu_custom_call" | custom-call | flops 100000000 | bytes 100000 | tf_op jit(solution)/shard_map/pallas_call | solution.py:52
  136.2 5.6 %collective-permute-done.41 = f32[8,744,128]{2,1,0:T(8,128)S(1)} collective-permute-done((f32[8,744,128]{2,1,0:T(8,128)}, f32[8,744,128]{2,1,0:T(8,128)S(1)}, u32[]{:S(2)}, u32[]{:S(2)}) %collective-permute-start.41) | collective-permute-done | bytes 3047456 | tf_op jit(solution)/shard_map/ppermute | solution.py:733
  141.8 3.8 %add.546.refs_20_ = f32[8,744,128]{2,1,0:T(8,128)} add(f32[8,744,128]{2,1,0:T(8,128)} %get-tuple-element.110, f32[8,744,128]{2,1,0:T(8,128)S(1)} %collective-permute-done.41) | non-fusion elementwise | flops 761856 | bytes 9142272 | tf_op jit(solution)/shard_map/add | solution.py:1008
  148.9 2.2 collective-permute-start.38
  159.0 2.1 collective-permute-start.46
  165.0 4.0 %shard_map.281 = (bf16[896,512]{1,0:T(8,128)(2,1)S(1)}, f32[896,1024]{1,0:T(8,128)S(1)}, f32[2,1024]{1,0:T(2,128)S(1)}) custom-call(f32[2,2560]{1,0:T(2,128)S(1)} %add.537.refs_0_.refs_4_.refs_14_, f32[2,2560]{1,0:T(2,128)S(1)} %collective-permute-done.17.refs_1_.refs_5_.refs_15_, f32[2,2560]{1,0:T(2,128)S(1)} %collective-permute-done.18.refs_2_.refs_6_.refs_16_, ...), custom_call_target="tpu_custom_call" | custom-call | flops 100000000 | bytes 100000 | tf_op jit(solution)/shard_map/pallas_call | solution.py:52
  174.0 7.4 %shard_map.283 = (f32[8,320,128]{2,1,0:T(8,128)}, f32[8,320,128]{2,1,0:T(8,128)}, f32[8,848,128]{2,1,0:T(8,128)}, f32[8,320,128]{2,1,0:T(8,128)}, f32[8,320,128]{2,1,0:T(8,128)}, /*index=5*/f32[8,848,128]{2,1,0:T(8,128)}) custom-call(bf16[896,1024]{1,0:T(8,128)(2,1)S(1)} %get-tuple-element.89.refs_0_, bf16[896,512]{1,0:T(8,128)(2,1)S(1)} %get-tuple-element.118.refs_1_, ...), custom_call_target="tpu_custom_call" | custom-call | flops 100000000 | bytes 100000 | tf_op jit(solution)/shard_map/pallas_call | solution.py:52
  184.3 2.9 collective-permute-done.51.refs_7_
  187.3 3.9 %collective-permute-done.50.refs_6_ = f32[2,1024]{1,0:T(2,128)S(1)} collective-permute-done((f32[2,1024]{1,0:T(2,128)S(1)}, f32[2,1024]{1,0:T(2,128)S(1)}, u32[]{:S(2)}, u32[]{:S(2)}) %collective-permute-start.50) | collective-permute-done | bytes 8224 | tf_op jit(solution)/shard_map/ppermute | solution.py:733
  191.2 3.1 collective-permute-done.49.refs_5_
  194.3 2.6 shard_map.282
  203.7 2.3 collective-permute-start.56
  206.0 2.5 collective-permute-done.56.refs_7_
  208.6 2.2 collective-permute-start.54
  210.8 3.1 add.553.refs_20_
  214.0 2.1 shard_map.284
  221.4 3.1 add.556
  229.2 2.9 fusion.1.refs_15_
  244.2 3.7 %shard_map.285 = (bf16[896,256]{1,0:T(8,128)(2,1)S(1)}, bf16[14,7,2,4,1024]{4,3,2,1,0:T(4,128)(2,1)}) custom-call(f32[4,256]{1,0:T(4,128)S(1)} %add.531.refs_0_.refs_14_, f32[4,256]{1,0:T(4,128)S(1)} %collective-permute-done.2.refs_1_.refs_15_, f32[4,256]{1,0:T(4,128)S(1)} %collective-permute-done.3.refs_2_.refs_16_, ...), custom_call_target="tpu_custom_call" | custom-call | flops 100000000 | bytes 100000 | tf_op jit(solution)/shard_map/pallas_call | solution.py:52
  247.9 7.8 %collective-permute-done.66.refs_3_ = f32[8,320,128]{2,1,0:T(8,128)} collective-permute-done((f32[8,320,128]{2,1,0:T(8,128)}, f32[8,320,128]{2,1,0:T(8,128)}, u32[]{:S(2)}, u32[]{:S(2)}) %collective-permute-start.66) | collective-permute-done | bytes 1310752 | tf_op jit(solution)/shard_map/ppermute | solution.py:733
  255.8 3.2 shard_map.287
  264.3 3.9 %collective-permute-done.73 = f32[4,744,128]{2,1,0:T(8,128)} collective-permute-done((f32[4,744,128]{2,1,0:T(8,128)}, f32[4,744,128]{2,1,0:T(8,128)}, u32[]{:S(2)}, u32[]{:S(2)}) %collective-permute-start.73) | collective-permute-done | bytes 1523744 | tf_op jit(solution)/shard_map/ppermute | solution.py:733
  272.8 4.4 %collective-permute-done.70 = f32[4,848,128]{2,1,0:T(8,128)} collective-permute-done((f32[4,848,128]{2,1,0:T(8,128)}, f32[4,848,128]{2,1,0:T(8,128)}, u32[]{:S(2)}, u32[]{:S(2)}) %collective-permute-start.70) | collective-permute-done | bytes 1736736 | tf_op jit(solution)/shard_map/ppermute | solution.py:733
  281.9 10.3 %collective-permute-done.74 = f32[2,744,128]{2,1,0:T(8,128)S(1)} collective-permute-done((f32[2,744,128]{2,1,0:T(8,128)S(1)}, f32[2,744,128]{2,1,0:T(8,128)S(1)}, u32[]{:S(2)}, u32[]{:S(2)}) %collective-permute-start.74) | collective-permute-done | bytes 761888 | tf_op jit(solution)/shard_map/ppermute | solution.py:733
  298.0 13.1 %collective-permute-done.80 = f32[1,744,128]{2,1,0:T(8,128)S(1)} collective-permute-done((f32[1,744,128]{2,1,0:T(8,128)S(1)}, f32[1,744,128]{2,1,0:T(8,128)S(1)}, u32[]{:S(2)}, u32[]{:S(2)}) %collective-permute-start.80) | collective-permute-done | bytes 380960 | tf_op jit(solution)/shard_map/ppermute | solution.py:733
  315.2 11.4 %collective-permute-done.78 = f32[2,320,128]{2,1,0:T(8,128)S(1)} collective-permute-done((f32[2,320,128]{2,1,0:T(8,128)S(1)}, f32[2,320,128]{2,1,0:T(8,128)S(1)}, u32[]{:S(2)}, u32[]{:S(2)}) %collective-permute-start.78) | collective-permute-done | bytes 327712 | tf_op jit(solution)/shard_map/ppermute | solution.py:733
  328.5 12.2 %collective-permute-done.79 = f32[1,320,128]{2,1,0:T(8,128)S(1)} collective-permute-done((f32[1,320,128]{2,1,0:T(8,128)S(1)}, f32[1,320,128]{2,1,0:T(8,128)S(1)}, u32[]{:S(2)}, u32[]{:S(2)}) %collective-permute-start.79) | collective-permute-done | bytes 163872 | tf_op jit(solution)/shard_map/ppermute | solution.py:733
  341.2 2.2 collective-permute-start.75
  344.8 3.6 collective-permute-done.75
  349.1 2.3 collective-permute-start.76
  351.4 5.4 %collective-permute-done.76 = f32[1,288,128]{2,1,0:T(8,128)S(1)} collective-permute-done((f32[1,288,128]{2,1,0:T(8,128)S(1)}, f32[1,288,128]{2,1,0:T(8,128)S(1)}, u32[]{:S(2)}, u32[]{:S(2)}) %collective-permute-start.76) | collective-permute-done | bytes 147488 | tf_op jit(solution)/shard_map/ppermute | solution.py:733
  358.2 2.7 collective-permute-done.77
  (416 shorter events, 159.0 us)
Async XLA Ops:
  11.9 6.1 %collective-permute-start.4 = (f32[4,256]{1,0:T(4,128)S(1)}, f32[4,256]{1,0:T(4,128)S(1)}, u32[]{:S(2)}, u32[]{:S(2)}) collective-permute-start(f32[4,256]{1,0:T(4,128)S(1)} %add.531.refs_0_.refs_14_), channel_id=1, source_target_pairs={{0,13},{1,12},{2,15},{3,14},{4,9},{5,8},{6,11},{7,10},{8,5},{9,4},... | collective-permute-start | bytes 12296 | tf_op jit(solution)/shard_map/ppermute | solution.py:733
  29.2 5.4 %collective-permute-start.9 = (f32[2,256]{1,0:T(2,128)S(1)}, f32[2,256]{1,0:T(2,128)S(1)}, u32[]{:S(2)}, u32[]{:S(2)}) collective-permute-start(f32[2,256]{1,0:T(2,128)S(1)} %add.533.refs_0_.refs_14_), channel_id=1, source_target_pairs={{0,13},{1,12},{2,15},{3,14},{4,9},{5,8},{6,11},{7,10},{8,5},{9,4},... | collective-permute-start | bytes 6152 | tf_op jit(solution)/shard_map/ppermute | solution.py:733
  43.6 5.2 %collective-permute-start.14 = (f32[2,1024]{1,0:T(2,128)S(1)}, f32[2,1024]{1,0:T(2,128)S(1)}, u32[]{:S(2)}, u32[]{:S(2)}) collective-permute-start(f32[2,1024]{1,0:T(2,128)S(1)} %add.535.refs_0_.refs_15_), channel_id=1, source_target_pairs={{0,13},{1,12},{2,15},{3,14},{4,9},{5,8},{6,11},{7,10},{8,5},{9,4},... | collective-permute-start | bytes 24584 | tf_op jit(solution)/shard_map/ppermute | solution.py:733
  61.0 8.8 %collective-permute-start.19 = (f32[2,2560]{1,0:T(2,128)S(1)}, f32[2,2560]{1,0:T(2,128)S(1)}, u32[]{:S(2)}, u32[]{:S(2)}) collective-permute-start(f32[2,2560]{1,0:T(2,128)S(1)} %add.537.refs_0_.refs_4_.refs_14_), channel_id=1, source_target_pairs={{0,13},{1,12},{2,15},{3,14},{4,9},{5,8},{6,11},{7,10},{8,5},{9,4},... | collective-permute-start | bytes 61448 | tf_op jit(solution)/shard_map/ppermute | solution.py:733
  63.0 6.9 %collective-permute-start.18 = (f32[2,2560]{1,0:T(2,128)S(1)}, f32[2,2560]{1,0:T(2,128)S(1)}, u32[]{:S(2)}, u32[]{:S(2)}) collective-permute-start(f32[2,2560]{1,0:T(2,128)S(1)} %add.537.refs_0_.refs_4_.refs_14_), channel_id=1, source_target_pairs={{0,9},{1,8},{2,11},{3,10},{4,13},{5,12},{6,15},{7,14},{8,1},{9,0},... | collective-permute-start | bytes 61448 | tf_op jit(solution)/shard_map/ppermute | solution.py:733
  63.8 6.1 %collective-permute-start.17 = (f32[2,2560]{1,0:T(2,128)S(1)}, f32[2,2560]{1,0:T(2,128)S(1)}, u32[]{:S(2)}, u32[]{:S(2)}) collective-permute-start(f32[2,2560]{1,0:T(2,128)S(1)} %add.537.refs_0_.refs_4_.refs_14_), channel_id=1, source_target_pairs={{0,5},{1,4},{2,7},{3,6},{4,1},{5,0},{6,3},{7,2},{8,13},{9,12},{10,... | collective-permute-start | bytes 61448 | tf_op jit(solution)/shard_map/ppermute | solution.py:733
  77.9 6.2 %collective-permute-start.24 = (f32[2,512]{1,0:T(2,128)S(1)}, f32[2,512]{1,0:T(2,128)S(1)}, u32[]{:S(2)}, u32[]{:S(2)}) collective-permute-start(f32[2,512]{1,0:T(2,128)S(1)} %add.539.refs_0_.refs_20_), channel_id=1, source_target_pairs={{0,13},{1,12},{2,15},{3,14},{4,9},{5,8},{6,11},{7,10},{8,5},{9,4},... | collective-permute-start | bytes 12296 | tf_op jit(solution)/shard_map/ppermute | solution.py:733
  79.6 4.5 %collective-permute-start.23 = (f32[2,512]{1,0:T(2,128)S(1)}, f32[2,512]{1,0:T(2,128)S(1)}, u32[]{:S(2)}, u32[]{:S(2)}) collective-permute-start(f32[2,512]{1,0:T(2,128)S(1)} %add.539.refs_0_.refs_20_), channel_id=1, source_target_pairs={{0,9},{1,8},{2,11},{3,10},{4,13},{5,12},{6,15},{7,14},{8,1},{9,0},... | collective-permute-start | bytes 12296 | tf_op jit(solution)/shard_map/ppermute | solution.py:733
  79.6 4.5 %collective-permute-start.22 = (f32[2,512]{1,0:T(2,128)S(1)}, f32[2,512]{1,0:T(2,128)S(1)}, u32[]{:S(2)}, u32[]{:S(2)}) collective-permute-start(f32[2,512]{1,0:T(2,128)S(1)} %add.539.refs_0_.refs_20_), channel_id=1, source_target_pairs={{0,5},{1,4},{2,7},{3,6},{4,1},{5,0},{6,3},{7,2},{8,13},{9,12},{10,... | collective-permute-start | bytes 12296 | tf_op jit(solution)/shard_map/ppermute | solution.py:733
  93.5 5.0 %collective-permute-start.29 = (f32[2,2048]{1,0:T(2,128)S(1)}, f32[2,2048]{1,0:T(2,128)S(1)}, u32[]{:S(2)}, u32[]{:S(2)}) collective-permute-start(f32[2,2048]{1,0:T(2,128)S(1)} %add.541.refs_0_), channel_id=1, source_target_pairs={{0,13},{1,12},{2,15},{3,14},{4,9},{5,8},{6,11},{7,10},{8,5},{9,4},... | collective-permute-start | bytes 49160 | tf_op jit(solution)/shard_map/ppermute | solution.py:733
  95.5 4.1 %collective-permute-start.28 = (f32[2,2048]{1,0:T(2,128)S(1)}, f32[2,2048]{1,0:T(2,128)S(1)}, u32[]{:S(2)}, u32[]{:S(2)}) collective-permute-start(f32[2,2048]{1,0:T(2,128)S(1)} %add.541.refs_0_), channel_id=1, source_target_pairs={{0,9},{1,8},{2,11},{3,10},{4,13},{5,12},{6,15},{7,14},{8,1},{9,0},... | collective-permute-start | bytes 49160 | tf_op jit(solution)/shard_map/ppermute | solution.py:733
  103.1 4.1 %collective-permute-start.30 = (f32[4,2048]{1,0:T(4,128)S(1)}, f32[4,2048]{1,0:T(4,128)S(1)}, u32[]{:S(2)}, u32[]{:S(2)}) collective-permute-start(f32[4,2048]{1,0:T(4,128)S(1)} %get-tuple-element.94.refs_0_), channel_id=1, source_target_pairs={{0,16},{16,0},{1,17},{17,1},{2,18},{18,2},{3,19},{19,3},{4,20},{20... | collective-permute-start | bytes 98312 | tf_op jit(solution)/shard_map/ppermute | solution.py:733
  112.8 5.2 %collective-permute-start.35 = (f32[3,2048]{1,0:T(4,128)S(1)}, f32[3,2048]{1,0:T(4,128)S(1)}, u32[]{:S(2)}, u32[]{:S(2)}) collective-permute-start(f32[3,2048]{1,0:T(4,128)S(1)} %add.543.refs_8_), channel_id=1, source_target_pairs={{0,13},{1,12},{2,15},{3,14},{4,9},{5,8},{6,11},{7,10},{8,5},{9,4},... | collective-permute-start | bytes 73736 | tf_op jit(solution)/shard_map/ppermute | solution.py:733
  114.5 5.1 %collective-permute-start.34 = (f32[3,2048]{1,0:T(4,128)S(1)}, f32[3,2048]{1,0:T(4,128)S(1)}, u32[]{:S(2)}, u32[]{:S(2)}) collective-permute-start(f32[3,2048]{1,0:T(4,128)S(1)} %add.543.refs_8_), channel_id=1, source_target_pairs={{0,9},{1,8},{2,11},{3,10},{4,13},{5,12},{6,15},{7,14},{8,1},{9,0},... | collective-permute-start | bytes 73736 | tf_op jit(solution)/shard_map/ppermute | solution.py:733
  115.3 4.3 %collective-permute-start.33 = (f32[3,2048]{1,0:T(4,128)S(1)}, f32[3,2048]{1,0:T(4,128)S(1)}, u32[]{:S(2)}, u32[]{:S(2)}) collective-permute-start(f32[3,2048]{1,0:T(4,128)S(1)} %add.543.refs_8_), channel_id=1, source_target_pairs={{0,5},{1,4},{2,7},{3,6},{4,1},{5,0},{6,3},{7,2},{8,13},{9,12},{10,... | collective-permute-start | bytes 73736 | tf_op jit(solution)/shard_map/ppermute | solution.py:733
  136.0 5.8 %collective-permute-start.41 = (f32[8,744,128]{2,1,0:T(8,128)}, f32[8,744,128]{2,1,0:T(8,128)S(1)}, u32[]{:S(2)}, u32[]{:S(2)}) collective-permute-start(f32[8,744,128]{2,1,0:T(8,128)} %get-tuple-element.111), channel_id=1, source_target_pairs={{0,1},{1,0},{2,3},{3,2},{4,5},{5,4},{6,7},{7,6},{8,9},{9,8},{10,11... | collective-permute-start | bytes 9142280 | tf_op jit(solution)/shard_map/ppermute | solution.py:733
  145.6 68.4 %collective-permute-start.58 = (f32[8,744,128]{2,1,0:T(8,128)}, f32[8,744,128]{2,1,0:T(8,128)}, u32[]{:S(2)}, u32[]{:S(2)}) collective-permute-start(f32[8,744,128]{2,1,0:T(8,128)} %add.546.refs_20_), channel_id=1, source_target_pairs={{0,16},{16,0},{1,17},{17,1},{2,18},{18,2},{3,19},{19,3},{4,20},{20... | collective-permute-start | bytes 9142280 | tf_op jit(solution)/shard_map/ppermute | solution.py:733
  146.9 74.5 %collective-permute-start.64 = (f32[8,744,128]{2,1,0:T(8,128)}, f32[8,744,128]{2,1,0:T(8,128)}, u32[]{:S(2)}, u32[]{:S(2)}) collective-permute-start(f32[8,744,128]{2,1,0:T(8,128)} %get-tuple-element.128), channel_id=1, source_target_pairs={{0,1},{1,0},{2,3},{3,2},{4,5},{5,4},{6,7},{7,6},{8,9},{9,8},{10,11... | collective-permute-start | bytes 9142280 | tf_op jit(solution)/shard_map/ppermute | solution.py:733
  146.9 5.6 %collective-permute-start.40 = (f32[2,512]{1,0:T(2,128)S(1)}, f32[2,512]{1,0:T(2,128)S(1)}, u32[]{:S(2)}, u32[]{:S(2)}) collective-permute-start(f32[2,512]{1,0:T(2,128)S(1)} %add.545.refs_4_), channel_id=1, source_target_pairs={{0,13},{1,12},{2,15},{3,14},{4,9},{5,8},{6,11},{7,10},{8,5},{9,4},... | collective-permute-start | bytes 12296 | tf_op jit(solution)/shard_map/ppermute | solution.py:733
  159.0 4.8 %collective-permute-start.46 = (f32[2,512]{1,0:T(2,128)S(1)}, f32[2,512]{1,0:T(2,128)S(1)}, u32[]{:S(2)}, u32[]{:S(2)}) collective-permute-start(f32[2,512]{1,0:T(2,128)S(1)} %add.548.refs_4_), channel_id=1, source_target_pairs={{0,13},{1,12},{2,15},{3,14},{4,9},{5,8},{6,11},{7,10},{8,5},{9,4},... | collective-permute-start | bytes 12296 | tf_op jit(solution)/shard_map/ppermute | solution.py:733
  181.4 51.5 %collective-permute-start.65 = (f32[8,848,128]{2,1,0:T(8,128)}, f32[8,848,128]{2,1,0:T(8,128)}, u32[]{:S(2)}, u32[]{:S(2)}) collective-permute-start(f32[8,848,128]{2,1,0:T(8,128)} %get-tuple-element.130), channel_id=1, source_target_pairs={{0,1},{1,0},{2,3},{3,2},{4,5},{5,4},{6,7},{7,6},{8,9},{9,8},{10,11... | collective-permute-start | bytes 10420232 | tf_op jit(solution)/shard_map/ppermute | solution.py:733
  182.2 26.3 %collective-permute-start.57 = (f32[8,320,128]{2,1,0:T(8,128)}, f32[8,320,128]{2,1,0:T(8,128)}, u32[]{:S(2)}, u32[]{:S(2)}) collective-permute-start(f32[8,320,128]{2,1,0:T(8,128)} %get-tuple-element.124), channel_id=1, source_target_pairs={{0,1},{1,0},{2,3},{3,2},{4,5},{5,4},{6,7},{7,6},{8,9},{9,8},{10,11... | collective-permute-start | bytes 3932168 | tf_op jit(solution)/shard_map/ppermute | solution.py:733
  182.3 4.9 %collective-permute-start.51 = (f32[2,1024]{1,0:T(2,128)S(1)}, f32[2,1024]{1,0:T(2,128)S(1)}, u32[]{:S(2)}, u32[]{:S(2)}) collective-permute-start(f32[2,1024]{1,0:T(2,128)S(1)} %add.550.refs_4_.refs_6_), channel_id=1, source_target_pairs={{0,13},{1,12},{2,15},{3,14},{4,9},{5,8},{6,11},{7,10},{8,5},{9,4},... | collective-permute-start | bytes 24584 | tf_op jit(solution)/shard_map/ppermute | solution.py:733
  203.7 4.8 %collective-permute-start.56 = (f32[2,256]{1,0:T(2,128)S(1)}, f32[2,256]{1,0:T(2,128)S(1)}, u32[]{:S(2)}, u32[]{:S(2)}) collective-permute-start(f32[2,256]{1,0:T(2,128)S(1)} %add.552.refs_4_), channel_id=1, source_target_pairs={{0,13},{1,12},{2,15},{3,14},{4,9},{5,8},{6,11},{7,10},{8,5},{9,4},... | collective-permute-start | bytes 6152 | tf_op jit(solution)/shard_map/ppermute | solution.py:733
  208.5 5.3 %collective-permute-start.55 = (f32[2,256]{1,0:T(2,128)S(1)}, f32[2,256]{1,0:T(2,128)S(1)}, u32[]{:S(2)}, u32[]{:S(2)}) collective-permute-start(f32[2,256]{1,0:T(2,128)S(1)} %add.552.refs_4_), channel_id=1, source_target_pairs={{0,9},{1,8},{2,11},{3,10},{4,13},{5,12},{6,15},{7,14},{8,1},{9,0},... | collective-permute-start | bytes 6152 | tf_op jit(solution)/shard_map/ppermute | solution.py:733
  208.6 5.3 %collective-permute-start.54 = (f32[2,256]{1,0:T(2,128)S(1)}, f32[2,256]{1,0:T(2,128)S(1)}, u32[]{:S(2)}, u32[]{:S(2)}) collective-permute-start(f32[2,256]{1,0:T(2,128)S(1)} %add.552.refs_4_), channel_id=1, source_target_pairs={{0,5},{1,4},{2,7},{3,6},{4,1},{5,0},{6,3},{7,2},{8,13},{9,12},{10,... | collective-permute-start | bytes 6152 | tf_op jit(solution)/shard_map/ppermute | solution.py:733
  219.3 6.1 %collective-permute-start.60 = (f32[2,256]{1,0:T(2,128)S(1)}, f32[2,256]{1,0:T(2,128)S(1)}, u32[]{:S(2)}, u32[]{:S(2)}) collective-permute-start(f32[2,256]{1,0:T(2,128)S(1)} %add.554), channel_id=1, source_target_pairs={{0,3},{1,2},{2,1},{3,0},{4,7},{5,6},{6,5},{7,4},{8,11},{9,10},{10,... | collective-permute-start | bytes 6152 | tf_op jit(solution)/shard_map/ppermute | solution.py:733
  224.5 31.2 %collective-permute-start.66 = (f32[8,320,128]{2,1,0:T(8,128)}, f32[8,320,128]{2,1,0:T(8,128)}, u32[]{:S(2)}, u32[]{:S(2)}) collective-permute-start(f32[8,320,128]{2,1,0:T(8,128)} %add.553.refs_20_), channel_id=1, source_target_pairs={{0,16},{16,0},{1,17},{17,1},{2,18},{18,2},{3,19},{19,3},{4,20},{20... | collective-permute-start | bytes 3932168 | tf_op jit(solution)/shard_map/ppermute | solution.py:733
  225.4 6.7 %collective-permute-start.63 = (f32[2,256]{1,0:T(2,128)S(1)}, f32[2,256]{1,0:T(2,128)S(1)}, u32[]{:S(2)}, u32[]{:S(2)}) collective-permute-start(f32[2,256]{1,0:T(2,128)S(1)} %add.555.refs_4_), channel_id=1, source_target_pairs={{0,13},{1,12},{2,15},{3,14},{4,9},{5,8},{6,11},{7,10},{8,5},{9,4},... | collective-permute-start | bytes 6152 | tf_op jit(solution)/shard_map/ppermute | solution.py:733
  226.9 5.6 %collective-permute-start.62 = (f32[2,256]{1,0:T(2,128)S(1)}, f32[2,256]{1,0:T(2,128)S(1)}, u32[]{:S(2)}, u32[]{:S(2)}) collective-permute-start(f32[2,256]{1,0:T(2,128)S(1)} %add.555.refs_4_), channel_id=1, source_target_pairs={{0,9},{1,8},{2,11},{3,10},{4,13},{5,12},{6,15},{7,14},{8,1},{9,0},... | collective-permute-start | bytes 6152 | tf_op jit(solution)/shard_map/ppermute | solution.py:733
  227.2 5.8 %collective-permute-start.61 = (f32[2,256]{1,0:T(2,128)S(1)}, f32[2,256]{1,0:T(2,128)S(1)}, u32[]{:S(2)}, u32[]{:S(2)}) collective-permute-start(f32[2,256]{1,0:T(2,128)S(1)} %add.555.refs_4_), channel_id=1, source_target_pairs={{0,5},{1,4},{2,7},{3,6},{4,1},{5,0},{6,3},{7,2},{8,13},{9,12},{10,... | collective-permute-start | bytes 6152 | tf_op jit(solution)/shard_map/ppermute | solution.py:733
  232.1 27.3 %collective-permute-start.69 = (f32[8,320,128]{2,1,0:T(8,128)}, f32[8,320,128]{2,1,0:T(8,128)}, u32[]{:S(2)}, u32[]{:S(2)}) collective-permute-start(f32[8,320,128]{2,1,0:T(8,128)} %get-tuple-element.141), channel_id=1, source_target_pairs={{0,1},{1,0},{2,3},{3,2},{4,5},{5,4},{6,7},{7,6},{8,9},{9,8},{10,11... | collective-permute-start | bytes 3932168 | tf_op jit(solution)/shard_map/ppermute | solution.py:733
  232.5 35.6 %collective-permute-start.73 = (f32[4,744,128]{2,1,0:T(8,128)}, f32[4,744,128]{2,1,0:T(8,128)}, u32[]{:S(2)}, u32[]{:S(2)}) collective-permute-start(f32[4,744,128]{2,1,0:T(8,128)} %fusion.1.refs_15_), channel_id=1, source_target_pairs={{0,2},{1,3},{2,0},{3,1},{4,6},{5,7},{6,4},{7,5},{8,10},{9,11},{10,... | collective-permute-start | bytes 4571144 | tf_op jit(solution)/shard_map/ppermute | solution.py:733
  236.1 41.1 %collective-permute-start.70 = (f32[4,848,128]{2,1,0:T(8,128)}, f32[4,848,128]{2,1,0:T(8,128)}, u32[]{:S(2)}, u32[]{:S(2)}) collective-permute-start(f32[4,848,128]{2,1,0:T(8,128)} %bitcast_add_fusion.1.refs_16_), channel_id=1, source_target_pairs={{0,4},{1,5},{2,6},{3,7},{4,0},{5,1},{6,2},{7,3},{8,12},{9,13},{10,... | collective-permute-start | bytes 5210120 | tf_op jit(solution)/shard_map/ppermute | solution.py:733
  259.0 35.6 %collective-permute-start.67 = (f32[16,288,128]{2,1,0:T(8,128)}, f32[16,288,128]{2,1,0:T(8,128)}, u32[]{:S(2)}, u32[]{:S(2)}) collective-permute-start(f32[16,288,128]{2,1,0:T(8,128)} %get-tuple-element.139), channel_id=1, source_target_pairs={{0,1},{1,0},{2,3},{3,2},{4,5},{5,4},{6,7},{7,6},{8,9},{9,8},{10,11... | collective-permute-start | bytes 7077896 | tf_op jit(solution)/shard_map/ppermute | solution.py:733
  269.4 22.8 %collective-permute-start.74 = (f32[2,744,128]{2,1,0:T(8,128)S(1)}, f32[2,744,128]{2,1,0:T(8,128)S(1)}, u32[]{:S(2)}, u32[]{:S(2)}) collective-permute-start(f32[2,744,128]{2,1,0:T(8,128)S(1)} %fusion.5), channel_id=1, source_target_pairs={{0,4},{1,5},{2,6},{3,7},{4,0},{5,1},{6,2},{7,3},{8,12},{9,13},{10,... | collective-permute-start | bytes 2285576 | tf_op jit(solution)/shard_map/ppermute | solution.py:733
  280.2 30.9 %collective-permute-start.72 = (f32[4,320,128]{2,1,0:T(8,128)S(1)}, f32[4,320,128]{2,1,0:T(8,128)S(1)}, u32[]{:S(2)}, u32[]{:S(2)}) collective-permute-start(f32[4,320,128]{2,1,0:T(8,128)S(1)} %fusion.7), channel_id=1, source_target_pairs={{0,2},{1,3},{2,0},{3,1},{4,6},{5,7},{6,4},{7,5},{8,10},{9,11},{10,... | collective-permute-start | bytes 1966088 | tf_op jit(solution)/shard_map/ppermute | solution.py:733
  292.3 18.8 %collective-permute-start.80 = (f32[1,744,128]{2,1,0:T(8,128)S(1)}, f32[1,744,128]{2,1,0:T(8,128)S(1)}, u32[]{:S(2)}, u32[]{:S(2)}) collective-permute-start(f32[1,744,128]{2,1,0:T(8,128)S(1)} %bitcast_add_fusion.12), channel_id=1, source_target_pairs={{0,8},{1,9},{2,10},{3,11},{4,12},{5,13},{6,14},{7,15},{8,0},{9,1},... | collective-permute-start | bytes 1142792 | tf_op jit(solution)/shard_map/ppermute | solution.py:733
  293.1 20.2 %collective-permute-start.81 = (f32[2,848,128]{2,1,0:T(8,128)S(1)}, f32[2,848,128]{2,1,0:T(8,128)S(1)}, u32[]{:S(2)}, u32[]{:S(2)}) collective-permute-start(f32[2,848,128]{2,1,0:T(8,128)S(1)} %get-tuple-element.145), channel_id=1, source_target_pairs={{0,2},{1,3},{2,0},{3,1},{4,6},{5,7},{6,4},{7,5},{8,10},{9,11},{10,... | collective-permute-start | bytes 2605064 | tf_op jit(solution)/shard_map/ppermute | solution.py:733
  296.7 30.1 %collective-permute-start.68 = (f32[8,288,128]{2,1,0:T(8,128)S(1)}, f32[8,288,128]{2,1,0:T(8,128)S(1)}, u32[]{:S(2)}, u32[]{:S(2)}) collective-permute-start(f32[8,288,128]{2,1,0:T(8,128)S(1)} %get-tuple-element.143), channel_id=1, source_target_pairs={{0,16},{16,0},{1,17},{17,1},{2,18},{18,2},{3,19},{19,3},{4,20},{20... | collective-permute-start | bytes 3538952 | tf_op jit(solution)/shard_map/ppermute | solution.py:733
  311.2 15.4 %collective-permute-start.78 = (f32[2,320,128]{2,1,0:T(8,128)S(1)}, f32[2,320,128]{2,1,0:T(8,128)S(1)}, u32[]{:S(2)}, u32[]{:S(2)}) collective-permute-start(f32[2,320,128]{2,1,0:T(8,128)S(1)} %fusion.13), channel_id=1, source_target_pairs={{0,4},{1,5},{2,6},{3,7},{4,0},{5,1},{6,2},{7,3},{8,12},{9,13},{10,... | collective-permute-start | bytes 983048 | tf_op jit(solution)/shard_map/ppermute | solution.py:733
  313.4 27.4 %collective-permute-start.82 = (f32[1,848,128]{2,1,0:T(8,128)S(1)}, f32[1,848,128]{2,1,0:T(8,128)S(1)}, u32[]{:S(2)}, u32[]{:S(2)}) collective-permute-start(f32[1,848,128]{2,1,0:T(8,128)S(1)} %bitcast_add_fusion.9), channel_id=1, source_target_pairs={{0,8},{1,9},{2,10},{3,11},{4,12},{5,13},{6,14},{7,15},{8,0},{9,1},... | collective-permute-start | bytes 1302536 | tf_op jit(solution)/shard_map/ppermute | solution.py:733
  326.7 14.1 %collective-permute-start.79 = (f32[1,320,128]{2,1,0:T(8,128)S(1)}, f32[1,320,128]{2,1,0:T(8,128)S(1)}, u32[]{:S(2)}, u32[]{:S(2)}) collective-permute-start(f32[1,320,128]{2,1,0:T(8,128)S(1)} %bitcast_add_fusion.15), channel_id=1, source_target_pairs={{0,8},{1,9},{2,10},{3,11},{4,12},{5,13},{6,14},{7,15},{8,0},{9,1},... | collective-permute-start | bytes 491528 | tf_op jit(solution)/shard_map/ppermute | solution.py:733
  326.9 14.3 %collective-permute-start.71 = (f32[4,288,128]{2,1,0:T(8,128)S(1)}, f32[4,288,128]{2,1,0:T(8,128)S(1)}, u32[]{:S(2)}, u32[]{:S(2)}) collective-permute-start(f32[4,288,128]{2,1,0:T(8,128)S(1)} %bitcast_add_fusion.8), channel_id=1, source_target_pairs={{0,2},{1,3},{2,0},{3,1},{4,6},{5,7},{6,4},{7,5},{8,10},{9,11},{10,... | collective-permute-start | bytes 1769480 | tf_op jit(solution)/shard_map/ppermute | solution.py:733
  341.2 7.2 %collective-permute-start.75 = (f32[2,288,128]{2,1,0:T(8,128)S(1)}, f32[2,288,128]{2,1,0:T(8,128)S(1)}, u32[]{:S(2)}, u32[]{:S(2)}) collective-permute-start(f32[2,288,128]{2,1,0:T(8,128)S(1)} %bitcast_add_fusion.14), channel_id=1, source_target_pairs={{0,4},{1,5},{2,6},{3,7},{4,0},{5,1},{6,2},{7,3},{8,12},{9,13},{10,... | collective-permute-start | bytes 884744 | tf_op jit(solution)/shard_map/ppermute | solution.py:733
  343.5 14.6 %collective-permute-start.83 = (f32[1168,128]{1,0:T(8,128)S(1)}, f32[1168,128]{1,0:T(8,128)S(1)}, u32[]{:S(2)}, u32[]{:S(2)}) collective-permute-start(f32[1168,128]{1,0:T(8,128)S(1)} %maximum_select_fusion.1), channel_id=1, source_target_pairs={{0,16},{16,0},{1,17},{17,1},{2,18},{18,2},{3,19},{19,3},{4,20},{20... | collective-permute-start | bytes 1794056 | tf_op jit(solution)/shard_map/ppermute | solution.py:733
  349.1 7.7 %collective-permute-start.76 = (f32[1,288,128]{2,1,0:T(8,128)S(1)}, f32[1,288,128]{2,1,0:T(8,128)S(1)}, u32[]{:S(2)}, u32[]{:S(2)}) collective-permute-start(f32[1,288,128]{2,1,0:T(8,128)S(1)} %bitcast_add_fusion.18), channel_id=1, source_target_pairs={{0,8},{1,9},{2,10},{3,11},{4,12},{5,13},{6,14},{7,15},{8,0},{9,1},... | collective-permute-start | bytes 442376 | tf_op jit(solution)/shard_map/ppermute | solution.py:733
  356.8 4.1 %collective-permute-start.77 = (f32[88,128]{1,0:T(8,128)S(1)}, f32[88,128]{1,0:T(8,128)S(1)}, u32[]{:S(2)}, u32[]{:S(2)}) collective-permute-start(f32[88,128]{1,0:T(8,128)S(1)} %broadcast_add_fusion), channel_id=1, source_target_pairs={{0,16},{16,0},{1,17},{17,1},{2,18},{18,2},{3,19},{19,3},{4,20},{20... | collective-permute-start | bytes 135176 | tf_op jit(solution)/shard_map/ppermute | solution.py:733
  (118 other events, 1028.0 us)

commit v3 on v2

--- a/solution.py
+++ b/solution.py
@@ -13,8 +13,7 @@
 low_type = jnp.bfloat16
 full_type = jnp.float32
 vmem_small, vmem_large = 6 * 1024 * 1024, 18 * 1024 * 1024
-cost_small, cost_large = 0.1, 0.1
-halved_of_128 = 56
+cost_small = 0.1
 
 even_width = 8
 
@@ -638,29 +637,63 @@
 
 
 def low_rows(rows):
-    part = rows * halved_of_128 // 2048 * 8
-    return [part, part, rows - 2 * part]
-
-
-def copy_windows(source, outs, sems, first_device, first_row, share_size, offsets):
-    owners, _, width = outs[0].shape
-    pieces = len(offsets)
-    core = lax.axis_index("dp") % 2
-    copies = []
-    for piece in range(pieces):
-        for which, chosen in enumerate((1 - core, core)):
-            out = outs[which * pieces + piece]
-            for owner in range(owners):
-                begin = window_start(first_device + 2 * owner + chosen, share_size, width) - first_row + offsets[piece]
-                rows_here = pl.ds(pl.multiple_of(begin, 8), out.shape[1])
-                copies.append(pltpu.make_async_copy(source.at[rows_here], out.at[owner], sems.at[len(copies)]))
-    for copy in copies:
-        copy.start()
-    for copy in copies:
-        copy.wait()
-
-
-def put_filter(store, begin, value, grad):
+    first = rows // 32 * 8
+    return [first, rows // 2 - first] * 2
+
+
+class AllCopies:
+    def __init__(self, source, out, sems, first_device, first_row, share_size):
+        self.waiting, self.started = [], []
+        owners, rows, width = out.shape
+        for owner in range(owners):
+            begin = window_start(first_device + owner, share_size, width) - first_row
+            copy = pltpu.make_async_copy(source.at[pl.ds(begin, rows)], out.at[owner], sems.at[owner])
+            self.waiting.append((begin + rows, copy))
+
+    def start(self, filled):
+        for end, copy in self.waiting:
+            if end <= filled:
+                copy.start()
+                self.started.append(copy)
+        self.waiting = [item for item in self.waiting if item[0] > filled]
+
+    def finish(self, filled):
+        self.start(filled)
+        for copy in self.started:
+            copy.wait()
+
+
+class Copies:
+    def __init__(self, source, outs, sems, first_device, first_row, share_size, offsets):
+        self.waiting, self.started = [], []
+        owners, _, width = outs[0].shape
+        pieces = len(offsets)
+        core = lax.axis_index("dp") % 2
+        for owner in range(owners):
+            device = first_device + 2 * owner
+            end = window_start(device + 1, share_size, width) + window_rows(share_size, width) - first_row
+            for piece in range(pieces):
+                for which, chosen in enumerate((1 - core, core)):
+                    out = outs[which * pieces + piece]
+                    begin = window_start(device + chosen, share_size, width) - first_row + offsets[piece]
+                    rows = pl.ds(pl.multiple_of(begin, 8), out.shape[1])
+                    sem = sems.at[(owner * pieces + piece) * 2 + which]
+                    self.waiting.append((end, pltpu.make_async_copy(source.at[rows], out.at[owner], sem)))
+
+    def start(self, filled):
+        for end, copy in self.waiting:
+            if end <= filled:
+                copy.start()
+                self.started.append(copy)
+        self.waiting = [item for item in self.waiting if item[0] > filled]
+
+    def finish(self, filled):
+        self.start(filled)
+        for copy in self.started:
+            copy.wait()
+
+
+def put_filter(store, begin, value, grad, copies=None):
     step, across = 256, min(512, grad.shape[1])
     lanes = store.shape[1]
     cuts = grad.shape[1] // lanes
@@ -670,32 +703,35 @@
             for cut in range(across // lanes):
                 place = begin + row * cuts + column // lanes + cut
                 store[pl.ds(place, step, stride=cuts), :] = result[:, cut * lanes : cut * lanes + lanes]
+        if copies is not None:
+            copies.start(begin + (row + step) * cuts)
     return begin + value.shape[1] * cuts
 
 
-def late_filters_body(first_device, first_row, share_size, hidden_ref, picked_ref, low_ref, side_low_ref, *rest):
-    *outs, spill_ref, store, sems = rest
-    filled = put_filter(store, 0, hidden_ref, low_ref)
-    filled = put_filter(store, filled, picked_ref, side_low_ref)
+def late_filters_body(first_device, first_row, share_size, hidden_ref, picked_ref, low_ref, side_low_ref, out_ref, spill_ref, store, sems):
+    copies = AllCopies(store, out_ref, sems, first_device, first_row, share_size)
+    filled = hidden_ref.shape[1] * low_ref.shape[1] // 128 + picked_ref.shape[1] * side_low_ref.shape[1] // 128
     store[filled:, :] = jnp.zeros((store.shape[0] - filled, store.shape[1]), full_type)
+    filled = put_filter(store, 0, hidden_ref, low_ref, copies)
     spill_ref[...] = store[: spill_ref.shape[0], :]
-    view = lax.axis_index("view")
-    rows = outs[0].shape[1]
-    copy_windows(store, outs, sems, first_device, first_row, share_size, ((1 - view) * rows, view * rows))
+    put_filter(store, filled, picked_ref, side_low_ref, copies)
+    copies.finish(store.shape[0])
 
 
 def middle_filters_body(share_size, block_ref, low_ref, even_ref, moved_ref, inner_low_ref, spill_ref, *rest):
     *outs, store, sems = rest
-    filled = put_filter(store, 0, block_ref, low_ref)
+    view = lax.axis_index("view")
+    first, half = outs[0].shape[1], outs[0].shape[1] + outs[1].shape[1]
+    far, near = (1 - view) * half, view * half
+    copies = Copies(store, outs, sems, 0, 0, share_size, (far, far + first, near, near + first))
+    store[store.shape[0] - spill_ref.shape[0] :, :] = spill_ref[...]
+    filled = put_filter(store, 0, block_ref, low_ref, copies)
     half = even_ref.shape[0] // 2 - 1
     for row in range(3):
         for ref, plane in ((moved_ref, 1), (even_ref, 0), (even_ref, 1)):
             lhs = jnp.concatenate([ref[2 * index + row, plane] for index in range(half)], axis=0)
-            filled = put_filter(store, filled, lhs, inner_low_ref)
-    store[filled:, :] = spill_ref[...]
-    view = lax.axis_index("view")
-    rows = outs[0].shape[1]
-    copy_windows(store, outs, sems, 0, 0, share_size, ((1 - view) * rows, view * rows, 2 * rows))
+            filled = put_filter(store, filled, lhs, inner_low_ref, copies)
+    copies.finish(store.shape[0])
 
 
 def block_filter_body(even_ref, moved_ref, inner_low_ref, hidden_ref, outer_low_ref, out_ref):
@@ -721,12 +757,36 @@
 
 def early_filters_body(share_size, start_ref, low_ref, later_ref, *rest):
     *outs, store, sems = rest
+    copies = Copies(store, outs, sems, 0, 0, share_size, (0,))
     filled = put_filter(store, 0, start_ref, low_ref)
     later = later_ref.shape[0]
     store[filled : filled + later, :] = later_ref[...]
     filled += later
     store[filled:, :] = jnp.zeros((store.shape[0] - filled, store.shape[1]), full_type)
-    copy_windows(store, outs, sems, 0, 0, share_size, (0,))
+    copies.finish(store.shape[0])
+
+
+def late_window_body(place, high_ref, high_got_ref, low_ref, low_got_ref, norms_ref, out_ref):
+    view = lax.axis_index("view")
+    half = low_ref.shape[0]
+
+    @pl.when(view == 0)
+    def _():
+        out_ref[:half, :] = low_ref[...]
+        out_ref[half:, :] = low_got_ref[...]
+
+    @pl.when(view == 1)
+    def _():
+        out_ref[...] = high_ref[...] + high_got_ref[...]
+
+    rows = pl.ds(place, norms_ref.shape[0])
+    out_ref[rows, :] += norms_ref[...]
+
+
+def early_window_body(place, refs, norms_ref, out_ref):
+    out_ref[...] = add_terms(refs)
+    rows = pl.ds(place, norms_ref.shape[0])
+    out_ref[rows, :] += norms_ref[...]
 
 
 def exchange(value, axis, bits):
@@ -750,38 +810,49 @@
     return parts
 
 
-def own_bit(axis, bit):
-    return (lax.axis_index(axis) >> bit) & 1
-
-
-class Windows:
-    def __init__(self, kept, received, bits):
-        self.kept, self.received, self.bits = kept, received, list(bits)
-
-    def step(self, item, *gates):
-        axis, bit = item
-        place = self.bits.index(item)
-        own = own_bit(axis, bit)
-        rows, width = self.kept.shape[1:]
-        before, after = 1 << place, 1 << (len(self.bits) - place - 1)
-
-        def pick(value, index):
-            cut = value.reshape(before, 2, after, rows, width)
-            part = lax.dynamic_slice(cut, (0, index, 0, 0, 0), (before, 1, after, rows, width))
-            return part.reshape(before * after, rows, width)
-
-        self.sent = pick(self.kept, 1 - own) + pick(self.received, 1 - own) + sum(gates, 0.0)
-        self.kept = pick(self.kept, own) + pick(self.received, own)
-        self.received = exchange(self.sent, axis, 1 << bit)
-        self.bits.pop(place)
-
-    def total(self):
-        return (self.kept + self.received)[0]
+def add_terms(refs):
+    result = refs[0][...]
+    for ref in refs[1:]:
+        result = result + ref[...]
+    return result
 
 
 def gate(value):
     corner = value[(slice(0, 1),) * (value.ndim - 1) + (slice(0, 128),)]
     return 0.0 * corner.reshape(1, 1, 128)
+
+
+class Term:
+    def __init__(self, value, bits):
+        self.value, self.bits, self.chosen = value, list(bits), {}
+
+    def part(self, chosen):
+        rows, width = self.value.shape[1:]
+        cut = self.value.reshape((2,) * len(self.bits) + (rows, width))
+        starts = [chosen.get(item, 0) for item in self.bits] + [0, 0]
+        sizes = [1 if item in chosen else 2 for item in self.bits] + [rows, width]
+        return lax.dynamic_slice(cut, starts, sizes).reshape(-1, rows, width)
+
+
+class Windows:
+    def __init__(self, terms, bits):
+        self.terms, self.bits, self.chosen = [Term(value, bits) for value in terms], list(bits), {}
+
+    def step(self, item, *after):
+        axis, bit = item
+        own = (lax.axis_index(axis) >> bit) & 1
+        chosen = dict(self.chosen)
+        chosen[item] = 1 - own
+        self.sent = sum([term.part(chosen) for term in self.terms[1:]], self.terms[0].part(chosen))
+        if after:
+            self.sent = self.sent + sum(gate(value) for value in after)
+        self.received = exchange(self.sent, axis, 1 << bit)
+        self.chosen[item] = own
+        self.bits.remove(item)
+        self.terms.append(Term(self.received, self.bits))
+
+    def total(self):
+        return (sum([term.part(self.chosen)[0] for term in self.terms[1:]], self.terms[0].part(self.chosen)[0]),)
 
 
 def per_device(
@@ -993,26 +1064,23 @@
         scratch=[((8, 128), full_type)],
     )
     grads_sb = share(sums)
-    *outs, spill = call(
+    late_windows, spill = call(
         functools.partial(late_filters_body, size, first_rows, share_b),
-        windows(half, [window_b // 2] * 2) + [shaped(end_low - first_rows, lanes)],
+        [pltpu.HBM((size, window_b, lanes), full_type), shaped(end_low - first_rows, lanes)],
         [hidden_two_b, picked, low_eb, low_sc],
         scratch=[((end_high - first_rows, lanes), full_type)],
-        copies=4 * half,
+        copies=size,
         vmem=vmem_large,
-        cost_us=cost_large,
         after=(grads_sb[0],),
     )
     grad_picked = call(times_back_body, [shaped(rows_small, depth_a)], [low_sc, shortcut_b])[0]
-    far, near = pairs_of(outs)
-    far_sum = far[0] + far[1]
-    high = Windows(near[0] + near[1], exchange(far_sum, "view", 1), bits)
+    high_sum = lax.psum_scatter(late_windows, "dp", scatter_dimension=0, tiled=False)
     low_sb, grad_rb, sums = call(
         with_images(shrink_back_body),
         [shaped(rows_small, middle_b, kind=low_type), shaped(rows_big, middle_b), shaped(2, middle_b)],
         [sums_sb, grads_sb, grad_sb, mixed_b, counts, scale_sb, mask_small, spatial_b9, sums_rb, reduced_b, slope_rb],
         scratch=[((16, middle_b), full_type)],
-        after=(far_sum, grad_picked),
+        after=(spill, grad_picked),
     )
     grads_rb = share(sums)
     low_rb, joined_grad, sums = call(
@@ -1022,27 +1090,29 @@
         scratch=[((16, depth_a), full_type)],
     )
     grads_ea = share(sums)
+    outs_low = call(
+        functools.partial(middle_filters_body, share_b),
+        windows(half, low_rows(window_b)),
+        [block_a, low_rb, even_b, moved_b, low_sb, spill],
+        scratch=[((end_low, lanes), full_type)],
+        copies=8 * half,
+        vmem=vmem_large,
+        after=(grads_ea[0],),
+    )
     low_ea, grad_sa, sums = call(
         functools.partial(expand_back_body, rows_step=4 * line),
         [shaped(rows_big, depth_a, kind=low_type), shaped(rows_big, middle_a), shaped(2, middle_a)],
         [sums_ea, grads_ea, joined_grad, expanded_a, counts, scale_ea, mask_big, expand_a, sums_sa, mixed_a, slope_sa],
         scratch=[((16, middle_a), full_type)],
+        after=(outs_low[0],),
     )
     grads_sa = share(sums)
-    outs = call(
-        functools.partial(middle_filters_body, share_b),
-        windows(half, low_rows(window_b)),
-        [block_a, low_rb, even_b, moved_b, low_sb, spill],
-        scratch=[((end_low, lanes), full_type)],
-        copies=6 * half,
-        vmem=vmem_large,
-        cost_us=cost_large,
-        after=(grads_ea[0],),
-    )
-    far, near, whole = pairs_of(outs)
-    far_sum = far[0] + far[1]
-    low_half = Windows(near[0] + near[1], exchange(far_sum, "view", 1), bits)
-    low_whole = Windows(*whole, bits)
+    far_one, far_two, near_one, near_two = pairs_of(outs_low)
+    far_sum_one = far_one[0] + far_one[1]
+    far_sum_two = far_two[0] + far_two[1]
+    got_one, got_two = exchange(far_sum_one, "view", 1), exchange(far_sum_two, "view", 1)
+    low_one = Windows(near_one + (got_one,), bits)
+    low_two = Windows(near_two + (got_two,), bits)
     low_sa, grad_ra, sums = call(
         with_images(block_back_body),
         [shaped(rows_big, middle_a, kind=low_type), shaped(rows_big, middle_a), shaped(2, middle_a)],
@@ -1052,15 +1122,14 @@
             ((height + 2, 2, line, middle_a), low_type),
             ((16, middle_a), full_type),
         ],
-        after=(far_sum, high.received),
+        after=(far_sum_one, far_sum_two),
     )
     grads_ra = share(sums)
     ready, x_bit, z_bits = [], low_first[:1], low_first[1:]
     if bits:
         x_bit = x_bit[0]
-        high.step(x_bit, gate(grads_ra[0]))
-        low_whole.step(z_bits[0] if z_bits else x_bit, *(gate(part) for part in grads_ra[1:]))
-        ready = [high.sent, low_whole.sent]
+        low_one.step(x_bit, *grads_ra[1:])
+        ready = [low_one.sent]
     low_ra, input_grad = call(
         with_images(exit_body),
         [shaped(rows_big, middle_a, kind=low_type), shaped(height, pairs, 2, images, depth_a, kind=low_type)],
@@ -1076,7 +1145,7 @@
         block_filter_body,
         [shaped((total_a - norm_rows_a) - depth_a * middle_a // lanes, lanes)],
         [even_a, moved_a, low_sa, hidden_two_a, low_ea],
-        cost_us=cost_large,
+        after=(low_ra,),
     )[0]
     outs = call(
         functools.partial(early_filters_body, share_a),
@@ -1085,46 +1154,28 @@
         scratch=[((end_a, lanes), full_type)],
         copies=2 * size,
         vmem=2 * vmem_small,
-        cost_us=cost_large,
-        after=(low_half.received,),
-    )
-    early = Windows(*pairs_of(outs)[0], [("view", 0)] + bits)
+        after=(got_two,) + ((low_one.received,) if bits else ()),
+    )
+    early = Windows(pairs_of(outs)[0], [("view", 0)] + bits)
     early.step(("view", 0))
-    if z_bits:
-        high.step(z_bits[0])
-        low_whole.step(x_bit)
-        low_half.step(x_bit, gate(low_whole.sent))
+    early_got = early.received
+    if bits:
+        for item in z_bits[:1]:
+            low_one.step(item)
+        low_two.step(x_bit, early.sent)
         for item in z_bits[1:]:
-            high.step(item)
-            low_whole.step(item)
-        early.step(x_bit, gate(low_half.sent))
-        low_half.step(z_bits[0], gate(high.sent))
-        early.step(z_bits[0], gate(low_half.sent))
-        for item in z_bits[1:]:
-            low_half.step(item)
+            low_one.step(item)
+        early.step(x_bit)
+        for item in z_bits:
+            low_two.step(item)
+        for item in z_bits:
             early.step(item)
-    elif bits:
-        low_half.step(x_bit)
-        early.step(x_bit)
-    early_window = early.total()
-    view = lax.axis_index("view")
     all_grads = [sum(parts[1:], parts[0]) for parts in (grads_rb, grads_sb, grads_eb, grads_ra, grads_sa, grads_ea)]
     norms = jnp.concatenate([value.reshape(-1, lanes) for value in all_grads], axis=0)
-    norms = norms + exchange(norms + gate(early.received)[0], "view", 1)
-    high_half, low_half, low_rest = high.total(), low_half.total(), low_whole.total()
-    short = low_half.shape[0] + low_rest.shape[0] - high_half.shape[0]
-    swapped = exchange(
-        jnp.where(
-            view == 0, jnp.pad(high_half, ((0, short), (0, 0))), jnp.concatenate([low_half, low_rest], axis=0)
-        ),
-        "view",
-        1,
-    )
-    late_window = jnp.where(
-        view == 0,
-        jnp.concatenate([low_half, swapped[: low_half.shape[0]], low_rest + swapped[low_half.shape[0] :]], axis=0),
-        jnp.concatenate([swapped[: high_half.shape[0]], high_half], axis=0),
-    )
+    norms = norms + exchange(norms + 0.0 * early_got[0, :1], "view", 1)
+    packed_last = jnp.concatenate([low_one.total()[0], low_two.total()[0]], axis=0)
+    high_got = lax.ppermute(high_sum, "view", [(0, 1)])
+    low_last = lax.ppermute(packed_last, "view", [(1, 0)])
     cut = []
     for value in all_grads:
         rows = value.size // lanes
@@ -1134,17 +1185,29 @@
     norms_a = cut[3:]
     device = lax.axis_index("view") * size + lax.axis_index("dp")
 
-    def finish(window, norms, rows, norm_rows, share_size):
-        width = window.shape[1]
-        place = rows - norm_rows - window_start(2 * size - 1, share_size, width)
-        values = jnp.concatenate([value.reshape(-1) for value in norms]).reshape(norm_rows, width)
-        values = jnp.where(device == 2 * size - 1, values, 0.0)
-        window = window + jnp.pad(values, ((place, window.shape[0] - place - norm_rows), (0, 0)))
-        begin = device * share_size - window_start(device, share_size, width) * width
+    def norm_block(norms):
+        values = jnp.concatenate([value.reshape(-1, lanes) for value in norms], axis=0)
+        return jnp.where(device == 2 * size - 1, values, 0.0)
+
+    def cut_out(window, share_size):
+        begin = device * share_size - window_start(device, share_size, lanes) * lanes
         return lax.dynamic_slice(window.reshape(-1), (begin,), (share_size,))
 
-    late_done = finish(late_window, norms_b, total_b, norm_rows_b, share_b)
-    early_done = finish(early_window, norms_a, total_a, norm_rows_a, share_a)
+    late_place = total_b - norm_rows_b - window_start(2 * size - 1, share_b, lanes)
+    late_window = call(
+        functools.partial(late_window_body, late_place),
+        [shaped(window_b, lanes)],
+        [high_sum, high_got, packed_last, low_last, norm_block(norms_b)],
+        cost_us=0,
+    )[0]
+    early_place = total_a - norm_rows_a - window_start(2 * size - 1, share_a, lanes)
+    early_window = call(
+        functools.partial(early_window_body, early_place),
+        [shaped(window_a, lanes)],
+        [early.total(), norm_block(norms_a)],
+        cost_us=0,
+    )[0]
+    late_done, early_done = cut_out(late_window, share_b), cut_out(early_window, share_a)
 
     def natural(value):
         return value.reshape(height, height, images, depth_a).transpose(2, 0, 1, 3)[None]

time: 364 us -> 357 us (0.981)
  waiting for transfers between devices: 132 us -> 109 us
  between operations: 1.99 us -> 15.9 us
  starting transfers between devices: 92.4 us -> 102 us
  other arithmetic: 31.2 us -> 24.9 us
  Pallas kernels: 80.6 us -> 76.2 us
    ppermute x84 -> x79, waiting for transfers between devices: 132 us -> 107 us  [exchange(): lax.ppermute(value, axis, [(i, i ^ bits) for i in range(lax.axis_size(axi...]
    add x34 -> x22, other arithmetic: 30.6 us -> 23.9 us  [the longest x11 14.6 us: step(): sum([term.part(chosen) for term in self.terms[1:]], self.terms[0].part(ch...]
    ppermute x84 -> x79, starting transfers between devices: 92.4 us -> 98.1 us  [exchange(): lax.ppermute(value, axis, [(i, i ^ bits) for i in range(lax.axis_size(axi...]
    pallas_call x26 -> x28, Pallas kernels: 80.6 us -> 76.2 us  [call(): pl.pallas_call(run, out_shape=outs, in_specs=[pl.BlockSpec(memory_space=p...]
    ppermute x0 -> x2, starting transfers between devices: none -> 3.98 us  [the longest x1 2.68 us: per_device(): high_got = lax.ppermute(high_sum, 'view', [(0, 1)])]
    unnamed x169 -> x257, local copies, waits for them, and re-layouts: 20.4 us -> 24.3 us
  transfers between devices with their start and end apart: 84 -> 82, of which waited for: 51 -> 54; matrix products, arithmetic and copies ran while one was open for 8% -> 8% of each run, Pallas kernels for 12% -> 12%
where the time goes in v3:
time: 357 us; the launch traced here: 356 us
  waiting for transfers between devices  109 us (31%)
  starting transfers between devices  102 us (29%)
  Pallas kernels  76.2 us (21%)
  local copies, waits for them, and re-layouts  28.3 us (8%)
  other arithmetic  24.9 us (7%)
  between operations  15.9 us (4%)
    ppermute x79, waiting for transfers between devices, exchange(): lax.ppermute(value, axis, [(i, i ^ bits) for i in range(lax.axis_size(axi...  107 us
    ppermute x79, starting transfers between devices, exchange(): lax.ppermute(value, axis, [(i, i ^ bits) for i in range(lax.axis_size(axi...  98.1 us
    pallas_call x28, Pallas kernels, call(): pl.pallas_call(run, out_shape=outs, in_specs=[pl.BlockSpec(memory_space=p...  76.2 us
    unnamed x257, local copies, waits for them, and re-layouts  24.3 us
    add x11, other arithmetic, step(): sum([term.part(chosen) for term in self.terms[1:]], self.terms[0].part(ch...  14.6 us
  transfers between devices with their start and end apart: 82, of which 54 were waited for; matrix products, arithmetic and copies ran while one was open for 8% of the time, Pallas kernels for 12%

profile of v3, /device:TPU:0, one launch (start us, length us, event | category | flops | bytes accessed | tf_op | source)
XLA Modules:
  0.0 356.2 jit_solution(5035155500751356478)
XLA Ops:
  10.5 2.9 shard_map.262
  16.4 2.6 collective-permute-start.1
  20.4 3.8 %collective-permute-start.4 = (f32[4,256]{1,0:T(4,128)S(1)}, f32[4,256]{1,0:T(4,128)S(1)}, u32[]{:S(2)}, u32[]{:S(2)}) collective-permute-start(f32[4,256]{1,0:T(4,128)S(1)} %add.595.refs_0_.refs_14_), channel_id=1, source_target_pairs={{0,13},{1,12},{2,15},{3,14},{4,9},{5,8},{6,11},{7,10},{8,5},{9,4},... | collective-permute-start | bytes 12296 | tf_op jit(solution)/shard_map/ppermute | solution.py:793
  25.5 2.6 collective-permute-done.3.refs_2_.refs_16_
  29.4 2.5 shard_map.263
  39.5 2.2 collective-permute-start.7
  43.2 2.7 shard_map.265
  57.0 7.2 %shard_map.267 = (bf16[896,1024]{1,0:T(8,128)(2,1)S(1)}, f32[896,512]{1,0:T(8,128)S(1)}, bf16[224,1024]{1,0:T(8,128)(2,1)S(1)}, f32[224,2048]{1,0:T(8,128)S(1)},...) custom-call(f32[2,1024]{1,0:T(2,128)S(1)} %add.599.refs_0_.refs_15_, ...), custom_call_target="tpu_custom_call" | custom-call | flops 100000000 | bytes 100000 | tf_op jit(solution)/shard_map/pallas_call | solution.py:51
  72.9 4.7 %shard_map.268.refs_10_.refs_20_ = bf16[896,1024]{1,0:T(8,128)(2,1)S(1)} custom-call(f32[2,1024]{1,0:T(2,128)S(1)} %add.599.refs_0_.refs_15_, f32[2,1024]{1,0:T(2,128)S(1)} %collective-permute-done.12.refs_1_.refs_16_, f32[2,1024]{1,0:T(2,128)S(1)} %collective-permute-done.13.refs_2_.refs_17_, f32[2,1024]{1,0:T(2,128)S(1)} %collective-permute-done.14.refs_3_.refs_18_, ...), custom_call_target="tpu_custom_call" | custom-call | flops 100000000 | bytes 100000 | tf_op jit(solution)/shard_map/pallas_call | solution.py:51
  77.7 3.7 %shard_map.269 = (bf16[16,2,32,512]{3,2,1,0:T(8,128)(2,1)S(1)}, bf16[16,2,32,512]{3,2,1,0:T(8,128)(2,1)S(1)}, f32[224,512]{1,0:T(8,128)S(1)}, f32[2,512]{1,0:T(2,128)S(1)}) custom-call(f32[2,2560]{1,0:T(2,128)S(1)} %add.601.refs_0_.refs_4_.refs_14_, f32[2,2560]{1,0:T(2,128)S(1)} %collective-permute-done.17.refs_1_.refs_5_.refs_15_, ...), custom_call_target="tpu_custom_call" | custom-call | flops 100000000 | bytes 100000 | tf_op jit(solution)/shard_map/pallas_call | solution.py:51
  88.1 2.5 collective-permute-start.22
  90.6 2.3 shard_map.270.refs_9_.refs_19_
  94.7 3.4 shard_map.272
  104.5 2.3 collective-permute-start.27
  108.6 3.6 %shard_map.274 = (bf16[7,7,4,2048]{3,2,1,0:T(4,128)(2,1)}, f32[224,2048]{1,0:T(8,128)S(1)}, f32[4,2048]{1,0:T(4,128)S(1)}) custom-call(f32[2,2048]{1,0:T(2,128)S(1)} %add.605.refs_0_, f32[2,2048]{1,0:T(2,128)S(1)} %collective-permute-done.27.refs_1_, f32[2,2048]{1,0:T(2,128)S(1)} %collective-permute-done.28.refs_2_, ...), custom_call_target="tpu_custom_call" | custom-call | flops 100000000 | bytes 100000 | tf_op jit(solution)/shard_map/pallas_call | solution.py:51
  113.7 2.6 shard_map.275
  128.3 2.4 shard_map.277
  135.7 6.4 %shard_map.278 = (f32[16,1488,128]{2,1,0:T(8,128)}, f32[1072,128]{1,0:T(8,128)S(1)}) custom-call(bf16[224,512]{1,0:T(8,128)(2,1)S(1)} %get-tuple-element.105.refs_0_, bf16[224,1024]{1,0:T(8,128)(2,1)S(1)} %get-tuple-element.106.refs_1_, bf16[224,2048]{1,0:T(8,128)(2,1)S(1)} %get-tuple-element.107.refs_2_, ...), custom_call_target="tpu_custom_call" | custom-call | flops 100000000 | bytes 100000 | tf_op jit(solution)/shard_map/pallas_call | solution.py:51
  145.7 2.2 collective-permute-start.38
  147.9 2.6 copy-done.4
  153.8 3.0 copy-done.2
  164.0 2.9 collective-permute-start.43
  168.3 4.1 %shard_map.281 = (bf16[896,512]{1,0:T(8,128)(2,1)S(1)}, f32[896,1024]{1,0:T(8,128)S(1)}, f32[2,1024]{1,0:T(2,128)S(1)}) custom-call(f32[2,2560]{1,0:T(2,128)S(1)} %add.601.refs_0_.refs_4_.refs_14_, f32[2,2560]{1,0:T(2,128)S(1)} %collective-permute-done.17.refs_1_.refs_5_.refs_15_, f32[2,2560]{1,0:T(2,128)S(1)} %collective-permute-done.18.refs_2_.refs_6_.refs_16_, ...), custom_call_target="tpu_custom_call" | custom-call | flops 100000000 | bytes 100000 | tf_op jit(solution)/shard_map/pallas_call | solution.py:51
  176.7 6.1 %shard_map.282 = (f32[8,368,128]{2,1,0:T(8,128)}, f32[8,376,128]{2,1,0:T(8,128)}, f32[8,368,128]{2,1,0:T(8,128)}, f32[8,376,128]{2,1,0:T(8,128)}, f32[8,368,128]...) custom-call(bf16[896,1024]{1,0:T(8,128)(2,1)S(1)} %copy-done.20, ...), custom_call_target="tpu_custom_call" | custom-call | flops 100000000 | bytes 100000 | tf_op jit(solution)/shard_map/pallas_call | solution.py:51
  183.6 2.8 collective-permute-done.56
  186.5 2.8 add.616.refs_20_
  196.7 2.4 collective-permute-done.50.refs_7_
  203.0 2.6 shard_map.283
  209.8 4.6 %collective-permute-start.55 = (f32[2,256]{1,0:T(2,128)S(1)}, f32[2,256]{1,0:T(2,128)S(1)}, u32[]{:S(2)}, u32[]{:S(2)}) collective-permute-start(f32[2,256]{1,0:T(2,128)S(1)} %add.615.refs_4_), channel_id=1, source_target_pairs={{0,13},{1,12},{2,15},{3,14},{4,9},{5,8},{6,11},{7,10},{8,5},{9,4},... | collective-permute-start | bytes 6152 | tf_op jit(solution)/shard_map/ppermute | solution.py:793
  227.4 4.5 %collective-permute-start.62 = (f32[2,256]{1,0:T(2,128)S(1)}, f32[2,256]{1,0:T(2,128)S(1)}, u32[]{:S(2)}, u32[]{:S(2)}) collective-permute-start(f32[2,256]{1,0:T(2,128)S(1)} %add.619.refs_4_), channel_id=1, source_target_pairs={{0,13},{1,12},{2,15},{3,14},{4,9},{5,8},{6,11},{7,10},{8,5},{9,4},... | collective-permute-start | bytes 6152 | tf_op jit(solution)/shard_map/ppermute | solution.py:793
  233.2 2.6 collective-permute-done.61.refs_6_
  241.1 3.5 shard_map.285
  246.7 10.9 %collective-permute-done.65.refs_3_ = f32[8,376,128]{2,1,0:T(8,128)} collective-permute-done((f32[8,376,128]{2,1,0:T(8,128)}, f32[8,376,128]{2,1,0:T(8,128)}, u32[]{:S(2)}, u32[]{:S(2)}) %collective-permute-start.65) | collective-permute-done | bytes 1540128 | tf_op jit(solution)/shard_map/ppermute | solution.py:793
  257.7 7.1 %collective-permute-done.66.refs_4_ = f32[4,368,128]{2,1,0:T(8,128)S(1)} collective-permute-done((f32[4,368,128]{2,1,0:T(8,128)S(1)}, f32[4,368,128]{2,1,0:T(8,128)S(1)}, u32[]{:S(2)}, u32[]{:S(2)}) %collective-permute-start.66) | collective-permute-done | bytes 753696 | tf_op jit(solution)/shard_map/ppermute | solution.py:793
  264.8 3.3 shard_map.287
  269.5 5.7 %collective-permute-done.76 = f32[8,376,128]{2,1,0:T(8,128)} collective-permute-done((f32[8,376,128]{2,1,0:T(8,128)}, f32[8,376,128]{2,1,0:T(8,128)}, u32[]{:S(2)}, u32[]{:S(2)}) %collective-permute-start.76) | collective-permute-done | bytes 1540128 | tf_op jit(solution)/shard_map/ppermute | solution.py:793
  278.3 2.5 dynamic-slice_add_fusion
  282.4 2.5 collective-permute-start.77
  285.0 4.1 %collective-permute-done.74 = f32[2,368,128]{2,1,0:T(8,128)S(1)} collective-permute-done((f32[2,368,128]{2,1,0:T(8,128)S(1)}, f32[2,368,128]{2,1,0:T(8,128)S(1)}, u32[]{:S(2)}, u32[]{:S(2)}) %collective-permute-start.74) | collective-permute-done | bytes 376864 | tf_op jit(solution)/shard_map/ppermute | solution.py:793
  290.2 2.6 collective-permute-start.75
  292.8 8.8 %collective-permute-done.75 = f32[1,368,128]{2,1,0:T(8,128)S(1)} collective-permute-done((f32[1,368,128]{2,1,0:T(8,128)S(1)}, f32[1,368,128]{2,1,0:T(8,128)S(1)}, u32[]{:S(2)}, u32[]{:S(2)}) %collective-permute-start.75) | collective-permute-done | bytes 188448 | tf_op jit(solution)/shard_map/ppermute | solution.py:793
  306.2 2.8 collective-permute-done.68
  310.3 2.6 collective-permute-start.69
  316.5 3.4 collective-permute-start.79
  320.0 5.6 %collective-permute-done.69 = f32[4,288,128]{2,1,0:T(8,128)S(1)} collective-permute-done((f32[4,288,128]{2,1,0:T(8,128)S(1)}, f32[4,288,128]{2,1,0:T(8,128)S(1)}, u32[]{:S(2)}, u32[]{:S(2)}) %collective-permute-start.69) | collective-permute-done | bytes 589856 | tf_op jit(solution)/shard_map/ppermute | solution.py:793
  329.5 2.7 collective-permute-start.73
  335.5 3.9 %collective-permute-start.71 = (f32[1,288,128]{2,1,0:T(8,128)S(1)}, f32[1,288,128]{2,1,0:T(8,128)S(1)}, u32[]{:S(2)}, u32[]{:S(2)}) collective-permute-start(f32[1,288,128]{2,1,0:T(8,128)S(1)} %fusion.7), channel_id=1, source_target_pairs={{0,8},{1,9},{2,10},{3,11},{4,12},{5,13},{6,14},{7,15},{8,0},{9,1},... | collective-permute-start | bytes 442376 | tf_op jit(solution)/shard_map/ppermute | solution.py:793
  339.5 4.8 %collective-permute-done.71 = f32[1,288,128]{2,1,0:T(8,128)S(1)} collective-permute-done((f32[1,288,128]{2,1,0:T(8,128)S(1)}, f32[1,288,128]{2,1,0:T(8,128)S(1)}, u32[]{:S(2)}, u32[]{:S(2)}) %collective-permute-start.71) | collective-permute-done | bytes 147488 | tf_op jit(solution)/shard_map/ppermute | solution.py:793
  (484 shorter events, 159.9 us)
Async XLA Ops:
  7.2 322.3 %reduce-scatter.2.cloned.1.call-start = ((), (), s32[]{:S(2)}) async-start(), calls=%async_computation.1 | async-start | bytes 12951552 | tf_op jit(solution)/shard_map/reduce_scatter | solution.py:1077
  20.4 5.1 %collective-permute-start.4 = (f32[4,256]{1,0:T(4,128)S(1)}, f32[4,256]{1,0:T(4,128)S(1)}, u32[]{:S(2)}, u32[]{:S(2)}) collective-permute-start(f32[4,256]{1,0:T(4,128)S(1)} %add.595.refs_0_.refs_14_), channel_id=1, source_target_pairs={{0,13},{1,12},{2,15},{3,14},{4,9},{5,8},{6,11},{7,10},{8,5},{9,4},... | collective-permute-start | bytes 12296 | tf_op jit(solution)/shard_map/ppermute | solution.py:793
  37.7 5.4 %collective-permute-start.9 = (f32[2,256]{1,0:T(2,128)S(1)}, f32[2,256]{1,0:T(2,128)S(1)}, u32[]{:S(2)}, u32[]{:S(2)}) collective-permute-start(f32[2,256]{1,0:T(2,128)S(1)} %add.597.refs_0_.refs_14_), channel_id=1, source_target_pairs={{0,13},{1,12},{2,15},{3,14},{4,9},{5,8},{6,11},{7,10},{8,5},{9,4},... | collective-permute-start | bytes 6152 | tf_op jit(solution)/shard_map/ppermute | solution.py:793
  39.1 4.0 %collective-permute-start.8 = (f32[2,256]{1,0:T(2,128)S(1)}, f32[2,256]{1,0:T(2,128)S(1)}, u32[]{:S(2)}, u32[]{:S(2)}) collective-permute-start(f32[2,256]{1,0:T(2,128)S(1)} %add.597.refs_0_.refs_14_), channel_id=1, source_target_pairs={{0,9},{1,8},{2,11},{3,10},{4,13},{5,12},{6,15},{7,14},{8,1},{9,0},... | collective-permute-start | bytes 6152 | tf_op jit(solution)/shard_map/ppermute | solution.py:793
  50.9 5.3 %collective-permute-start.14 = (f32[2,1024]{1,0:T(2,128)S(1)}, f32[2,1024]{1,0:T(2,128)S(1)}, u32[]{:S(2)}, u32[]{:S(2)}) collective-permute-start(f32[2,1024]{1,0:T(2,128)S(1)} %add.599.refs_0_.refs_15_), channel_id=1, source_target_pairs={{0,13},{1,12},{2,15},{3,14},{4,9},{5,8},{6,11},{7,10},{8,5},{9,4},... | collective-permute-start | bytes 24584 | tf_op jit(solution)/shard_map/ppermute | solution.py:793
  52.9 4.0 %collective-permute-start.13 = (f32[2,1024]{1,0:T(2,128)S(1)}, f32[2,1024]{1,0:T(2,128)S(1)}, u32[]{:S(2)}, u32[]{:S(2)}) collective-permute-start(f32[2,1024]{1,0:T(2,128)S(1)} %add.599.refs_0_.refs_15_), channel_id=1, source_target_pairs={{0,9},{1,8},{2,11},{3,10},{4,13},{5,12},{6,15},{7,14},{8,1},{9,0},... | collective-permute-start | bytes 24584 | tf_op jit(solution)/shard_map/ppermute | solution.py:793
  68.8 8.8 %collective-permute-start.19 = (f32[2,2560]{1,0:T(2,128)S(1)}, f32[2,2560]{1,0:T(2,128)S(1)}, u32[]{:S(2)}, u32[]{:S(2)}) collective-permute-start(f32[2,2560]{1,0:T(2,128)S(1)} %add.601.refs_0_.refs_4_.refs_14_), channel_id=1, source_target_pairs={{0,13},{1,12},{2,15},{3,14},{4,9},{5,8},{6,11},{7,10},{8,5},{9,4},... | collective-permute-start | bytes 61448 | tf_op jit(solution)/shard_map/ppermute | solution.py:793
  70.4 7.3 %collective-permute-start.18 = (f32[2,2560]{1,0:T(2,128)S(1)}, f32[2,2560]{1,0:T(2,128)S(1)}, u32[]{:S(2)}, u32[]{:S(2)}) collective-permute-start(f32[2,2560]{1,0:T(2,128)S(1)} %add.601.refs_0_.refs_4_.refs_14_), channel_id=1, source_target_pairs={{0,9},{1,8},{2,11},{3,10},{4,13},{5,12},{6,15},{7,14},{8,1},{9,0},... | collective-permute-start | bytes 61448 | tf_op jit(solution)/shard_map/ppermute | solution.py:793
  71.2 6.4 %collective-permute-start.17 = (f32[2,2560]{1,0:T(2,128)S(1)}, f32[2,2560]{1,0:T(2,128)S(1)}, u32[]{:S(2)}, u32[]{:S(2)}) collective-permute-start(f32[2,2560]{1,0:T(2,128)S(1)} %add.601.refs_0_.refs_4_.refs_14_), channel_id=1, source_target_pairs={{0,5},{1,4},{2,7},{3,6},{4,1},{5,0},{6,3},{7,2},{8,13},{9,12},{10,... | collective-permute-start | bytes 61448 | tf_op jit(solution)/shard_map/ppermute | solution.py:793
  86.6 6.3 %collective-permute-start.24 = (f32[2,512]{1,0:T(2,128)S(1)}, f32[2,512]{1,0:T(2,128)S(1)}, u32[]{:S(2)}, u32[]{:S(2)}) collective-permute-start(f32[2,512]{1,0:T(2,128)S(1)} %add.603.refs_0_.refs_20_), channel_id=1, source_target_pairs={{0,13},{1,12},{2,15},{3,14},{4,9},{5,8},{6,11},{7,10},{8,5},{9,4},... | collective-permute-start | bytes 12296 | tf_op jit(solution)/shard_map/ppermute | solution.py:793
  88.1 4.9 %collective-permute-start.23 = (f32[2,512]{1,0:T(2,128)S(1)}, f32[2,512]{1,0:T(2,128)S(1)}, u32[]{:S(2)}, u32[]{:S(2)}) collective-permute-start(f32[2,512]{1,0:T(2,128)S(1)} %add.603.refs_0_.refs_20_), channel_id=1, source_target_pairs={{0,9},{1,8},{2,11},{3,10},{4,13},{5,12},{6,15},{7,14},{8,1},{9,0},... | collective-permute-start | bytes 12296 | tf_op jit(solution)/shard_map/ppermute | solution.py:793
  88.1 4.9 %collective-permute-start.22 = (f32[2,512]{1,0:T(2,128)S(1)}, f32[2,512]{1,0:T(2,128)S(1)}, u32[]{:S(2)}, u32[]{:S(2)}) collective-permute-start(f32[2,512]{1,0:T(2,128)S(1)} %add.603.refs_0_.refs_20_), channel_id=1, source_target_pairs={{0,5},{1,4},{2,7},{3,6},{4,1},{5,0},{6,3},{7,2},{8,13},{9,12},{10,... | collective-permute-start | bytes 12296 | tf_op jit(solution)/shard_map/ppermute | solution.py:793
  102.7 5.0 %collective-permute-start.29 = (f32[2,2048]{1,0:T(2,128)S(1)}, f32[2,2048]{1,0:T(2,128)S(1)}, u32[]{:S(2)}, u32[]{:S(2)}) collective-permute-start(f32[2,2048]{1,0:T(2,128)S(1)} %add.605.refs_0_), channel_id=1, source_target_pairs={{0,13},{1,12},{2,15},{3,14},{4,9},{5,8},{6,11},{7,10},{8,5},{9,4},... | collective-permute-start | bytes 49160 | tf_op jit(solution)/shard_map/ppermute | solution.py:793
  104.2 4.3 %collective-permute-start.28 = (f32[2,2048]{1,0:T(2,128)S(1)}, f32[2,2048]{1,0:T(2,128)S(1)}, u32[]{:S(2)}, u32[]{:S(2)}) collective-permute-start(f32[2,2048]{1,0:T(2,128)S(1)} %add.605.refs_0_), channel_id=1, source_target_pairs={{0,9},{1,8},{2,11},{3,10},{4,13},{5,12},{6,15},{7,14},{8,1},{9,0},... | collective-permute-start | bytes 49160 | tf_op jit(solution)/shard_map/ppermute | solution.py:793
  104.5 4.1 %collective-permute-start.27 = (f32[2,2048]{1,0:T(2,128)S(1)}, f32[2,2048]{1,0:T(2,128)S(1)}, u32[]{:S(2)}, u32[]{:S(2)}) collective-permute-start(f32[2,2048]{1,0:T(2,128)S(1)} %add.605.refs_0_), channel_id=1, source_target_pairs={{0,5},{1,4},{2,7},{3,6},{4,1},{5,0},{6,3},{7,2},{8,13},{9,12},{10,... | collective-permute-start | bytes 49160 | tf_op jit(solution)/shard_map/ppermute | solution.py:793
  112.1 4.1 %collective-permute-start.30 = (f32[4,2048]{1,0:T(4,128)S(1)}, f32[4,2048]{1,0:T(4,128)S(1)}, u32[]{:S(2)}, u32[]{:S(2)}) collective-permute-start(f32[4,2048]{1,0:T(4,128)S(1)} %get-tuple-element.93.refs_0_), channel_id=1, source_target_pairs={{0,16},{16,0},{1,17},{17,1},{2,18},{18,2},{3,19},{19,3},{4,20},{20... | collective-permute-start | bytes 98312 | tf_op jit(solution)/shard_map/ppermute | solution.py:793
  121.3 5.2 %collective-permute-start.35 = (f32[3,2048]{1,0:T(4,128)S(1)}, f32[3,2048]{1,0:T(4,128)S(1)}, u32[]{:S(2)}, u32[]{:S(2)}) collective-permute-start(f32[3,2048]{1,0:T(4,128)S(1)} %add.607.refs_8_), channel_id=1, source_target_pairs={{0,13},{1,12},{2,15},{3,14},{4,9},{5,8},{6,11},{7,10},{8,5},{9,4},... | collective-permute-start | bytes 73736 | tf_op jit(solution)/shard_map/ppermute | solution.py:793
  123.1 5.2 %collective-permute-start.34 = (f32[3,2048]{1,0:T(4,128)S(1)}, f32[3,2048]{1,0:T(4,128)S(1)}, u32[]{:S(2)}, u32[]{:S(2)}) collective-permute-start(f32[3,2048]{1,0:T(4,128)S(1)} %add.607.refs_8_), channel_id=1, source_target_pairs={{0,9},{1,8},{2,11},{3,10},{4,13},{5,12},{6,15},{7,14},{8,1},{9,0},... | collective-permute-start | bytes 73736 | tf_op jit(solution)/shard_map/ppermute | solution.py:793
  124.0 4.3 %collective-permute-start.33 = (f32[3,2048]{1,0:T(4,128)S(1)}, f32[3,2048]{1,0:T(4,128)S(1)}, u32[]{:S(2)}, u32[]{:S(2)}) collective-permute-start(f32[3,2048]{1,0:T(4,128)S(1)} %add.607.refs_8_), channel_id=1, source_target_pairs={{0,5},{1,4},{2,7},{3,6},{4,1},{5,0},{6,3},{7,2},{8,13},{9,12},{10,... | collective-permute-start | bytes 73736 | tf_op jit(solution)/shard_map/ppermute | solution.py:793
  144.0 9.4 %collective-permute-start.40 = (f32[2,512]{1,0:T(2,128)}, f32[2,512]{1,0:T(2,128)S(1)}, u32[]{:S(2)}, u32[]{:S(2)}) collective-permute-start(f32[2,512]{1,0:T(2,128)} %copy-done.81), channel_id=1, source_target_pairs={{0,13},{1,12},{2,15},{3,14},{4,9},{5,8},{6,11},{7,10},{8,5},{9,4},... | collective-permute-start | bytes 12296 | tf_op jit(solution)/shard_map/ppermute | solution.py:793
  145.6 7.8 %collective-permute-start.39 = (f32[2,512]{1,0:T(2,128)}, f32[2,512]{1,0:T(2,128)S(1)}, u32[]{:S(2)}, u32[]{:S(2)}) collective-permute-start(f32[2,512]{1,0:T(2,128)} %copy-done.81), channel_id=1, source_target_pairs={{0,9},{1,8},{2,11},{3,10},{4,13},{5,12},{6,15},{7,14},{8,1},{9,0},... | collective-permute-start | bytes 12296 | tf_op jit(solution)/shard_map/ppermute | solution.py:793
  145.7 7.6 %collective-permute-start.38 = (f32[2,512]{1,0:T(2,128)}, f32[2,512]{1,0:T(2,128)S(1)}, u32[]{:S(2)}, u32[]{:S(2)}) collective-permute-start(f32[2,512]{1,0:T(2,128)} %copy-done.81), channel_id=1, source_target_pairs={{0,5},{1,4},{2,7},{3,6},{4,1},{5,0},{6,3},{7,2},{8,13},{9,12},{10,... | collective-permute-start | bytes 12296 | tf_op jit(solution)/shard_map/ppermute | solution.py:793
  162.9 4.8 %collective-permute-start.45 = (f32[2,512]{1,0:T(2,128)S(1)}, f32[2,512]{1,0:T(2,128)S(1)}, u32[]{:S(2)}, u32[]{:S(2)}) collective-permute-start(f32[2,512]{1,0:T(2,128)S(1)} %add.611.refs_4_), channel_id=1, source_target_pairs={{0,13},{1,12},{2,15},{3,14},{4,9},{5,8},{6,11},{7,10},{8,5},{9,4},... | collective-permute-start | bytes 12296 | tf_op jit(solution)/shard_map/ppermute | solution.py:793
  164.0 4.2 %collective-permute-start.43 = (f32[2,512]{1,0:T(2,128)S(1)}, f32[2,512]{1,0:T(2,128)S(1)}, u32[]{:S(2)}, u32[]{:S(2)}) collective-permute-start(f32[2,512]{1,0:T(2,128)S(1)} %add.611.refs_4_), channel_id=1, source_target_pairs={{0,5},{1,4},{2,7},{3,6},{4,1},{5,0},{6,3},{7,2},{8,13},{9,12},{10,... | collective-permute-start | bytes 12296 | tf_op jit(solution)/shard_map/ppermute | solution.py:793
  183.1 7.7 %collective-permute-start.57 = (f32[8,376,128]{2,1,0:T(8,128)}, f32[8,376,128]{2,1,0:T(8,128)S(1)}, u32[]{:S(2)}, u32[]{:S(2)}) collective-permute-start(f32[8,376,128]{2,1,0:T(8,128)} %get-tuple-element.123), channel_id=1, source_target_pairs={{0,1},{1,0},{2,3},{3,2},{4,5},{5,4},{6,7},{7,6},{8,9},{9,8},{10,11... | collective-permute-start | bytes 4620296 | tf_op jit(solution)/shard_map/ppermute | solution.py:793
  183.5 52.8 %collective-permute-start.63 = (f32[8,368,128]{2,1,0:T(8,128)}, f32[8,368,128]{2,1,0:T(8,128)}, u32[]{:S(2)}, u32[]{:S(2)}) collective-permute-start(f32[8,368,128]{2,1,0:T(8,128)} %get-tuple-element.127), channel_id=1, source_target_pairs={{0,1},{1,0},{2,3},{3,2},{4,5},{5,4},{6,7},{7,6},{8,9},{9,8},{10,11... | collective-permute-start | bytes 4521992 | tf_op jit(solution)/shard_map/ppermute | solution.py:793
  189.3 47.0 %collective-permute-start.64 = (f32[8,368,128]{2,1,0:T(8,128)}, f32[8,368,128]{2,1,0:T(8,128)}, u32[]{:S(2)}, u32[]{:S(2)}) collective-permute-start(f32[8,368,128]{2,1,0:T(8,128)} %add.616.refs_20_), channel_id=1, source_target_pairs={{0,16},{16,0},{1,17},{17,1},{2,18},{18,2},{3,19},{19,3},{4,20},{20... | collective-permute-start | bytes 4521992 | tf_op jit(solution)/shard_map/ppermute | solution.py:793
  192.2 65.4 %collective-permute-start.65 = (f32[8,376,128]{2,1,0:T(8,128)}, f32[8,376,128]{2,1,0:T(8,128)}, u32[]{:S(2)}, u32[]{:S(2)}) collective-permute-start(f32[8,376,128]{2,1,0:T(8,128)} %add.617.refs_21_), channel_id=1, source_target_pairs={{0,16},{16,0},{1,17},{17,1},{2,18},{18,2},{3,19},{19,3},{4,20},{20... | collective-permute-start | bytes 4620296 | tf_op jit(solution)/shard_map/ppermute | solution.py:793
  193.8 5.4 %collective-permute-start.50 = (f32[2,1024]{1,0:T(2,128)S(1)}, f32[2,1024]{1,0:T(2,128)S(1)}, u32[]{:S(2)}, u32[]{:S(2)}) collective-permute-start(f32[2,1024]{1,0:T(2,128)S(1)} %add.613.refs_6_.refs_4_), channel_id=1, source_target_pairs={{0,13},{1,12},{2,15},{3,14},{4,9},{5,8},{6,11},{7,10},{8,5},{9,4},... | collective-permute-start | bytes 24584 | tf_op jit(solution)/shard_map/ppermute | solution.py:793
  195.8 5.2 %collective-permute-start.49 = (f32[2,1024]{1,0:T(2,128)S(1)}, f32[2,1024]{1,0:T(2,128)S(1)}, u32[]{:S(2)}, u32[]{:S(2)}) collective-permute-start(f32[2,1024]{1,0:T(2,128)S(1)} %add.613.refs_6_.refs_4_), channel_id=1, source_target_pairs={{0,9},{1,8},{2,11},{3,10},{4,13},{5,12},{6,15},{7,14},{8,1},{9,0},... | collective-permute-start | bytes 24584 | tf_op jit(solution)/shard_map/ppermute | solution.py:793
  209.8 6.2 %collective-permute-start.55 = (f32[2,256]{1,0:T(2,128)S(1)}, f32[2,256]{1,0:T(2,128)S(1)}, u32[]{:S(2)}, u32[]{:S(2)}) collective-permute-start(f32[2,256]{1,0:T(2,128)S(1)} %add.615.refs_4_), channel_id=1, source_target_pairs={{0,13},{1,12},{2,15},{3,14},{4,9},{5,8},{6,11},{7,10},{8,5},{9,4},... | collective-permute-start | bytes 6152 | tf_op jit(solution)/shard_map/ppermute | solution.py:793
  214.4 4.2 %collective-permute-start.54 = (f32[2,256]{1,0:T(2,128)S(1)}, f32[2,256]{1,0:T(2,128)S(1)}, u32[]{:S(2)}, u32[]{:S(2)}) collective-permute-start(f32[2,256]{1,0:T(2,128)S(1)} %add.615.refs_4_), channel_id=1, source_target_pairs={{0,9},{1,8},{2,11},{3,10},{4,13},{5,12},{6,15},{7,14},{8,1},{9,0},... | collective-permute-start | bytes 6152 | tf_op jit(solution)/shard_map/ppermute | solution.py:793
  227.4 5.8 %collective-permute-start.62 = (f32[2,256]{1,0:T(2,128)S(1)}, f32[2,256]{1,0:T(2,128)S(1)}, u32[]{:S(2)}, u32[]{:S(2)}) collective-permute-start(f32[2,256]{1,0:T(2,128)S(1)} %add.619.refs_4_), channel_id=1, source_target_pairs={{0,13},{1,12},{2,15},{3,14},{4,9},{5,8},{6,11},{7,10},{8,5},{9,4},... | collective-permute-start | bytes 6152 | tf_op jit(solution)/shard_map/ppermute | solution.py:793
  238.1 26.6 %collective-permute-start.66 = (f32[4,368,128]{2,1,0:T(8,128)S(1)}, f32[4,368,128]{2,1,0:T(8,128)S(1)}, u32[]{:S(2)}, u32[]{:S(2)}) collective-permute-start(f32[4,368,128]{2,1,0:T(8,128)S(1)} %bitcast_add_fusion.1.refs_15_), channel_id=1, source_target_pairs={{0,2},{1,3},{2,0},{3,1},{4,6},{5,7},{6,4},{7,5},{8,10},{9,11},{10,... | collective-permute-start | bytes 2261000 | tf_op jit(solution)/shard_map/ppermute | solution.py:793
  268.0 10.2 %collective-permute-start.67 = (f32[16,288,128]{2,1,0:T(8,128)}, f32[16,288,128]{2,1,0:T(8,128)}, u32[]{:S(2)}, u32[]{:S(2)}) collective-permute-start(f32[16,288,128]{2,1,0:T(8,128)} %get-tuple-element.136), channel_id=1, source_target_pairs={{0,1},{1,0},{2,3},{3,2},{4,5},{5,4},{6,7},{7,6},{8,9},{9,8},{10,11... | collective-permute-start | bytes 7077896 | tf_op jit(solution)/shard_map/ppermute | solution.py:793
  268.1 7.1 %collective-permute-start.76 = (f32[8,376,128]{2,1,0:T(8,128)}, f32[8,376,128]{2,1,0:T(8,128)}, u32[]{:S(2)}, u32[]{:S(2)}) collective-permute-start(f32[8,376,128]{2,1,0:T(8,128)} %get-tuple-element.139), channel_id=1, source_target_pairs={{0,1},{1,0},{2,3},{3,2},{4,5},{5,4},{6,7},{7,6},{8,9},{9,8},{10,11... | collective-permute-start | bytes 4620296 | tf_op jit(solution)/shard_map/ppermute | solution.py:793
  278.2 10.9 %collective-permute-start.74 = (f32[2,368,128]{2,1,0:T(8,128)S(1)}, f32[2,368,128]{2,1,0:T(8,128)S(1)}, u32[]{:S(2)}, u32[]{:S(2)}) collective-permute-start(f32[2,368,128]{2,1,0:T(8,128)S(1)} %bitcast_add_fusion.5), channel_id=1, source_target_pairs={{0,4},{1,5},{2,6},{3,7},{4,0},{5,1},{6,2},{7,3},{8,12},{9,13},{10,... | collective-permute-start | bytes 1130504 | tf_op jit(solution)/shard_map/ppermute | solution.py:793
  280.8 28.3 %collective-permute-start.68 = (f32[8,288,128]{2,1,0:T(8,128)}, f32[8,288,128]{2,1,0:T(8,128)}, u32[]{:S(2)}, u32[]{:S(2)}) collective-permute-start(f32[8,288,128]{2,1,0:T(8,128)} %bitcast.37), channel_id=1, source_target_pairs={{0,16},{16,0},{1,17},{17,1},{2,18},{18,2},{3,19},{19,3},{4,20},{20... | collective-permute-start | bytes 3538952 | tf_op jit(solution)/shard_map/ppermute | solution.py:793
  282.4 21.7 %collective-permute-start.77 = (f32[4,376,128]{2,1,0:T(8,128)}, f32[4,376,128]{2,1,0:T(8,128)}, u32[]{:S(2)}, u32[]{:S(2)}) collective-permute-start(f32[4,376,128]{2,1,0:T(8,128)} %bitcast_add_fusion), channel_id=1, source_target_pairs={{0,2},{1,3},{2,0},{3,1},{4,6},{5,7},{6,4},{7,5},{8,10},{9,11},{10,... | collective-permute-start | bytes 2310152 | tf_op jit(solution)/shard_map/ppermute | solution.py:793
  290.2 11.4 %collective-permute-start.75 = (f32[1,368,128]{2,1,0:T(8,128)S(1)}, f32[1,368,128]{2,1,0:T(8,128)S(1)}, u32[]{:S(2)}, u32[]{:S(2)}) collective-permute-start(f32[1,368,128]{2,1,0:T(8,128)S(1)} %fusion.6), channel_id=1, source_target_pairs={{0,8},{1,9},{2,10},{3,11},{4,12},{5,13},{6,14},{7,15},{8,0},{9,1},... | collective-permute-start | bytes 565256 | tf_op jit(solution)/shard_map/ppermute | solution.py:793
  305.4 9.9 %collective-permute-start.78 = (f32[2,376,128]{2,1,0:T(8,128)S(1)}, f32[2,376,128]{2,1,0:T(8,128)S(1)}, u32[]{:S(2)}, u32[]{:S(2)}) collective-permute-start(f32[2,376,128]{2,1,0:T(8,128)S(1)} %fusion.1), channel_id=1, source_target_pairs={{0,4},{1,5},{2,6},{3,7},{4,0},{5,1},{6,2},{7,3},{8,12},{9,13},{10,... | collective-permute-start | bytes 1155080 | tf_op jit(solution)/shard_map/ppermute | solution.py:793
  310.3 15.3 %collective-permute-start.69 = (f32[4,288,128]{2,1,0:T(8,128)S(1)}, f32[4,288,128]{2,1,0:T(8,128)S(1)}, u32[]{:S(2)}, u32[]{:S(2)}) collective-permute-start(f32[4,288,128]{2,1,0:T(8,128)S(1)} %bitcast_add_fusion.2), channel_id=1, source_target_pairs={{0,2},{1,3},{2,0},{3,1},{4,6},{5,7},{6,4},{7,5},{8,10},{9,11},{10,... | collective-permute-start | bytes 1769480 | tf_op jit(solution)/shard_map/ppermute | solution.py:793
  313.5 6.5 %collective-permute-start.72 = (f32[88,128]{1,0:T(8,128)S(1)}, f32[88,128]{1,0:T(8,128)S(1)}, u32[]{:S(2)}, u32[]{:S(2)}) collective-permute-start(f32[88,128]{1,0:T(8,128)S(1)} %broadcast_add_fusion), channel_id=1, source_target_pairs={{0,16},{16,0},{1,17},{17,1},{2,18},{18,2},{3,19},{19,3},{4,20},{20... | collective-permute-start | bytes 135176 | tf_op jit(solution)/shard_map/ppermute | solution.py:793
  316.5 11.7 %collective-permute-start.79 = (f32[1,376,128]{2,1,0:T(8,128)S(1)}, f32[1,376,128]{2,1,0:T(8,128)S(1)}, u32[]{:S(2)}, u32[]{:S(2)}) collective-permute-start(f32[1,376,128]{2,1,0:T(8,128)S(1)} %fusion.5), channel_id=1, source_target_pairs={{0,8},{1,9},{2,10},{3,11},{4,12},{5,13},{6,14},{7,15},{8,0},{9,1},... | collective-permute-start | bytes 577544 | tf_op jit(solution)/shard_map/ppermute | solution.py:793
  326.8 7.6 %collective-permute-start.70 = (f32[2,288,128]{2,1,0:T(8,128)S(1)}, f32[2,288,128]{2,1,0:T(8,128)S(1)}, u32[]{:S(2)}, u32[]{:S(2)}) collective-permute-start(f32[2,288,128]{2,1,0:T(8,128)S(1)} %fusion.3), channel_id=1, source_target_pairs={{0,4},{1,5},{2,6},{3,7},{4,0},{5,1},{6,2},{7,3},{8,12},{9,13},{10,... | collective-permute-start | bytes 884744 | tf_op jit(solution)/shard_map/ppermute | solution.py:793
  329.5 18.6 %collective-permute-start.73 = (f32[1488,128]{1,0:T(8,128)}, f32[1488,128]{1,0:T(8,128)S(1)}, u32[]{:S(2)}, u32[]{:S(2)}) collective-permute-start(f32[1488,128]{1,0:T(8,128)} %bitcast.199), channel_id=1, source_target_pairs={{0,16},{1,17},{2,18},{3,19},{4,20},{5,21},{6,22},{7,23},{8,24},{9,... | collective-permute-start | bytes 2285576 | tf_op jit(solution)/shard_map/ppermute | solution.py:1177
  332.2 13.9 %collective-permute-start.80 = (f32[744,128]{1,0:T(8,128)S(1)}, f32[744,128]{1,0:T(8,128)S(1)}, u32[]{:S(2)}, u32[]{:S(2)}) collective-permute-start(f32[744,128]{1,0:T(8,128)S(1)} %pad_maximum_fusion.refs_2_), channel_id=1, source_target_pairs={{16,0},{17,1},{18,2},{19,3},{20,4},{21,5},{22,6},{23,7},{24,8},{25... | collective-permute-start | bytes 1142792 | tf_op jit(solution)/shard_map/ppermute | solution.py:1178
  335.5 8.7 %collective-permute-start.71 = (f32[1,288,128]{2,1,0:T(8,128)S(1)}, f32[1,288,128]{2,1,0:T(8,128)S(1)}, u32[]{:S(2)}, u32[]{:S(2)}) collective-permute-start(f32[1,288,128]{2,1,0:T(8,128)S(1)} %fusion.7), channel_id=1, source_target_pairs={{0,8},{1,9},{2,10},{3,11},{4,12},{5,13},{6,14},{7,15},{8,0},{9,1},... | collective-permute-start | bytes 442376 | tf_op jit(solution)/shard_map/ppermute | solution.py:793
  (162 other events, 1599.8 us)
Sparse Core Ops, SparseCore 0:
  144.1 135.9 reduce-scatter.1

commit v4 on v3

--- a/solution.py
+++ b/solution.py
@@ -16,6 +16,7 @@
 cost_small = 0.1
 
 even_width = 8
+spare_rows = 16
 
 
 class View:
@@ -759,8 +760,8 @@
     *outs, store, sems = rest
     copies = Copies(store, outs, sems, 0, 0, share_size, (0,))
     filled = put_filter(store, 0, start_ref, low_ref)
-    later = later_ref.shape[0]
-    store[filled : filled + later, :] = later_ref[...]
+    later = later_ref.shape[0] - spare_rows
+    store[filled : filled + later, :] = later_ref[:later, :]
     filled += later
     store[filled:, :] = jnp.zeros((store.shape[0] - filled, store.shape[1]), full_type)
     copies.finish(store.shape[0])
@@ -1143,7 +1144,7 @@
     end_a = window_start(2 * size - 1, share_a, lanes) + window_a
     later = call(
         block_filter_body,
-        [shaped((total_a - norm_rows_a) - depth_a * middle_a // lanes, lanes)],
+        [shaped(total_a - norm_rows_a - depth_a * middle_a // lanes + spare_rows, lanes)],
         [even_a, moved_a, low_sa, hidden_two_a, low_ea],
         after=(low_ra,),
     )[0]

time: 357 us -> 357 us (level)
  no operation moved by 1% of the time
where the time goes in v4:
time: 357 us; the launch traced here: 356 us
  waiting for transfers between devices  109 us (31%)
  starting transfers between devices  102 us (29%)
  Pallas kernels  76.2 us (21%)
  local copies, waits for them, and re-layouts  28.3 us (8%)
  other arithmetic  24.8 us (7%)
  between operations  15.9 us (4%)
    ppermute x79, waiting for transfers between devices, exchange(): lax.ppermute(value, axis, [(i, i ^ bits) for i in range(lax.axis_size(axi...  107 us
    ppermute x79, starting transfers between devices, exchange(): lax.ppermute(value, axis, [(i, i ^ bits) for i in range(lax.axis_size(axi...  98.1 us
    pallas_call x28, Pallas kernels, call(): pl.pallas_call(run, out_shape=outs, in_specs=[pl.BlockSpec(memory_space=p...  76.2 us
    unnamed x257, local copies, waits for them, and re-layouts  24.3 us
    add x11, other arithmetic, step(): sum([term.part(chosen) for term in self.terms[1:]], self.terms[0].part(ch...  14.6 us
  transfers between devices with their start and end apart: 82, of which 54 were waited for; matrix products, arithmetic and copies ran while one was open for 8% of the time, Pallas kernels for 12%

profile of v4, /device:TPU:0, one launch (start us, length us, event | category | flops | bytes accessed | tf_op | source)
XLA Modules:
  0.0 356.2 jit_solution(3044507602927542710)
XLA Ops:
  10.5 2.9 shard_map.262
  16.4 2.6 collective-permute-start.1
  20.4 3.8 %collective-permute-start.4 = (f32[4,256]{1,0:T(4,128)S(1)}, f32[4,256]{1,0:T(4,128)S(1)}, u32[]{:S(2)}, u32[]{:S(2)}) collective-permute-start(f32[4,256]{1,0:T(4,128)S(1)} %add.595.refs_0_.refs_14_), channel_id=1, source_target_pairs={{0,13},{1,12},{2,15},{3,14},{4,9},{5,8},{6,11},{7,10},{8,5},{9,4},... | collective-permute-start | bytes 12296 | tf_op jit(solution)/shard_map/ppermute | solution.py:794
  25.5 2.6 collective-permute-done.3.refs_2_.refs_16_
  29.4 2.5 shard_map.263
  39.5 2.2 collective-permute-start.7
  43.2 2.7 shard_map.265
  57.0 7.2 %shard_map.267 = (bf16[896,1024]{1,0:T(8,128)(2,1)S(1)}, f32[896,512]{1,0:T(8,128)S(1)}, bf16[224,1024]{1,0:T(8,128)(2,1)S(1)}, f32[224,2048]{1,0:T(8,128)S(1)},...) custom-call(f32[2,1024]{1,0:T(2,128)S(1)} %add.599.refs_0_.refs_15_, ...), custom_call_target="tpu_custom_call" | custom-call | flops 100000000 | bytes 100000 | tf_op jit(solution)/shard_map/pallas_call | solution.py:52
  72.9 4.7 %shard_map.268.refs_10_.refs_20_ = bf16[896,1024]{1,0:T(8,128)(2,1)S(1)} custom-call(f32[2,1024]{1,0:T(2,128)S(1)} %add.599.refs_0_.refs_15_, f32[2,1024]{1,0:T(2,128)S(1)} %collective-permute-done.12.refs_1_.refs_16_, f32[2,1024]{1,0:T(2,128)S(1)} %collective-permute-done.13.refs_2_.refs_17_, f32[2,1024]{1,0:T(2,128)S(1)} %collective-permute-done.14.refs_3_.refs_18_, ...), custom_call_target="tpu_custom_call" | custom-call | flops 100000000 | bytes 100000 | tf_op jit(solution)/shard_map/pallas_call | solution.py:52
  77.7 3.7 %shard_map.269 = (bf16[16,2,32,512]{3,2,1,0:T(8,128)(2,1)S(1)}, bf16[16,2,32,512]{3,2,1,0:T(8,128)(2,1)S(1)}, f32[224,512]{1,0:T(8,128)S(1)}, f32[2,512]{1,0:T(2,128)S(1)}) custom-call(f32[2,2560]{1,0:T(2,128)S(1)} %add.601.refs_0_.refs_4_.refs_14_, f32[2,2560]{1,0:T(2,128)S(1)} %collective-permute-done.17.refs_1_.refs_5_.refs_15_, ...), custom_call_target="tpu_custom_call" | custom-call | flops 100000000 | bytes 100000 | tf_op jit(solution)/shard_map/pallas_call | solution.py:52
  88.1 2.5 collective-permute-start.22
  90.6 2.3 shard_map.270.refs_9_.refs_19_
  94.7 3.4 shard_map.272
  104.5 2.3 collective-permute-start.27
  108.6 3.6 %shard_map.274 = (bf16[7,7,4,2048]{3,2,1,0:T(4,128)(2,1)}, f32[224,2048]{1,0:T(8,128)S(1)}, f32[4,2048]{1,0:T(4,128)S(1)}) custom-call(f32[2,2048]{1,0:T(2,128)S(1)} %add.605.refs_0_, f32[2,2048]{1,0:T(2,128)S(1)} %collective-permute-done.27.refs_1_, f32[2,2048]{1,0:T(2,128)S(1)} %collective-permute-done.28.refs_2_, ...), custom_call_target="tpu_custom_call" | custom-call | flops 100000000 | bytes 100000 | tf_op jit(solution)/shard_map/pallas_call | solution.py:52
  113.7 2.6 shard_map.275
  128.3 2.4 shard_map.277
  135.7 6.4 %shard_map.278 = (f32[16,1488,128]{2,1,0:T(8,128)}, f32[1072,128]{1,0:T(8,128)S(1)}) custom-call(bf16[224,512]{1,0:T(8,128)(2,1)S(1)} %get-tuple-element.105.refs_0_, bf16[224,1024]{1,0:T(8,128)(2,1)S(1)} %get-tuple-element.106.refs_1_, bf16[224,2048]{1,0:T(8,128)(2,1)S(1)} %get-tuple-element.107.refs_2_, ...), custom_call_target="tpu_custom_call" | custom-call | flops 100000000 | bytes 100000 | tf_op jit(solution)/shard_map/pallas_call | solution.py:52
  145.7 2.2 collective-permute-start.38
  147.9 2.6 copy-done.4
  153.8 3.0 copy-done.2
  164.0 2.9 collective-permute-start.43
  168.3 4.1 %shard_map.281 = (bf16[896,512]{1,0:T(8,128)(2,1)S(1)}, f32[896,1024]{1,0:T(8,128)S(1)}, f32[2,1024]{1,0:T(2,128)S(1)}) custom-call(f32[2,2560]{1,0:T(2,128)S(1)} %add.601.refs_0_.refs_4_.refs_14_, f32[2,2560]{1,0:T(2,128)S(1)} %collective-permute-done.17.refs_1_.refs_5_.refs_15_, f32[2,2560]{1,0:T(2,128)S(1)} %collective-permute-done.18.refs_2_.refs_6_.refs_16_, ...), custom_call_target="tpu_custom_call" | custom-call | flops 100000000 | bytes 100000 | tf_op jit(solution)/shard_map/pallas_call | solution.py:52
  176.7 6.1 %shard_map.282 = (f32[8,368,128]{2,1,0:T(8,128)}, f32[8,376,128]{2,1,0:T(8,128)}, f32[8,368,128]{2,1,0:T(8,128)}, f32[8,376,128]{2,1,0:T(8,128)}, f32[8,368,128]...) custom-call(bf16[896,1024]{1,0:T(8,128)(2,1)S(1)} %copy-done.20, ...), custom_call_target="tpu_custom_call" | custom-call | flops 100000000 | bytes 100000 | tf_op jit(solution)/shard_map/pallas_call | solution.py:52
  183.6 2.8 collective-permute-done.56
  186.5 2.8 add.616.refs_20_
  196.7 2.4 collective-permute-done.50.refs_7_
  203.0 2.6 shard_map.283
  209.8 4.6 %collective-permute-start.55 = (f32[2,256]{1,0:T(2,128)S(1)}, f32[2,256]{1,0:T(2,128)S(1)}, u32[]{:S(2)}, u32[]{:S(2)}) collective-permute-start(f32[2,256]{1,0:T(2,128)S(1)} %add.615.refs_4_), channel_id=1, source_target_pairs={{0,13},{1,12},{2,15},{3,14},{4,9},{5,8},{6,11},{7,10},{8,5},{9,4},... | collective-permute-start | bytes 6152 | tf_op jit(solution)/shard_map/ppermute | solution.py:794
  227.4 4.5 %collective-permute-start.62 = (f32[2,256]{1,0:T(2,128)S(1)}, f32[2,256]{1,0:T(2,128)S(1)}, u32[]{:S(2)}, u32[]{:S(2)}) collective-permute-start(f32[2,256]{1,0:T(2,128)S(1)} %add.619.refs_4_), channel_id=1, source_target_pairs={{0,13},{1,12},{2,15},{3,14},{4,9},{5,8},{6,11},{7,10},{8,5},{9,4},... | collective-permute-start | bytes 6152 | tf_op jit(solution)/shard_map/ppermute | solution.py:794
  233.2 2.6 collective-permute-done.61.refs_6_
  241.1 3.5 shard_map.285
  246.7 10.9 %collective-permute-done.65.refs_3_ = f32[8,376,128]{2,1,0:T(8,128)} collective-permute-done((f32[8,376,128]{2,1,0:T(8,128)}, f32[8,376,128]{2,1,0:T(8,128)}, u32[]{:S(2)}, u32[]{:S(2)}) %collective-permute-start.65) | collective-permute-done | bytes 1540128 | tf_op jit(solution)/shard_map/ppermute | solution.py:794
  257.7 7.1 %collective-permute-done.66.refs_4_ = f32[4,368,128]{2,1,0:T(8,128)S(1)} collective-permute-done((f32[4,368,128]{2,1,0:T(8,128)S(1)}, f32[4,368,128]{2,1,0:T(8,128)S(1)}, u32[]{:S(2)}, u32[]{:S(2)}) %collective-permute-start.66) | collective-permute-done | bytes 753696 | tf_op jit(solution)/shard_map/ppermute | solution.py:794
  264.8 3.3 shard_map.287
  269.5 5.7 %collective-permute-done.76 = f32[8,376,128]{2,1,0:T(8,128)} collective-permute-done((f32[8,376,128]{2,1,0:T(8,128)}, f32[8,376,128]{2,1,0:T(8,128)}, u32[]{:S(2)}, u32[]{:S(2)}) %collective-permute-start.76) | collective-permute-done | bytes 1540128 | tf_op jit(solution)/shard_map/ppermute | solution.py:794
  278.3 2.5 dynamic-slice_add_fusion
  282.4 2.5 collective-permute-start.77
  285.0 4.1 %collective-permute-done.74 = f32[2,368,128]{2,1,0:T(8,128)S(1)} collective-permute-done((f32[2,368,128]{2,1,0:T(8,128)S(1)}, f32[2,368,128]{2,1,0:T(8,128)S(1)}, u32[]{:S(2)}, u32[]{:S(2)}) %collective-permute-start.74) | collective-permute-done | bytes 376864 | tf_op jit(solution)/shard_map/ppermute | solution.py:794
  290.2 2.6 collective-permute-start.75
  292.8 8.8 %collective-permute-done.75 = f32[1,368,128]{2,1,0:T(8,128)S(1)} collective-permute-done((f32[1,368,128]{2,1,0:T(8,128)S(1)}, f32[1,368,128]{2,1,0:T(8,128)S(1)}, u32[]{:S(2)}, u32[]{:S(2)}) %collective-permute-start.75) | collective-permute-done | bytes 188448 | tf_op jit(solution)/shard_map/ppermute | solution.py:794
  306.2 2.9 collective-permute-done.68
  310.3 2.6 collective-permute-start.69
  316.5 3.4 collective-permute-start.79
  320.0 5.6 %collective-permute-done.69 = f32[4,288,128]{2,1,0:T(8,128)S(1)} collective-permute-done((f32[4,288,128]{2,1,0:T(8,128)S(1)}, f32[4,288,128]{2,1,0:T(8,128)S(1)}, u32[]{:S(2)}, u32[]{:S(2)}) %collective-permute-start.69) | collective-permute-done | bytes 589856 | tf_op jit(solution)/shard_map/ppermute | solution.py:794
  329.5 2.7 collective-permute-start.73
  335.5 3.9 %collective-permute-start.71 = (f32[1,288,128]{2,1,0:T(8,128)S(1)}, f32[1,288,128]{2,1,0:T(8,128)S(1)}, u32[]{:S(2)}, u32[]{:S(2)}) collective-permute-start(f32[1,288,128]{2,1,0:T(8,128)S(1)} %fusion.7), channel_id=1, source_target_pairs={{0,8},{1,9},{2,10},{3,11},{4,12},{5,13},{6,14},{7,15},{8,0},{9,1},... | collective-permute-start | bytes 442376 | tf_op jit(solution)/shard_map/ppermute | solution.py:794
  339.5 4.8 %collective-permute-done.71 = f32[1,288,128]{2,1,0:T(8,128)S(1)} collective-permute-done((f32[1,288,128]{2,1,0:T(8,128)S(1)}, f32[1,288,128]{2,1,0:T(8,128)S(1)}, u32[]{:S(2)}, u32[]{:S(2)}) %collective-permute-start.71) | collective-permute-done | bytes 147488 | tf_op jit(solution)/shard_map/ppermute | solution.py:794
  (484 shorter events, 159.9 us)
Async XLA Ops:
  7.2 322.3 %reduce-scatter.2.cloned.1.call-start = ((), (), s32[]{:S(2)}) async-start(), calls=%async_computation.1 | async-start | bytes 12951552 | tf_op jit(solution)/shard_map/reduce_scatter | solution.py:1078
  20.4 5.1 %collective-permute-start.4 = (f32[4,256]{1,0:T(4,128)S(1)}, f32[4,256]{1,0:T(4,128)S(1)}, u32[]{:S(2)}, u32[]{:S(2)}) collective-permute-start(f32[4,256]{1,0:T(4,128)S(1)} %add.595.refs_0_.refs_14_), channel_id=1, source_target_pairs={{0,13},{1,12},{2,15},{3,14},{4,9},{5,8},{6,11},{7,10},{8,5},{9,4},... | collective-permute-start | bytes 12296 | tf_op jit(solution)/shard_map/ppermute | solution.py:794
  37.7 5.4 %collective-permute-start.9 = (f32[2,256]{1,0:T(2,128)S(1)}, f32[2,256]{1,0:T(2,128)S(1)}, u32[]{:S(2)}, u32[]{:S(2)}) collective-permute-start(f32[2,256]{1,0:T(2,128)S(1)} %add.597.refs_0_.refs_14_), channel_id=1, source_target_pairs={{0,13},{1,12},{2,15},{3,14},{4,9},{5,8},{6,11},{7,10},{8,5},{9,4},... | collective-permute-start | bytes 6152 | tf_op jit(solution)/shard_map/ppermute | solution.py:794
  39.1 4.0 %collective-permute-start.8 = (f32[2,256]{1,0:T(2,128)S(1)}, f32[2,256]{1,0:T(2,128)S(1)}, u32[]{:S(2)}, u32[]{:S(2)}) collective-permute-start(f32[2,256]{1,0:T(2,128)S(1)} %add.597.refs_0_.refs_14_), channel_id=1, source_target_pairs={{0,9},{1,8},{2,11},{3,10},{4,13},{5,12},{6,15},{7,14},{8,1},{9,0},... | collective-permute-start | bytes 6152 | tf_op jit(solution)/shard_map/ppermute | solution.py:794
  50.9 5.3 %collective-permute-start.14 = (f32[2,1024]{1,0:T(2,128)S(1)}, f32[2,1024]{1,0:T(2,128)S(1)}, u32[]{:S(2)}, u32[]{:S(2)}) collective-permute-start(f32[2,1024]{1,0:T(2,128)S(1)} %add.599.refs_0_.refs_15_), channel_id=1, source_target_pairs={{0,13},{1,12},{2,15},{3,14},{4,9},{5,8},{6,11},{7,10},{8,5},{9,4},... | collective-permute-start | bytes 24584 | tf_op jit(solution)/shard_map/ppermute | solution.py:794
  52.9 4.0 %collective-permute-start.13 = (f32[2,1024]{1,0:T(2,128)S(1)}, f32[2,1024]{1,0:T(2,128)S(1)}, u32[]{:S(2)}, u32[]{:S(2)}) collective-permute-start(f32[2,1024]{1,0:T(2,128)S(1)} %add.599.refs_0_.refs_15_), channel_id=1, source_target_pairs={{0,9},{1,8},{2,11},{3,10},{4,13},{5,12},{6,15},{7,14},{8,1},{9,0},... | collective-permute-start | bytes 24584 | tf_op jit(solution)/shard_map/ppermute | solution.py:794
  68.8 8.8 %collective-permute-start.19 = (f32[2,2560]{1,0:T(2,128)S(1)}, f32[2,2560]{1,0:T(2,128)S(1)}, u32[]{:S(2)}, u32[]{:S(2)}) collective-permute-start(f32[2,2560]{1,0:T(2,128)S(1)} %add.601.refs_0_.refs_4_.refs_14_), channel_id=1, source_target_pairs={{0,13},{1,12},{2,15},{3,14},{4,9},{5,8},{6,11},{7,10},{8,5},{9,4},... | collective-permute-start | bytes 61448 | tf_op jit(solution)/shard_map/ppermute | solution.py:794
  70.4 7.3 %collective-permute-start.18 = (f32[2,2560]{1,0:T(2,128)S(1)}, f32[2,2560]{1,0:T(2,128)S(1)}, u32[]{:S(2)}, u32[]{:S(2)}) collective-permute-start(f32[2,2560]{1,0:T(2,128)S(1)} %add.601.refs_0_.refs_4_.refs_14_), channel_id=1, source_target_pairs={{0,9},{1,8},{2,11},{3,10},{4,13},{5,12},{6,15},{7,14},{8,1},{9,0},... | collective-permute-start | bytes 61448 | tf_op jit(solution)/shard_map/ppermute | solution.py:794
  71.2 6.4 %collective-permute-start.17 = (f32[2,2560]{1,0:T(2,128)S(1)}, f32[2,2560]{1,0:T(2,128)S(1)}, u32[]{:S(2)}, u32[]{:S(2)}) collective-permute-start(f32[2,2560]{1,0:T(2,128)S(1)} %add.601.refs_0_.refs_4_.refs_14_), channel_id=1, source_target_pairs={{0,5},{1,4},{2,7},{3,6},{4,1},{5,0},{6,3},{7,2},{8,13},{9,12},{10,... | collective-permute-start | bytes 61448 | tf_op jit(solution)/shard_map/ppermute | solution.py:794
  86.6 6.3 %collective-permute-start.24 = (f32[2,512]{1,0:T(2,128)S(1)}, f32[2,512]{1,0:T(2,128)S(1)}, u32[]{:S(2)}, u32[]{:S(2)}) collective-permute-start(f32[2,512]{1,0:T(2,128)S(1)} %add.603.refs_0_.refs_20_), channel_id=1, source_target_pairs={{0,13},{1,12},{2,15},{3,14},{4,9},{5,8},{6,11},{7,10},{8,5},{9,4},... | collective-permute-start | bytes 12296 | tf_op jit(solution)/shard_map/ppermute | solution.py:794
  88.1 4.9 %collective-permute-start.23 = (f32[2,512]{1,0:T(2,128)S(1)}, f32[2,512]{1,0:T(2,128)S(1)}, u32[]{:S(2)}, u32[]{:S(2)}) collective-permute-start(f32[2,512]{1,0:T(2,128)S(1)} %add.603.refs_0_.refs_20_), channel_id=1, source_target_pairs={{0,9},{1,8},{2,11},{3,10},{4,13},{5,12},{6,15},{7,14},{8,1},{9,0},... | collective-permute-start | bytes 12296 | tf_op jit(solution)/shard_map/ppermute | solution.py:794
  88.1 4.9 %collective-permute-start.22 = (f32[2,512]{1,0:T(2,128)S(1)}, f32[2,512]{1,0:T(2,128)S(1)}, u32[]{:S(2)}, u32[]{:S(2)}) collective-permute-start(f32[2,512]{1,0:T(2,128)S(1)} %add.603.refs_0_.refs_20_), channel_id=1, source_target_pairs={{0,5},{1,4},{2,7},{3,6},{4,1},{5,0},{6,3},{7,2},{8,13},{9,12},{10,... | collective-permute-start | bytes 12296 | tf_op jit(solution)/shard_map/ppermute | solution.py:794
  102.7 5.0 %collective-permute-start.29 = (f32[2,2048]{1,0:T(2,128)S(1)}, f32[2,2048]{1,0:T(2,128)S(1)}, u32[]{:S(2)}, u32[]{:S(2)}) collective-permute-start(f32[2,2048]{1,0:T(2,128)S(1)} %add.605.refs_0_), channel_id=1, source_target_pairs={{0,13},{1,12},{2,15},{3,14},{4,9},{5,8},{6,11},{7,10},{8,5},{9,4},... | collective-permute-start | bytes 49160 | tf_op jit(solution)/shard_map/ppermute | solution.py:794
  104.2 4.3 %collective-permute-start.28 = (f32[2,2048]{1,0:T(2,128)S(1)}, f32[2,2048]{1,0:T(2,128)S(1)}, u32[]{:S(2)}, u32[]{:S(2)}) collective-permute-start(f32[2,2048]{1,0:T(2,128)S(1)} %add.605.refs_0_), channel_id=1, source_target_pairs={{0,9},{1,8},{2,11},{3,10},{4,13},{5,12},{6,15},{7,14},{8,1},{9,0},... | collective-permute-start | bytes 49160 | tf_op jit(solution)/shard_map/ppermute | solution.py:794
  104.5 4.1 %collective-permute-start.27 = (f32[2,2048]{1,0:T(2,128)S(1)}, f32[2,2048]{1,0:T(2,128)S(1)}, u32[]{:S(2)}, u32[]{:S(2)}) collective-permute-start(f32[2,2048]{1,0:T(2,128)S(1)} %add.605.refs_0_), channel_id=1, source_target_pairs={{0,5},{1,4},{2,7},{3,6},{4,1},{5,0},{6,3},{7,2},{8,13},{9,12},{10,... | collective-permute-start | bytes 49160 | tf_op jit(solution)/shard_map/ppermute | solution.py:794
  112.1 4.1 %collective-permute-start.30 = (f32[4,2048]{1,0:T(4,128)S(1)}, f32[4,2048]{1,0:T(4,128)S(1)}, u32[]{:S(2)}, u32[]{:S(2)}) collective-permute-start(f32[4,2048]{1,0:T(4,128)S(1)} %get-tuple-element.93.refs_0_), channel_id=1, source_target_pairs={{0,16},{16,0},{1,17},{17,1},{2,18},{18,2},{3,19},{19,3},{4,20},{20... | collective-permute-start | bytes 98312 | tf_op jit(solution)/shard_map/ppermute | solution.py:794
  121.3 5.2 %collective-permute-start.35 = (f32[3,2048]{1,0:T(4,128)S(1)}, f32[3,2048]{1,0:T(4,128)S(1)}, u32[]{:S(2)}, u32[]{:S(2)}) collective-permute-start(f32[3,2048]{1,0:T(4,128)S(1)} %add.607.refs_8_), channel_id=1, source_target_pairs={{0,13},{1,12},{2,15},{3,14},{4,9},{5,8},{6,11},{7,10},{8,5},{9,4},... | collective-permute-start | bytes 73736 | tf_op jit(solution)/shard_map/ppermute | solution.py:794
  123.1 5.2 %collective-permute-start.34 = (f32[3,2048]{1,0:T(4,128)S(1)}, f32[3,2048]{1,0:T(4,128)S(1)}, u32[]{:S(2)}, u32[]{:S(2)}) collective-permute-start(f32[3,2048]{1,0:T(4,128)S(1)} %add.607.refs_8_), channel_id=1, source_target_pairs={{0,9},{1,8},{2,11},{3,10},{4,13},{5,12},{6,15},{7,14},{8,1},{9,0},... | collective-permute-start | bytes 73736 | tf_op jit(solution)/shard_map/ppermute | solution.py:794
  124.0 4.3 %collective-permute-start.33 = (f32[3,2048]{1,0:T(4,128)S(1)}, f32[3,2048]{1,0:T(4,128)S(1)}, u32[]{:S(2)}, u32[]{:S(2)}) collective-permute-start(f32[3,2048]{1,0:T(4,128)S(1)} %add.607.refs_8_), channel_id=1, source_target_pairs={{0,5},{1,4},{2,7},{3,6},{4,1},{5,0},{6,3},{7,2},{8,13},{9,12},{10,... | collective-permute-start | bytes 73736 | tf_op jit(solution)/shard_map/ppermute | solution.py:794
  144.0 9.4 %collective-permute-start.40 = (f32[2,512]{1,0:T(2,128)}, f32[2,512]{1,0:T(2,128)S(1)}, u32[]{:S(2)}, u32[]{:S(2)}) collective-permute-start(f32[2,512]{1,0:T(2,128)} %copy-done.81), channel_id=1, source_target_pairs={{0,13},{1,12},{2,15},{3,14},{4,9},{5,8},{6,11},{7,10},{8,5},{9,4},... | collective-permute-start | bytes 12296 | tf_op jit(solution)/shard_map/ppermute | solution.py:794
  145.6 7.8 %collective-permute-start.39 = (f32[2,512]{1,0:T(2,128)}, f32[2,512]{1,0:T(2,128)S(1)}, u32[]{:S(2)}, u32[]{:S(2)}) collective-permute-start(f32[2,512]{1,0:T(2,128)} %copy-done.81), channel_id=1, source_target_pairs={{0,9},{1,8},{2,11},{3,10},{4,13},{5,12},{6,15},{7,14},{8,1},{9,0},... | collective-permute-start | bytes 12296 | tf_op jit(solution)/shard_map/ppermute | solution.py:794
  145.7 7.6 %collective-permute-start.38 = (f32[2,512]{1,0:T(2,128)}, f32[2,512]{1,0:T(2,128)S(1)}, u32[]{:S(2)}, u32[]{:S(2)}) collective-permute-start(f32[2,512]{1,0:T(2,128)} %copy-done.81), channel_id=1, source_target_pairs={{0,5},{1,4},{2,7},{3,6},{4,1},{5,0},{6,3},{7,2},{8,13},{9,12},{10,... | collective-permute-start | bytes 12296 | tf_op jit(solution)/shard_map/ppermute | solution.py:794
  162.9 4.8 %collective-permute-start.45 = (f32[2,512]{1,0:T(2,128)S(1)}, f32[2,512]{1,0:T(2,128)S(1)}, u32[]{:S(2)}, u32[]{:S(2)}) collective-permute-start(f32[2,512]{1,0:T(2,128)S(1)} %add.611.refs_4_), channel_id=1, source_target_pairs={{0,13},{1,12},{2,15},{3,14},{4,9},{5,8},{6,11},{7,10},{8,5},{9,4},... | collective-permute-start | bytes 12296 | tf_op jit(solution)/shard_map/ppermute | solution.py:794
  164.0 4.2 %collective-permute-start.43 = (f32[2,512]{1,0:T(2,128)S(1)}, f32[2,512]{1,0:T(2,128)S(1)}, u32[]{:S(2)}, u32[]{:S(2)}) collective-permute-start(f32[2,512]{1,0:T(2,128)S(1)} %add.611.refs_4_), channel_id=1, source_target_pairs={{0,5},{1,4},{2,7},{3,6},{4,1},{5,0},{6,3},{7,2},{8,13},{9,12},{10,... | collective-permute-start | bytes 12296 | tf_op jit(solution)/shard_map/ppermute | solution.py:794
  183.1 7.7 %collective-permute-start.57 = (f32[8,376,128]{2,1,0:T(8,128)}, f32[8,376,128]{2,1,0:T(8,128)S(1)}, u32[]{:S(2)}, u32[]{:S(2)}) collective-permute-start(f32[8,376,128]{2,1,0:T(8,128)} %get-tuple-element.123), channel_id=1, source_target_pairs={{0,1},{1,0},{2,3},{3,2},{4,5},{5,4},{6,7},{7,6},{8,9},{9,8},{10,11... | collective-permute-start | bytes 4620296 | tf_op jit(solution)/shard_map/ppermute | solution.py:794
  183.5 52.8 %collective-permute-start.63 = (f32[8,368,128]{2,1,0:T(8,128)}, f32[8,368,128]{2,1,0:T(8,128)}, u32[]{:S(2)}, u32[]{:S(2)}) collective-permute-start(f32[8,368,128]{2,1,0:T(8,128)} %get-tuple-element.127), channel_id=1, source_target_pairs={{0,1},{1,0},{2,3},{3,2},{4,5},{5,4},{6,7},{7,6},{8,9},{9,8},{10,11... | collective-permute-start | bytes 4521992 | tf_op jit(solution)/shard_map/ppermute | solution.py:794
  189.3 47.0 %collective-permute-start.64 = (f32[8,368,128]{2,1,0:T(8,128)}, f32[8,368,128]{2,1,0:T(8,128)}, u32[]{:S(2)}, u32[]{:S(2)}) collective-permute-start(f32[8,368,128]{2,1,0:T(8,128)} %add.616.refs_20_), channel_id=1, source_target_pairs={{0,16},{16,0},{1,17},{17,1},{2,18},{18,2},{3,19},{19,3},{4,20},{20... | collective-permute-start | bytes 4521992 | tf_op jit(solution)/shard_map/ppermute | solution.py:794
  192.2 65.4 %collective-permute-start.65 = (f32[8,376,128]{2,1,0:T(8,128)}, f32[8,376,128]{2,1,0:T(8,128)}, u32[]{:S(2)}, u32[]{:S(2)}) collective-permute-start(f32[8,376,128]{2,1,0:T(8,128)} %add.617.refs_21_), channel_id=1, source_target_pairs={{0,16},{16,0},{1,17},{17,1},{2,18},{18,2},{3,19},{19,3},{4,20},{20... | collective-permute-start | bytes 4620296 | tf_op jit(solution)/shard_map/ppermute | solution.py:794
  193.8 5.4 %collective-permute-start.50 = (f32[2,1024]{1,0:T(2,128)S(1)}, f32[2,1024]{1,0:T(2,128)S(1)}, u32[]{:S(2)}, u32[]{:S(2)}) collective-permute-start(f32[2,1024]{1,0:T(2,128)S(1)} %add.613.refs_6_.refs_4_), channel_id=1, source_target_pairs={{0,13},{1,12},{2,15},{3,14},{4,9},{5,8},{6,11},{7,10},{8,5},{9,4},... | collective-permute-start | bytes 24584 | tf_op jit(solution)/shard_map/ppermute | solution.py:794
  195.8 5.2 %collective-permute-start.49 = (f32[2,1024]{1,0:T(2,128)S(1)}, f32[2,1024]{1,0:T(2,128)S(1)}, u32[]{:S(2)}, u32[]{:S(2)}) collective-permute-start(f32[2,1024]{1,0:T(2,128)S(1)} %add.613.refs_6_.refs_4_), channel_id=1, source_target_pairs={{0,9},{1,8},{2,11},{3,10},{4,13},{5,12},{6,15},{7,14},{8,1},{9,0},... | collective-permute-start | bytes 24584 | tf_op jit(solution)/shard_map/ppermute | solution.py:794
  209.8 6.2 %collective-permute-start.55 = (f32[2,256]{1,0:T(2,128)S(1)}, f32[2,256]{1,0:T(2,128)S(1)}, u32[]{:S(2)}, u32[]{:S(2)}) collective-permute-start(f32[2,256]{1,0:T(2,128)S(1)} %add.615.refs_4_), channel_id=1, source_target_pairs={{0,13},{1,12},{2,15},{3,14},{4,9},{5,8},{6,11},{7,10},{8,5},{9,4},... | collective-permute-start | bytes 6152 | tf_op jit(solution)/shard_map/ppermute | solution.py:794
  214.4 4.2 %collective-permute-start.54 = (f32[2,256]{1,0:T(2,128)S(1)}, f32[2,256]{1,0:T(2,128)S(1)}, u32[]{:S(2)}, u32[]{:S(2)}) collective-permute-start(f32[2,256]{1,0:T(2,128)S(1)} %add.615.refs_4_), channel_id=1, source_target_pairs={{0,9},{1,8},{2,11},{3,10},{4,13},{5,12},{6,15},{7,14},{8,1},{9,0},... | collective-permute-start | bytes 6152 | tf_op jit(solution)/shard_map/ppermute | solution.py:794
  227.4 5.8 %collective-permute-start.62 = (f32[2,256]{1,0:T(2,128)S(1)}, f32[2,256]{1,0:T(2,128)S(1)}, u32[]{:S(2)}, u32[]{:S(2)}) collective-permute-start(f32[2,256]{1,0:T(2,128)S(1)} %add.619.refs_4_), channel_id=1, source_target_pairs={{0,13},{1,12},{2,15},{3,14},{4,9},{5,8},{6,11},{7,10},{8,5},{9,4},... | collective-permute-start | bytes 6152 | tf_op jit(solution)/shard_map/ppermute | solution.py:794
  238.1 26.6 %collective-permute-start.66 = (f32[4,368,128]{2,1,0:T(8,128)S(1)}, f32[4,368,128]{2,1,0:T(8,128)S(1)}, u32[]{:S(2)}, u32[]{:S(2)}) collective-permute-start(f32[4,368,128]{2,1,0:T(8,128)S(1)} %bitcast_add_fusion.1.refs_15_), channel_id=1, source_target_pairs={{0,2},{1,3},{2,0},{3,1},{4,6},{5,7},{6,4},{7,5},{8,10},{9,11},{10,... | collective-permute-start | bytes 2261000 | tf_op jit(solution)/shard_map/ppermute | solution.py:794
  268.1 10.2 %collective-permute-start.67 = (f32[16,288,128]{2,1,0:T(8,128)}, f32[16,288,128]{2,1,0:T(8,128)}, u32[]{:S(2)}, u32[]{:S(2)}) collective-permute-start(f32[16,288,128]{2,1,0:T(8,128)} %get-tuple-element.136), channel_id=1, source_target_pairs={{0,1},{1,0},{2,3},{3,2},{4,5},{5,4},{6,7},{7,6},{8,9},{9,8},{10,11... | collective-permute-start | bytes 7077896 | tf_op jit(solution)/shard_map/ppermute | solution.py:794
  268.1 7.1 %collective-permute-start.76 = (f32[8,376,128]{2,1,0:T(8,128)}, f32[8,376,128]{2,1,0:T(8,128)}, u32[]{:S(2)}, u32[]{:S(2)}) collective-permute-start(f32[8,376,128]{2,1,0:T(8,128)} %get-tuple-element.139), channel_id=1, source_target_pairs={{0,1},{1,0},{2,3},{3,2},{4,5},{5,4},{6,7},{7,6},{8,9},{9,8},{10,11... | collective-permute-start | bytes 4620296 | tf_op jit(solution)/shard_map/ppermute | solution.py:794
  278.2 10.9 %collective-permute-start.74 = (f32[2,368,128]{2,1,0:T(8,128)S(1)}, f32[2,368,128]{2,1,0:T(8,128)S(1)}, u32[]{:S(2)}, u32[]{:S(2)}) collective-permute-start(f32[2,368,128]{2,1,0:T(8,128)S(1)} %bitcast_add_fusion.5), channel_id=1, source_target_pairs={{0,4},{1,5},{2,6},{3,7},{4,0},{5,1},{6,2},{7,3},{8,12},{9,13},{10,... | collective-permute-start | bytes 1130504 | tf_op jit(solution)/shard_map/ppermute | solution.py:794
  280.8 28.3 %collective-permute-start.68 = (f32[8,288,128]{2,1,0:T(8,128)}, f32[8,288,128]{2,1,0:T(8,128)}, u32[]{:S(2)}, u32[]{:S(2)}) collective-permute-start(f32[8,288,128]{2,1,0:T(8,128)} %bitcast.37), channel_id=1, source_target_pairs={{0,16},{16,0},{1,17},{17,1},{2,18},{18,2},{3,19},{19,3},{4,20},{20... | collective-permute-start | bytes 3538952 | tf_op jit(solution)/shard_map/ppermute | solution.py:794
  282.4 21.7 %collective-permute-start.77 = (f32[4,376,128]{2,1,0:T(8,128)}, f32[4,376,128]{2,1,0:T(8,128)}, u32[]{:S(2)}, u32[]{:S(2)}) collective-permute-start(f32[4,376,128]{2,1,0:T(8,128)} %bitcast_add_fusion), channel_id=1, source_target_pairs={{0,2},{1,3},{2,0},{3,1},{4,6},{5,7},{6,4},{7,5},{8,10},{9,11},{10,... | collective-permute-start | bytes 2310152 | tf_op jit(solution)/shard_map/ppermute | solution.py:794
  290.2 11.4 %collective-permute-start.75 = (f32[1,368,128]{2,1,0:T(8,128)S(1)}, f32[1,368,128]{2,1,0:T(8,128)S(1)}, u32[]{:S(2)}, u32[]{:S(2)}) collective-permute-start(f32[1,368,128]{2,1,0:T(8,128)S(1)} %fusion.6), channel_id=1, source_target_pairs={{0,8},{1,9},{2,10},{3,11},{4,12},{5,13},{6,14},{7,15},{8,0},{9,1},... | collective-permute-start | bytes 565256 | tf_op jit(solution)/shard_map/ppermute | solution.py:794
  305.4 9.9 %collective-permute-start.78 = (f32[2,376,128]{2,1,0:T(8,128)S(1)}, f32[2,376,128]{2,1,0:T(8,128)S(1)}, u32[]{:S(2)}, u32[]{:S(2)}) collective-permute-start(f32[2,376,128]{2,1,0:T(8,128)S(1)} %fusion.1), channel_id=1, source_target_pairs={{0,4},{1,5},{2,6},{3,7},{4,0},{5,1},{6,2},{7,3},{8,12},{9,13},{10,... | collective-permute-start | bytes 1155080 | tf_op jit(solution)/shard_map/ppermute | solution.py:794
  310.3 15.3 %collective-permute-start.69 = (f32[4,288,128]{2,1,0:T(8,128)S(1)}, f32[4,288,128]{2,1,0:T(8,128)S(1)}, u32[]{:S(2)}, u32[]{:S(2)}) collective-permute-start(f32[4,288,128]{2,1,0:T(8,128)S(1)} %bitcast_add_fusion.2), channel_id=1, source_target_pairs={{0,2},{1,3},{2,0},{3,1},{4,6},{5,7},{6,4},{7,5},{8,10},{9,11},{10,... | collective-permute-start | bytes 1769480 | tf_op jit(solution)/shard_map/ppermute | solution.py:794
  313.5 6.5 %collective-permute-start.72 = (f32[88,128]{1,0:T(8,128)S(1)}, f32[88,128]{1,0:T(8,128)S(1)}, u32[]{:S(2)}, u32[]{:S(2)}) collective-permute-start(f32[88,128]{1,0:T(8,128)S(1)} %broadcast_add_fusion), channel_id=1, source_target_pairs={{0,16},{16,0},{1,17},{17,1},{2,18},{18,2},{3,19},{19,3},{4,20},{20... | collective-permute-start | bytes 135176 | tf_op jit(solution)/shard_map/ppermute | solution.py:794
  316.5 11.8 %collective-permute-start.79 = (f32[1,376,128]{2,1,0:T(8,128)S(1)}, f32[1,376,128]{2,1,0:T(8,128)S(1)}, u32[]{:S(2)}, u32[]{:S(2)}) collective-permute-start(f32[1,376,128]{2,1,0:T(8,128)S(1)} %fusion.5), channel_id=1, source_target_pairs={{0,8},{1,9},{2,10},{3,11},{4,12},{5,13},{6,14},{7,15},{8,0},{9,1},... | collective-permute-start | bytes 577544 | tf_op jit(solution)/shard_map/ppermute | solution.py:794
  326.8 7.6 %collective-permute-start.70 = (f32[2,288,128]{2,1,0:T(8,128)S(1)}, f32[2,288,128]{2,1,0:T(8,128)S(1)}, u32[]{:S(2)}, u32[]{:S(2)}) collective-permute-start(f32[2,288,128]{2,1,0:T(8,128)S(1)} %fusion.3), channel_id=1, source_target_pairs={{0,4},{1,5},{2,6},{3,7},{4,0},{5,1},{6,2},{7,3},{8,12},{9,13},{10,... | collective-permute-start | bytes 884744 | tf_op jit(solution)/shard_map/ppermute | solution.py:794
  329.5 18.6 %collective-permute-start.73 = (f32[1488,128]{1,0:T(8,128)}, f32[1488,128]{1,0:T(8,128)S(1)}, u32[]{:S(2)}, u32[]{:S(2)}) collective-permute-start(f32[1488,128]{1,0:T(8,128)} %bitcast.199), channel_id=1, source_target_pairs={{0,16},{1,17},{2,18},{3,19},{4,20},{5,21},{6,22},{7,23},{8,24},{9,... | collective-permute-start | bytes 2285576 | tf_op jit(solution)/shard_map/ppermute | solution.py:1178
  332.3 13.9 %collective-permute-start.80 = (f32[744,128]{1,0:T(8,128)S(1)}, f32[744,128]{1,0:T(8,128)S(1)}, u32[]{:S(2)}, u32[]{:S(2)}) collective-permute-start(f32[744,128]{1,0:T(8,128)S(1)} %pad_maximum_fusion.refs_2_), channel_id=1, source_target_pairs={{16,0},{17,1},{18,2},{19,3},{20,4},{21,5},{22,6},{23,7},{24,8},{25... | collective-permute-start | bytes 1142792 | tf_op jit(solution)/shard_map/ppermute | solution.py:1179
  335.5 8.7 %collective-permute-start.71 = (f32[1,288,128]{2,1,0:T(8,128)S(1)}, f32[1,288,128]{2,1,0:T(8,128)S(1)}, u32[]{:S(2)}, u32[]{:S(2)}) collective-permute-start(f32[1,288,128]{2,1,0:T(8,128)S(1)} %fusion.7), channel_id=1, source_target_pairs={{0,8},{1,9},{2,10},{3,11},{4,12},{5,13},{6,14},{7,15},{8,0},{9,1},... | collective-permute-start | bytes 442376 | tf_op jit(solution)/shard_map/ppermute | solution.py:794
  (162 other events, 1599.8 us)
Sparse Core Ops, SparseCore 0:
  144.1 135.9 reduce-scatter.1
